TPU v7x, 256 devices: a whole 4x4x8 slice. The times are simulated.
256 devices in a mesh: tm: 32 (over y, z_hi, x), space: 8 (over z_lo, core).
Axes of the slice: x: 4, y: 4, z: 8 (z_hi: 2, z_lo: 4; z = z_hi * 4 + z_lo), core: 2. Of those that a mesh axis runs over, the one named last changes fastest.
Arguments:
- features: bfloat16 [32, 64, 64, 256], P('tm', 'space'), may hold values from -6 to 6
- masks: int32 [32, 64, 64], P('tm', 'space'), may hold values from 0 to 1
- w_pix: bfloat16 [256, 256], replicated, may hold values from -0.375 to 0.375
- mask_embed: bfloat16 [256], replicated, may hold values from -4 to 4
- w_conv: bfloat16 [3, 3, 256, 256], replicated, may hold values from -0.125 to 0.125
- w_out: bfloat16 [256, 64], replicated, may hold values from -0.375 to 0.375
- w_ptr: bfloat16 [256, 256], replicated, may hold values from -0.375 to 0.375
- w_query: bfloat16 [256, 256], replicated, may hold values from -1 to 1
- w_key: bfloat16 [64, 256], replicated, may hold values from -0.75 to 0.75
- w_value: bfloat16 [64, 256], replicated, may hold values from -0.75 to 0.75
- w_proj: bfloat16 [256, 256], replicated, may hold values from -0.375 to 0.375
- mem_tpos: bfloat16 [3, 64], replicated, may hold values from -120 to 120
- ptr_tpos: bfloat16 [16, 256], replicated, may hold values from -4 to 4
- empty_memory: bfloat16 [64], replicated, may hold values from -4 to 4
Outputs:
- attended: bfloat16 [32, 64, 64, 256], P('tm', 'space')
- memory: bfloat16 [32, 64, 4096], P('tm', 'space')
- pointers: bfloat16 [32, 256], P('tm')
All inputs are finite; a program needn't handle non-finite values.
Results may differ from a plain program's by a relative error of at most 0.015.
The roundings to bfloat16 on the way count: a program that leaves them out, or rounds other values in their place, can miss the bound.
Values may be sent and summed in bfloat16 or wider, within the bound.
No kernel may reach another device: no remote copies, remote signals or barrier semaphores. Data moves between devices by JAX's collectives and lax.ppermute only.
A program may use at most 128 MiB of HBM per device.

v0:
```python
import jax
import jax.numpy as jnp
from jax import lax
from jax.sharding import PartitionSpec as P

MEMS = 3
POINTERS = 16


def from_behind(block, axis, distance):
    devices = range(lax.axis_size(axis))
    route = [(i - distance, i) for i in devices if i - distance in devices]
    return lax.ppermute(block, axis, route)


def with_halo(block, sides, width):
    for axis, dim in sides:
        count = lax.axis_size(axis)
        forward = [(i, i + 1) for i in range(count - 1)]
        backward = [(target, source) for source, target in forward]
        low = lax.ppermute(
            lax.slice_in_dim(block, block.shape[dim] - width, None, axis=dim), axis, forward
        )
        high = lax.ppermute(lax.slice_in_dim(block, 0, width, axis=dim), axis, backward)
        block = jnp.concatenate([low, block, high], axis=dim)
    return block


def fetch_earlier(carried, hop_count):
    pieces = []
    for step_index in range(hop_count):
        pieces.append(from_behind(carried, "tm", step_index + 1))
    return jnp.concatenate(pieces[::-1], axis=0)


def attend(query, blocks):
    scores = []
    row_top = None
    for key_rows, value_rows, is_valid in blocks:
        block_scores = lax.dot_general(
            query, key_rows, (((1,), (1,)), ((), ())), preferred_element_type=jnp.float32
        )
        block_scores = jnp.where(is_valid, block_scores, -jnp.inf)
        scores.append(block_scores)
        block_top = jnp.max(block_scores, axis=1, keepdims=True)
        row_top = block_top if row_top is None else jnp.maximum(row_top, block_top)
    row_total = jnp.zeros_like(row_top)
    for block_scores in scores:
        row_total = row_total + jnp.sum(jnp.exp(block_scores - row_top), axis=1, keepdims=True)
    mixed_sum = jnp.zeros((query.shape[0], blocks[0][1].shape[1]), jnp.float32)
    for block_scores, block in zip(scores, blocks):
        weights = (jnp.exp(block_scores - row_top) / row_total).astype(jnp.bfloat16)
        mixed_sum = mixed_sum + jnp.dot(weights, block[1], preferred_element_type=jnp.float32)
    return mixed_sum.astype(jnp.bfloat16)


def body(
    features,
    masks,
    w_pix,
    mask_embed,
    w_conv,
    w_out,
    w_ptr,
    w_query,
    w_key,
    w_value,
    w_proj,
    mem_tpos,
    ptr_tpos,
    empty_memory,
):
    frames_dev, rows_dev, columns, model_dim = features.shape
    mem_dim = w_key.shape[0]
    ptr_tok = model_dim // mem_dim
    band_tokens = rows_dev * columns
    flat_rows = features.reshape(frames_dev * band_tokens, model_dim)
    mask_rows = masks.reshape(frames_dev * band_tokens, 1).astype(jnp.float32)
    joined_map = (
        jnp.dot(flat_rows, w_pix, preferred_element_type=jnp.float32)
        + mask_rows * mask_embed.astype(jnp.float32)
    ).astype(jnp.bfloat16)
    joined_map = joined_map.reshape(frames_dev, rows_dev, columns, model_dim)
    padded = with_halo(joined_map, (("space", 1),), 1)
    padded = jnp.pad(padded, ((0, 0), (0, 0), (1, 1), (0, 0)))
    conv_sum = jnp.zeros((frames_dev * band_tokens, model_dim), jnp.float32)
    for row_tap in range(3):
        for col_tap in range(3):
            window_rows = padded[
                :, row_tap : row_tap + rows_dev, col_tap : col_tap + columns, :
            ].reshape(-1, model_dim)
            conv_sum = conv_sum + jnp.dot(
                window_rows, w_conv[row_tap, col_tap], preferred_element_type=jnp.float32
            )
    hidden = jax.nn.gelu(conv_sum, approximate=True).astype(jnp.bfloat16)
    memory = jnp.dot(hidden, w_out, preferred_element_type=jnp.float32).astype(jnp.bfloat16)
    memory = memory.reshape(frames_dev, rows_dev, columns * mem_dim)
    band_mask = masks.reshape(frames_dev, band_tokens).astype(jnp.bfloat16)
    partial_value = jnp.einsum(
        "ft,ftd->fd",
        band_mask,
        features.reshape(frames_dev, band_tokens, model_dim),
        preferred_element_type=jnp.float32,
    )
    pooled = lax.psum(partial_value, "space")
    normed = (pooled * lax.rsqrt(jnp.mean(pooled * pooled, axis=1, keepdims=True) + 1e-06)).astype(
        jnp.bfloat16
    )
    pointers = jnp.dot(normed, w_ptr, preferred_element_type=jnp.float32).astype(jnp.bfloat16)
    all_pointers = lax.all_gather(pointers, "tm", axis=0, tiled=True)
    hop_count = (MEMS + frames_dev - 1) // frames_dev
    carried = lax.all_gather(memory, "space", axis=1, tiled=True)
    history = jnp.concatenate(
        [fetch_earlier(carried, hop_count), carried[: frames_dev - 1]], axis=0
    )
    grid_tokens = columns * columns
    hist_frames = history.shape[0]
    history = history.reshape(hist_frames, grid_tokens, mem_dim)
    hist_values = jnp.dot(
        history.reshape(-1, mem_dim), w_value, preferred_element_type=jnp.float32
    ).astype(jnp.bfloat16)
    hist_values = hist_values.reshape(hist_frames, grid_tokens, model_dim)
    tpos_keys = jnp.dot(mem_tpos, w_key, preferred_element_type=jnp.float32)
    ptr_tpos_keys = jnp.dot(
        ptr_tpos[::-1].reshape(POINTERS * ptr_tok, mem_dim),
        w_key,
        preferred_element_type=jnp.float32,
    )
    null_key = jnp.dot(
        empty_memory.reshape(1, mem_dim), w_key, preferred_element_type=jnp.float32
    ).astype(jnp.bfloat16)
    null_value = jnp.dot(
        empty_memory.reshape(1, mem_dim), w_value, preferred_element_type=jnp.float32
    ).astype(jnp.bfloat16)
    padded_ptr = jnp.concatenate(
        [jnp.zeros((POINTERS, model_dim), jnp.bfloat16), all_pointers], axis=0
    )
    ptr_offsets = jnp.repeat(jnp.arange(POINTERS, dtype=jnp.int32) - POINTERS, ptr_tok)
    features_f = features.reshape(frames_dev, band_tokens, model_dim).astype(jnp.float32)
    first_frame = lax.axis_index("tm") * frames_dev
    frame = first_frame + 0
    rows_f = features_f[0]
    centred = rows_f - jnp.mean(rows_f, axis=1, keepdims=True)
    query_in = (
        centred * lax.rsqrt(jnp.mean(centred * centred, axis=1, keepdims=True) + 1e-05)
    ).astype(jnp.bfloat16)
    query = (
        jnp.dot(query_in, w_query, preferred_element_type=jnp.float32) * model_dim ** (-0.5)
    ).astype(jnp.bfloat16)
    blocks = []
    for distance in range(1, MEMS + 1):
        slot_index = hop_count * frames_dev - distance
        key_rows = (
            jnp.dot(history[slot_index], w_key, preferred_element_type=jnp.float32)
            + tpos_keys[distance - 1]
        ).astype(jnp.bfloat16)
        blocks.append((key_rows, hist_values[slot_index], frame - distance >= 0))
    window = lax.dynamic_slice_in_dim(padded_ptr, frame, POINTERS, 0)
    ptr_tokens = window.reshape(POINTERS * ptr_tok, mem_dim)
    ptr_keys = (
        jnp.dot(ptr_tokens, w_key, preferred_element_type=jnp.float32) + ptr_tpos_keys
    ).astype(jnp.bfloat16)
    ptr_values = jnp.dot(ptr_tokens, w_value, preferred_element_type=jnp.float32).astype(
        jnp.bfloat16
    )
    extra_valid = jnp.concatenate([frame + ptr_offsets >= 0, jnp.ones((1,), bool)], axis=0)
    blocks.append(
        (
            jnp.concatenate([ptr_keys, null_key], axis=0),
            jnp.concatenate([ptr_values, null_value], axis=0),
            extra_valid[None, :],
        )
    )
    mixed_rows = attend(query, blocks)
    outputs = [
        (rows_f + jnp.dot(mixed_rows, w_proj, preferred_element_type=jnp.float32)).astype(
            jnp.bfloat16
        )
    ]
    attended = jnp.stack(outputs, axis=0).reshape(frames_dev, rows_dev, columns, model_dim)
    return (attended, memory, pointers)


def solution(mesh):
    return jax.shard_map(
        body,
        mesh=mesh,
        in_specs=(
            P("tm", "space", None, None),
            P("tm", "space", None),
            P(),
            P(),
            P(),
            P(),
            P(),
            P(),
            P(),
            P(),
            P(),
            P(),
            P(),
            P(),
        ),
        out_specs=(P("tm", "space", None, None), P("tm", "space", None), P("tm", None)),
        check_vma=False,
    )
```

profile of v0, /device:TPU:128, one launch (start us, length us, event | category | flops | bytes accessed | tf_op | source)
XLA Modules:
  0.0 303.7 jit_solution(17939438171379081497)
XLA Ops:
  2.2 1.2 fusion.24
  3.4 1.7 collective-permute-start
  5.1 1.3 collective-permute-start.1
  6.4 1.1 convert_reduce_fusion
  8.4 0.9 fusion.96
  9.3 1.1 convolution_bitcast_fusion
  10.5 16.4 %psum.7 = f32[1,256]{1,0:T(1,128)S(1)} all-reduce(f32[1,256]{1,0:T(1,128)S(1)} %convolution_bitcast_fusion), channel_id=1, replica_groups=mesh['tm'=32,'space'=8] {'space'}, use_global_device_ids=true, to_apply=%region_5.6 | all-reduce | flops 256 | bytes 2048 | tf_op jit(solution)/shard_map/psum | solution.py:105
  28.2 1.0 fusion.90
  29.7 100.9 %all-gather.1 = bf16[32,1,256]{2,1,0:T(2,128)(2,1)S(1)} all-gather(bf16[1,1,256]{2,1,0:T(2,128)(2,1)S(1)} %reshape.203), channel_id=2, replica_groups=mesh['tm'=32,'space'=8] {'tm'}, dimensions={0}, use_global_device_ids=true | all-gather | bytes 16896 | tf_op jit(solution)/shard_map/all_gather | solution.py:110
  130.8 1.5 convolution_convert_fusion.2
  133.1 0.9 fusion.113
  134.6 1.2 fusion.31
  136.7 1.5 fusion.26
  139.2 1.1 fusion.63
  141.1 1.1 convolution_add_fusion.11
  142.2 1.1 convolution_add_fusion.10
  143.4 1.1 convolution_add_fusion.9
  144.5 1.2 convolution_add_fusion.8
  145.7 1.1 fusion.53
  146.8 1.1 convolution_add_fusion.7
  148.0 1.1 convolution_add_fusion.6
  149.1 1.5 convolution_convert_fusion.1
  151.0 15.0 %all_gather.6 = bf16[1,64,4096]{2,1,0:T(8,128)(2,1)S(1)} all-gather(bf16[1,8,4096]{2,1,0:T(8,128)(2,1)S(1)} %reshape.196), channel_id=1, replica_groups=mesh['tm'=32,'space'=8] {'space'}, dimensions={1}, use_global_device_ids=true | all-gather | bytes 589824 | tf_op jit(solution)/shard_map/all_gather | solution.py:112
  166.0 1.9 collective-permute-start.4
  167.9 3.8 %collective-permute-start.3 = (bf16[1,64,4096]{2,1,0:T(8,128)(2,1)S(1)}, bf16[1,64,4096]{2,1,0:T(8,128)(2,1)S(1)}, u32[]{:S(2)}, u32[]{:S(2)}) collective-permute-start(bf16[1,64,4096]{2,1,0:T(8,128)(2,1)S(1)} %all_gather.6), channel_id=1, source_target_pairs={{0,16},{8,24},{16,32},{24,40},{32,48},{40,56},{48,64},{56,72},{64,... | collective-permute-start | bytes 1572872 | tf_op jit(solution)/shard_map/ppermute | solution.py:13
  171.8 6.6 %collective-permute-start.2 = (bf16[1,64,4096]{2,1,0:T(8,128)(2,1)S(1)}, bf16[1,64,4096]{2,1,0:T(8,128)(2,1)S(1)}, u32[]{:S(2)}, u32[]{:S(2)}) collective-permute-start(bf16[1,64,4096]{2,1,0:T(8,128)(2,1)S(1)} %all_gather.6), channel_id=1, source_target_pairs={{0,8},{8,16},{16,24},{24,32},{32,40},{40,48},{48,56},{56,64},{64,7... | collective-permute-start | bytes 1572872 | tf_op jit(solution)/shard_map/ppermute | solution.py:13
  179.2 1.2 convert_element_type.121
  181.0 1.2 fusion.23
  182.2 1.7 fusion.112
  183.9 15.7 %collective-permute-done.4 = bf16[1,64,4096]{2,1,0:T(8,128)(2,1)S(1)} collective-permute-done((bf16[1,64,4096]{2,1,0:T(8,128)(2,1)S(1)}, bf16[1,64,4096]{2,1,0:T(8,128)(2,1)S(1)}, u32[]{:S(2)}, u32[]{:S(2)}) %collective-permute-start.4) | collective-permute-done | bytes 524320 | tf_op jit(solution)/shard_map/ppermute | solution.py:13
  199.6 30.7 %collective-permute-done.3 = bf16[1,64,4096]{2,1,0:T(8,128)(2,1)S(1)} collective-permute-done((bf16[1,64,4096]{2,1,0:T(8,128)(2,1)S(1)}, bf16[1,64,4096]{2,1,0:T(8,128)(2,1)S(1)}, u32[]{:S(2)}, u32[]{:S(2)}) %collective-permute-start.3) | collective-permute-done | bytes 524320 | tf_op jit(solution)/shard_map/ppermute | solution.py:13
  230.3 19.6 %collective-permute-done.2 = bf16[1,64,4096]{2,1,0:T(8,128)(2,1)S(1)} collective-permute-done((bf16[1,64,4096]{2,1,0:T(8,128)(2,1)S(1)}, bf16[1,64,4096]{2,1,0:T(8,128)(2,1)S(1)}, u32[]{:S(2)}, u32[]{:S(2)}) %collective-permute-start.2) | collective-permute-done | bytes 524320 | tf_op jit(solution)/shard_map/ppermute | solution.py:13
  250.6 1.3 pad_maximum_fusion
  252.0 4.3 %reshape_reshape.3 = bf16[12288,64]{1,0:T(8,128)(2,1)S(1)} reshape(bf16[3,64,4096]{2,1,0:T(8,128)(2,1)} %pad_maximum_fusion) | data formatting | bytes 3145728 | tf_op jit(solution)/shard_map/reshape;reshape | solution.py:120
  256.3 5.2 %convolution_convert_fusion = bf16[12288,256]{1,0:T(8,128)(2,1)} fusion(bf16[12288,64]{1,0:T(8,128)(2,1)S(1)} %reshape_reshape.3, bf16[64,256]{1,0:T(8,128)(2,1)} %param.23), kind=kOutput, calls=%fused_computation | convolution fusion | flops 405798912 | bytes 7897088 | tf_op jit(solution)/shard_map/dot_general | solution.py:119
  261.5 2.1 squeeze.50
  263.6 6.2 %select_reduce_fusion.1 = (f32[512]{0:T(512)S(1)}, f32[512,4096]{1,0:T(8,128)}) fusion(pred[]{:T(512)S(6)} %ge.20, bf16[512,256]{1,0:T(8,128)(2,1)} %copy-done.11, bf16[4096,64]{1,0:T(8,128)(2,1)S(1)} %squeeze.50, bf16[64,256]{1,0:T(8,128)(2,1)} %param.22, f32[256]{0:T(256)S(1)} %bitcast.130), kind=kOutput, calls=%fused_computation.8 | convolution fusion | flops 1214250496 | bytes 9210881 | tf_op jit(solution)/shard_map/dot_general | solution.py:40
  269.8 1.1 squeeze.51
  271.0 4.4 %select_reduce_fusion = (f32[512]{0:T(512)S(1)}, f32[512,4096]{1,0:T(8,128)}) fusion(pred[]{:T(512)S(6)} %ge.21, bf16[512,256]{1,0:T(8,128)(2,1)S(1)} %copy-done.12, bf16[4096,64]{1,0:T(8,128)(2,1)S(1)} %squeeze.51, bf16[64,256]{1,0:T(8,128)(2,1)S(1)} %copy-done.9, f32[256]{0:T(256)S(1)} %bitcast.129), kind=kOutput, calls=%fused_computation.7 | convolution fusion | flops 1214250496 | bytes 9210881 | tf_op jit(solution)/shard_map/dot_general | solution.py:40
  275.4 1.1 squeeze.49
  276.6 6.3 %select_reduce_fusion.2 = (f32[512]{0:T(512)S(1)}, f32[512,4096]{1,0:T(8,128)}) fusion(pred[]{:T(512)S(6)} %ge.19, bf16[512,256]{1,0:T(8,128)(2,1)} %copy-done.11, bf16[4096,64]{1,0:T(8,128)(2,1)S(1)} %squeeze.49, bf16[64,256]{1,0:T(8,128)(2,1)} %param.22, f32[256]{0:T(256)} %bitcast.128), kind=kOutput, calls=%fused_computation.9 | convolution fusion | flops 1214250496 | bytes 9210881 | tf_op jit(solution)/shard_map/dot_general | solution.py:40
  282.9 1.0 fusion.75
  283.8 10.8 %fusion.1 = (f32[512]{0:T(512)S(1)}, f32[512]{0:T(512)S(1)}, f32[512]{0:T(512)S(1)}) fusion(f32[512,4096]{1,0:T(8,128)} %get-tuple-element.28, f32[512]{0:T(512)S(1)} %maximum_maximum_fusion, pred[]{:T(512)S(6)} %ge.20, f32[512,4096]{1,0:T(8,128)} %get-tuple-element.24, pred[]{:T(512)S(6)} %ge.21, f32[512,4096]{1,0:T(8,128)} %get-tuple-element.26, pred[]{:T(512)S(6)} %ge.19), kind=kLoop, calls=%fused_computation.11 | loop fusion | flops 18872832 | bytes 25174020 | tf_op jit(solution)/shard_map/reduce_sum | solution.py:49
  294.7 1.0 copy-done.1
  295.7 1.7 fusion.6
  298.3 1.7 fusion.19
  300.8 1.7 fusion.16
  302.5 1.2 fusion.25
  (88 shorter events, 12.0 us)
Async XLA Ops:
  0.6 1.6 copy-start
  3.4 135.5 %collective-permute-start = (bf16[1,1,64,256]{3,2,1,0:T(8,128)(2,1)S(1)}, bf16[1,1,64,256]{3,2,1,0:T(8,128)(2,1)S(1)}, u32[]{:S(2)}, u32[]{:S(2)}) collective-permute-start(bf16[1,1,64,256]{3,2,1,0:T(8,128)(2,1)S(1)} %get-tuple-element.14), channel_id=1, source_target_pairs={{0,1},{1,2},{2,3},{3,4},{4,5},{5,6},{6,7},{8,9},{9,10},{10,11},{11... | collective-permute-start | bytes 98312 | tf_op jit(solution)/shard_map/ppermute | solution.py:21
  5.1 133.8 %collective-permute-start.1 = (bf16[1,1,64,256]{3,2,1,0:T(8,128)(2,1)S(1)}, bf16[1,1,64,256]{3,2,1,0:T(8,128)(2,1)S(1)}, u32[]{:S(2)}, u32[]{:S(2)}) collective-permute-start(bf16[1,1,64,256]{3,2,1,0:T(8,128)(2,1)S(1)} %get-tuple-element.15), channel_id=1, source_target_pairs={{1,0},{2,1},{3,2},{4,3},{5,4},{6,5},{7,6},{9,8},{10,9},{11,10},{12... | collective-permute-start | bytes 98312 | tf_op jit(solution)/shard_map/ppermute | solution.py:24
  29.2 0.5 copy-start.18
  144.5 36.5 %copy-start.2 = (bf16[1,8,64,256]{3,2,1,0:T(8,128)(2,1)S(1)}, bf16[1,8,64,256]{3,2,1,0:T(8,128)(2,1)}, u32[]{:S(2)}) copy-start(bf16[1,8,64,256]{3,2,1,0:T(8,128)(2,1)} %param.14) | copy-start | bytes 786436
  151.0 98.9 %copy-start.10 = (bf16[1,8,4096]{2,1,0:T(8,128)(2,1)}, bf16[1,8,4096]{2,1,0:T(8,128)(2,1)S(1)}, u32[]{:S(2)}) copy-start(bf16[1,8,4096]{2,1,0:T(8,128)(2,1)S(1)} %reshape.196) | copy-start | bytes 196612
  166.0 33.6 %collective-permute-start.4 = (bf16[1,64,4096]{2,1,0:T(8,128)(2,1)S(1)}, bf16[1,64,4096]{2,1,0:T(8,128)(2,1)S(1)}, u32[]{:S(2)}, u32[]{:S(2)}) collective-permute-start(bf16[1,64,4096]{2,1,0:T(8,128)(2,1)S(1)} %all_gather.6), channel_id=1, source_target_pairs={{0,24},{8,32},{16,40},{24,48},{32,56},{40,64},{48,72},{56,80},{64,... | collective-permute-start | bytes 1572872 | tf_op jit(solution)/shard_map/ppermute | solution.py:13
  167.9 62.3 %collective-permute-start.3 = (bf16[1,64,4096]{2,1,0:T(8,128)(2,1)S(1)}, bf16[1,64,4096]{2,1,0:T(8,128)(2,1)S(1)}, u32[]{:S(2)}, u32[]{:S(2)}) collective-permute-start(bf16[1,64,4096]{2,1,0:T(8,128)(2,1)S(1)} %all_gather.6), channel_id=1, source_target_pairs={{0,16},{8,24},{16,32},{24,40},{32,48},{40,56},{48,64},{56,72},{64,... | collective-permute-start | bytes 1572872 | tf_op jit(solution)/shard_map/ppermute | solution.py:13
  171.8 78.0 %collective-permute-start.2 = (bf16[1,64,4096]{2,1,0:T(8,128)(2,1)S(1)}, bf16[1,64,4096]{2,1,0:T(8,128)(2,1)S(1)}, u32[]{:S(2)}, u32[]{:S(2)}) collective-permute-start(bf16[1,64,4096]{2,1,0:T(8,128)(2,1)S(1)} %all_gather.6), channel_id=1, source_target_pairs={{0,8},{8,16},{16,24},{24,32},{32,40},{40,48},{48,56},{56,64},{64,7... | collective-permute-start | bytes 1572872 | tf_op jit(solution)/shard_map/ppermute | solution.py:13
  182.2 67.6 %copy-start.11 = (bf16[512,256]{1,0:T(8,128)(2,1)}, bf16[512,256]{1,0:T(8,128)(2,1)S(1)}, u32[]{:S(2)}) copy-start(bf16[512,256]{1,0:T(8,128)(2,1)S(1)} %fusion.23) | copy-start | bytes 786436
  199.6 50.3 %copy-start.3 = (bf16[1,64,4096]{2,1,0:T(8,128)(2,1)}, bf16[1,64,4096]{2,1,0:T(8,128)(2,1)S(1)}, u32[]{:S(2)}) copy-start(bf16[1,64,4096]{2,1,0:T(8,128)(2,1)S(1)} %collective-permute-done.4) | copy-start | bytes 1572868
  230.2 19.6 %copy-start.7 = (bf16[1,64,4096]{2,1,0:T(8,128)(2,1)}, bf16[1,64,4096]{2,1,0:T(8,128)(2,1)S(1)}, u32[]{:S(2)}) copy-start(bf16[1,64,4096]{2,1,0:T(8,128)(2,1)S(1)} %collective-permute-done.3) | copy-start | bytes 1572868
  249.8 0.8 copy-start.5
  256.3 7.3 %copy-start.15 = (f32[1,256]{1,0:T(1,128)S(1)}, f32[1,256]{1,0:T(1,128)}, u32[]{:S(2)}) copy-start(f32[1,256]{1,0:T(1,128)} %get-tuple-element.16) | copy-start | bytes 3076
  263.6 6.2 %copy-start.4 = (bf16[1,64,4096]{2,1,0:T(8,128)(2,1)S(1)}, bf16[1,64,4096]{2,1,0:T(8,128)(2,1)}, u32[]{:S(2)}) copy-start(bf16[1,64,4096]{2,1,0:T(8,128)(2,1)} %copy-done.3) | copy-start | bytes 1572868
  263.6 7.4 %copy-start.9 = (bf16[64,256]{1,0:T(8,128)(2,1)S(1)}, bf16[64,256]{1,0:T(8,128)(2,1)}, u32[]{:S(2)}) copy-start(bf16[64,256]{1,0:T(8,128)(2,1)} %param.22) | copy-start | bytes 98308
  263.6 7.4 %copy-start.12 = (bf16[512,256]{1,0:T(8,128)(2,1)S(1)}, bf16[512,256]{1,0:T(8,128)(2,1)}, u32[]{:S(2)}) copy-start(bf16[512,256]{1,0:T(8,128)(2,1)} %copy-done.11) | copy-start | bytes 786436
  263.6 7.4 %copy-start.14 = (f32[1,256]{1,0:T(1,128)S(1)}, f32[1,256]{1,0:T(1,128)}, u32[]{:S(2)}) copy-start(f32[1,256]{1,0:T(1,128)} %get-tuple-element.17) | copy-start | bytes 3076
  271.0 4.4 %copy-start.6 = (bf16[1,64,4096]{2,1,0:T(8,128)(2,1)S(1)}, bf16[1,64,4096]{2,1,0:T(8,128)(2,1)}, u32[]{:S(2)}) copy-start(bf16[1,64,4096]{2,1,0:T(8,128)(2,1)} %copy-done.5) | copy-start | bytes 1572868
  276.6 18.1 %slice-start = ((s8[6291456]{0:T(1024)(128)(4,1)}), s8[2097152]{0:T(1024)(128)(4,1)S(1)}, s32[]{:S(2)}) async-start(s8[6291456]{0:T(1024)(128)(4,1)} %bitcast.104), calls=%async_computation | async-start | bytes 4194304
  283.8 10.8 %slice-start.1 = ((s8[6291456]{0:T(1024)(128)(4,1)}), s8[4194304]{0:T(1024)(128)(4,1)S(1)}, s32[]{:S(2)}) async-start(s8[6291456]{0:T(1024)(128)(4,1)} %bitcast.104), calls=%async_computation.1 | async-start | bytes 8388608
  283.8 11.9 %copy-start.1 = (f32[512,4096]{1,0:T(8,128)S(1)}, f32[512,4096]{1,0:T(8,128)}, u32[]{:S(2)}) copy-start(f32[512,4096]{1,0:T(8,128)} %get-tuple-element.26) | copy-start | bytes 25165828
  283.8 13.6 %slice-start.2 = ((s8[8388608]{0:T(1024)(128)(4,1)}), s8[4194304]{0:T(1024)(128)(4,1)S(1)}, s32[]{:S(2)}) async-start(s8[8388608]{0:T(1024)(128)(4,1)} %bitcast.106), calls=%async_computation.2 | async-start | bytes 8388608
  295.7 2.6 slice-start.3
  295.7 4.3 %slice-start.4 = ((s8[8388608]{0:T(1024)(128)(4,1)}), s8[4194304]{0:T(1024)(128)(4,1)S(1)}, s32[]{:S(2)}) async-start(s8[8388608]{0:T(1024)(128)(4,1)} %bitcast.108), calls=%async_computation.4 | async-start | bytes 8388608
  298.3 2.4 slice-start.5
  300.8 1.7 copy-start.8
  300.8 1.7 copy-start.13
  300.8 1.7 copy-start.16
  300.8 1.8 copy-start.17
where the time goes:
time: 305 us; the launch traced here: 304 us
  blocking collectives  132 us (43%)
  waiting for transfers between devices  65.9 us (22%)
  matrix products  51.8 us (17%)
  other arithmetic  19.1 us (6%)
  local copies, waits for them, and re-layouts  17.3 us (6%)
  starting transfers between devices  15.4 us (5%)
    all_gather x1, blocking collectives, body(): all_pointers = lax.all_gather(pointers, 'tm', axis=0, tiled=True)  101 us
    ppermute x3, waiting for transfers between devices, from_behind(): return lax.ppermute(block, axis, route)  65.9 us
    dot_general x4, matrix products, attend(): lax.dot_general(query, key_rows, (((1,), (1,)), ((), ())), preferred_elem...  18.6 us
    psum x1, blocking collectives, body(): pooled = lax.psum(partial_value, 'space')  16.4 us
    all_gather x1, blocking collectives, body(): carried = lax.all_gather(memory, 'space', axis=1, tiled=True)  15 us
    ppermute x3, starting transfers between devices, from_behind(): return lax.ppermute(block, axis, route)  12.3 us
    reduce_sum x2, other arithmetic, attend(): jnp.sum(jnp.exp(block_scores - row_top), axis=1, keepdims=True)  11.7 us
    dot_general x8, matrix products, body(): jnp.dot(window_rows, w_conv[row_tap, col_tap], preferred_element_type=jnp...  9.09 us
  transfers between devices with their start and end apart: 5, of which 3 were waited for; matrix products, arithmetic and copies ran while one was open for 6% of the time, Pallas kernels for 0%

commit v1 on v0

v1 whole, which is shorter than its diff:
```python
import functools

import jax
import jax.numpy as jnp
from jax import lax
from jax.experimental import pallas as pl
from jax.experimental.pallas import tpu as pltpu
from jax.sharding import PartitionSpec as P

MEMS = 3
POINTERS = 16
FRAMES = 32
BANDS = 8
ROWS = 8
COLS = 64
TOK = ROWS * COLS
HALF = TOK // 2
D = 256
MEM = 64
PAY = MEMS * HALF + 16
BOTH = ("tm", "space")
bf16 = jnp.bfloat16
f32 = jnp.float32
NT = (((1,), (1,)), ((), ()))


def call(kernel, out_shape, *args, scratch=(), in_specs=None, aliases=None, flops=0, name=None):
    vmem = pl.BlockSpec(memory_space=pltpu.VMEM)
    return pl.pallas_call(
        kernel,
        out_shape=out_shape,
        in_specs=[vmem] * len(args) if in_specs is None else in_specs,
        out_specs=jax.tree.map(lambda _: vmem, out_shape),
        scratch_shapes=list(scratch),
        input_output_aliases=aliases or {},
        compiler_params=pltpu.CompilerParams(vmem_limit_bytes=48 << 20),
        cost_estimate=pl.CostEstimate(flops=flops, bytes_accessed=1 << 20, transcendentals=0),
        name=name,
    )(*args)


def sds(shape, dtype):
    return jax.ShapeDtypeStruct(shape, dtype)


def joined_kernel(feat, mask, w_pix, embed, joined, top, bottom, pooled):
    columns = mask[...].astype(f32).T
    row = embed[...].astype(f32)
    total = jnp.zeros((8, D), f32)
    for r in range(ROWS):
        rows = feat[r * COLS : (r + 1) * COLS, :]
        column = columns[:, r : r + 1]
        value = jnp.dot(rows, w_pix[...], preferred_element_type=f32) + column * row
        value = value.astype(bf16)
        joined[r * COLS : (r + 1) * COLS, :] = value
        if r == 0:
            top[...] = value
        if r == ROWS - 1:
            bottom[...] = value
        picked = rows.astype(f32) * column
        for k in range(COLS // 8):
            total = total + picked[k * 8 : (k + 1) * 8, :]
    pooled[...] = jnp.sum(total, axis=0, keepdims=True)


def query_kernel(feat, w_query, query):
    for r in range(0, TOK, 128):
        x = feat[r : r + 128, :].astype(f32)
        x = x - jnp.mean(x, axis=1, keepdims=True)
        x = x * lax.rsqrt(jnp.mean(x * x, axis=1, keepdims=True) + 1e-05)
        y = jnp.dot(x.astype(bf16), w_query[...], preferred_element_type=f32)
        query[r : r + 128, :] = (y * D ** (-0.5)).astype(bf16)


def conv_kernel(joined, above, below, w_conv, w_out, memory, pairs, wide, tokens):
    side = lax.broadcasted_iota(jnp.int32, (COLS, D), 0)
    for r in range(ROWS + 2):
        if r == 0:
            row = above[...]
        elif r == ROWS + 1:
            row = below[...]
        else:
            row = joined[(r - 1) * COLS : r * COLS, :]
        value = row.astype(f32)
        left = jnp.where(side == 0, 0.0, pltpu.roll(value, 1, 0))
        right = jnp.where(side == COLS - 1, 0.0, pltpu.roll(value, COLS - 1, 0))
        here = slice(r * COLS, (r + 1) * COLS)
        wide[here, 0:D] = left.astype(bf16)
        wide[here, D : 2 * D] = row
        wide[here, 2 * D : 3 * D] = right.astype(bf16)
    w_twice = jnp.concatenate([w_out[...], w_out[...]], axis=1)
    for part in range(4):
        start = part * 2 * COLS
        total = None
        for a in range(3):
            window = wide[start + a * COLS : start + a * COLS + 2 * COLS, :]
            term = jnp.dot(window, w_conv[a], preferred_element_type=f32)
            total = term if total is None else total + term
        hidden = 0.5 * total * (
            1.0 + jnp.tanh(0.7978845608028654 * (total + 0.044715 * (total * total * total)))
        )
        tokens[start : start + 2 * COLS, :] = jnp.dot(
            hidden.astype(bf16), w_twice, preferred_element_type=f32
        )
    lane = lax.broadcasted_iota(jnp.int32, (8, 128), 1)
    for k in range(COLS // 2):
        even = tokens[pl.ds(2 * k, ROWS, stride=COLS), :]
        odd = tokens[pl.ds(2 * k + 1, ROWS, stride=COLS), :]
        memory[:, k * 128 : (k + 1) * 128] = jnp.where(lane < MEM, even, odd).astype(bf16)
    lane = lax.broadcasted_iota(jnp.int32, (HALF, 128), 1)
    pairs[...] = jnp.where(lane < MEM, tokens[0:HALF, :], tokens[HALF:TOK, :]).astype(bf16)


def pointer_kernel(mine, other, w_ptr, pointer):
    pooled = mine[...] + other[...]
    scale = lax.rsqrt(jnp.mean(pooled * pooled, axis=1, keepdims=True) + 1e-06)
    normed = jnp.broadcast_to(pooled * scale, (8, D)).astype(bf16)
    y = jnp.dot(normed, w_ptr[...], preferred_element_type=f32)
    pointer[...] = y[0:1, :].astype(bf16)


def payload_kernel(first, second, third, near, far, out):
    out[0:HALF, :] = first[...]
    out[HALF : 2 * HALF, :] = second[...]
    out[2 * HALF : 3 * HALF, :] = third[...]
    row = lax.broadcasted_iota(jnp.int32, (16, 128), 0)
    tail = jnp.zeros((16, 128), f32)
    a = near[...].astype(f32)
    b = far[...].astype(f32)
    for i, piece in enumerate((a[:, 0:128], a[:, 128:256], b[:, 0:128], b[:, 128:256])):
        tail = jnp.where(row == i, piece, tail)
    out[3 * HALF : 3 * HALF + 16, :] = tail.astype(bf16)


def twice(w):
    zero = jnp.zeros_like(w)
    return jnp.concatenate(
        [jnp.concatenate([w, zero], axis=1), jnp.concatenate([zero, w], axis=1)], axis=0
    )


QT = 256
CHUNK = 2 * HALF


def attention_kernel(count, first, last, *refs):
    refs = list(refs)
    place, query, w_key, w_value, mem_tpos, empty = refs[:6]
    refs = refs[6:]
    blocks, refs = refs[:count], refs[count:]
    if first:
        state_in = None
    else:
        state_in, refs = refs[:4], refs[4:]
    if last:
        feat, w_proj, ptr_tpos, attended, keys, values, top, norm, mixed, ptr_tok = refs
    else:
        top, norm, mixed, ptr_tok, keys, values = refs
    frame = place[0]
    wk = twice(w_key[...])
    wv = twice(w_value[...])
    padded = jnp.concatenate([mem_tpos[...], jnp.zeros((8 - MEMS, MEM), bf16)], axis=0)
    tpos_keys = jnp.dot(padded, w_key[...], preferred_element_type=f32)
    if first:
        token = jnp.broadcast_to(empty[...], (8, MEM))
        null_key = jnp.dot(token, w_key[...], preferred_element_type=f32).astype(bf16)
        null_value = jnp.dot(token, w_value[...], preferred_element_type=f32).astype(bf16)
        score = jnp.sum(
            query[...].astype(f32) * null_key[0:1, :].astype(f32), axis=1, keepdims=True
        )
        top[...] = score
        norm[...] = jnp.ones_like(score)
        mixed[...] = jnp.broadcast_to(null_value[0:1, :].astype(f32), (TOK, D))
    else:
        for source, target in zip(state_in, (top, norm, mixed, ptr_tok)):
            target[...] = source[...]
    for b, block in enumerate(blocks):
        tail = block[MEMS * HALF : MEMS * HALF + 16, :].astype(f32)
        ptr_tok[pl.ds(pl.multiple_of(place[1 + b] * 8, 8), 8), :] = tail[0:8, :]

    def update(rows, scores, value_rows):
        old = top[rows, :]
        new = jnp.maximum(old, jnp.max(scores, axis=1, keepdims=True))
        weights = jnp.exp(scores - new)
        fade = jnp.exp(old - new)
        norm[rows, :] = norm[rows, :] * fade + jnp.sum(weights, axis=1, keepdims=True)
        mixed[rows, :] = mixed[rows, :] * fade + jnp.dot(
            weights.astype(bf16), value_rows, preferred_element_type=f32
        )
        top[rows, :] = new

    for d in range(MEMS):

        @pl.when(frame >= d + 1)
        def _(d=d):
            shift = tpos_keys[d : d + 1, :]
            for b, block in enumerate(blocks):
                x = block[d * HALF : (d + 1) * HALF, :]
                base = b * TOK
                k = jnp.dot(x, wk, preferred_element_type=f32)
                v = jnp.dot(x, wv, preferred_element_type=f32).astype(bf16)
                keys[base : base + HALF, :] = (k[:, :D] + shift).astype(bf16)
                keys[base + HALF : base + TOK, :] = (k[:, D:] + shift).astype(bf16)
                values[base : base + HALF, :] = v[:, :D]
                values[base + HALF : base + TOK, :] = v[:, D:]
            tiles = [slice(q * QT, (q + 1) * QT) for q in range(TOK // QT)]
            found = [
                lax.dot_general(query[rows, :], keys[...], NT, preferred_element_type=f32)
                for rows in tiles
            ]
            for rows, scores in zip(tiles, found):
                update(rows, scores, values[...])

    if last:
        widened = jnp.dot(ptr_tpos[...], wk, preferred_element_type=f32)
        lane = lax.broadcasted_iota(jnp.int32, (1, POINTERS * 2), 1)
        tok = jnp.concatenate(
            [ptr_tok[s * 8 : s * 8 + 4, :] for s in range(BANDS)], axis=0
        ).astype(bf16)
        k = (jnp.dot(tok, wk, preferred_element_type=f32) + widened).astype(bf16)
        v = jnp.dot(tok, wv, preferred_element_type=f32).astype(bf16)
        valid = frame >= lane // 2 + 1
        for half in range(2):
            k_half = k[:, half * D : (half + 1) * D]
            v_half = v[:, half * D : (half + 1) * D]
            for q in range(TOK // QT):
                rows = slice(q * QT, (q + 1) * QT)
                scores = lax.dot_general(query[rows, :], k_half, NT, preferred_element_type=f32)
                update(rows, jnp.where(valid, scores, -jnp.inf), v_half)
        for q in range(TOK // QT):
            rows = slice(q * QT, (q + 1) * QT)
            final = (mixed[rows, :] / norm[rows, :]).astype(bf16)
            attended[rows, :] = (
                feat[rows, :].astype(f32)
                + jnp.dot(final, w_proj[...], preferred_element_type=f32)
            ).astype(bf16)


def attend(place, query, weights, blocks, state=None, final=None):
    smem = pl.BlockSpec(memory_space=pltpu.SMEM)
    vmem = pl.BlockSpec(memory_space=pltpu.VMEM)
    args = [place, query, *weights, *blocks]
    specs = [smem] + [vmem] * (len(args) - 1)
    if state is not None:
        args += list(state)
        specs += [vmem] * 4
    state_shape = [((TOK, 1), f32), ((TOK, 1), f32), ((TOK, D), f32), ((BANDS * 8, 128), f32)]
    scratch = [pltpu.VMEM((len(blocks) * TOK, D), bf16)] * 2
    if final is None:
        out = tuple(sds(*s) for s in state_shape)
    else:
        args += final
        specs += [vmem] * len(final)
        out = sds((TOK, D), bf16)
        scratch += [pltpu.VMEM(*s) for s in state_shape]
    return call(
        functools.partial(attention_kernel, len(blocks), state is None, final is not None),
        out,
        *args,
        in_specs=specs,
        scratch=scratch,
        flops=len(blocks) * 1_200_000_000,
        name="attention",
    )


def mirrored(source, target, s):
    if (source // 4) % 2 == (target // 4) % 2:
        return s
    return (3 - s // 2) * 2 + s % 2


def later(distance):
    return [
        ((t - distance) * BANDS + mirrored(t - distance, t, s), t * BANDS + s)
        for t in range(distance, FRAMES)
        for s in range(BANDS)
    ]


def pointer_route(extra):
    pairs = []
    for t in range(FRAMES):
        for s in range(BANDS):
            source = t - (2 * s + extra)
            if source >= 0:
                pairs.append((source * BANDS + s, t * BANDS + s))
    return pairs


def over_space(x, target):
    return lax.ppermute(x, "space", [(i, target(i)) for i in range(BANDS)])


def sibling(i):
    return i ^ 1


def beside(i):
    return i ^ 2


def across(i):
    return (3 - i // 2) * 2 + i % 2


def body(
    features,
    masks,
    w_pix,
    mask_embed,
    w_conv,
    w_out,
    w_ptr,
    w_query,
    w_key,
    w_value,
    w_proj,
    mem_tpos,
    ptr_tpos,
    empty_memory,
):
    feat = features.reshape(TOK, D)
    joined, top, bottom, pooled = call(
        joined_kernel,
        (sds((TOK, D), bf16), sds((COLS, D), bf16), sds((COLS, D), bf16), sds((1, D), f32)),
        feat,
        masks.reshape(ROWS, COLS),
        w_pix,
        mask_embed.reshape(1, D),
        flops=70_000_000,
        name="joined",
    )
    above = lax.ppermute(bottom, "space", [(i, i + 1) for i in range(BANDS - 1)])
    below = lax.ppermute(top, "space", [(i + 1, i) for i in range(BANDS - 1)])
    pooled = pooled + over_space(pooled, sibling)
    pooled = pooled + over_space(pooled, beside)
    query = call(query_kernel, sds((TOK, D), bf16), feat, w_query, flops=70_000_000, name="query")
    memory, pairs = call(
        conv_kernel,
        (sds((ROWS, COLS * MEM), bf16), sds((HALF, 128), bf16)),
        joined,
        above,
        below,
        w_conv.reshape(3, 3 * D, D),
        w_out,
        scratch=[pltpu.VMEM(((ROWS + 2) * COLS, 3 * D), bf16), pltpu.VMEM((TOK, 128), f32)],
        flops=640_000_000,
        name="conv",
    )
    pointer = call(
        pointer_kernel,
        sds((1, D), bf16),
        pooled,
        over_space(pooled, across),
        w_ptr,
        flops=1_000_000,
        name="pointer",
    )
    near = lax.ppermute(pointer, BOTH, pointer_route(1))
    far = lax.ppermute(pointer, BOTH, pointer_route(2))
    earlier = [lax.ppermute(pairs, BOTH, later(d)) for d in range(1, MEMS + 1)]
    own = call(payload_kernel, sds((PAY, 128), bf16), *earlier, near, far, name="payload")

    here = lax.axis_index("space")
    holders = [here, beside(here), across(here), beside(across(here))]
    places = [jnp.stack([lax.axis_index("tm"), h, sibling(h)]).astype(jnp.int32) for h in holders]
    weights = (w_key, w_value, mem_tpos, empty_memory.reshape(1, MEM))

    one = over_space(own, beside)
    two = over_space(own, across)
    three = over_space(two, beside)
    arrivals = [own, one, two, three]
    siblings = [over_space(x, sibling) for x in arrivals]
    state = None
    for place, mine, theirs in zip(places[:3], arrivals, siblings):
        state = attend(place, query, weights, [mine, theirs], state)
    attended = attend(
        places[3],
        query,
        weights,
        [three, siblings[3]],
        state,
        [feat, w_proj, ptr_tpos.reshape(POINTERS * 2, 128)],
    )
    return (
        attended.reshape(1, ROWS, COLS, D),
        memory.reshape(1, ROWS, COLS * MEM),
        pointer,
    )


def solution(mesh):
    return jax.shard_map(
        body,
        mesh=mesh,
        in_specs=(
            P("tm", "space", None, None),
            P("tm", "space", None),
            P(),
            P(),
            P(),
            P(),
            P(),
            P(),
            P(),
            P(),
            P(),
            P(),
            P(),
            P(),
        ),
        out_specs=(P("tm", "space", None, None), P("tm", "space", None), P("tm", None)),
        check_vma=False,
    )
```

time: 305 us -> 97.1 us (0.32)
  the two profiles are of different devices: /device:TPU:128 before, /device:TPU:13 now
where the time goes in v1:
time: 97.1 us; the launch traced here: 95.8 us
  starting transfers between devices  46.2 us (48%)
  Pallas kernels  25.9 us (27%)
  waiting for transfers between devices  17.2 us (18%)
  local copies, waits for them, and re-layouts  5.39 us (6%)
    pallas_call x9, Pallas kernels, call(): pl.pallas_call(kernel, out_shape=out_shape, in_specs=[vmem] * len(args) i...  25.9 us
    ppermute x10, starting transfers between devices, over_space(): return lax.ppermute(x, 'space', [(i, target(i)) for i in range(BANDS)])  18 us
    ppermute x10, waiting for transfers between devices, over_space(): return lax.ppermute(x, 'space', [(i, target(i)) for i in range(BANDS)])  11.8 us
    ppermute x3, starting transfers between devices, body(): earlier = [lax.ppermute(pairs, BOTH, later(d)) for d in range(1, MEMS + 1)]  11.3 us
    ppermute x1, starting transfers between devices, body(): far = lax.ppermute(pointer, BOTH, pointer_route(2))  6.26 us
    ppermute x1, starting transfers between devices, body(): near = lax.ppermute(pointer, BOTH, pointer_route(1))  5.36 us
    unnamed x27, local copies, waits for them, and re-layouts  4.72 us
    ppermute x1, starting transfers between devices, body(): lax.ppermute(bottom, 'space', [(i, i + 1) for i in range(BANDS - 1)])  3.45 us
  transfers between devices with their start and end apart: 17, of which 6 were waited for; matrix products, arithmetic and copies ran while one was open for 1% of the time, Pallas kernels for 19%

profile of v1, /device:TPU:13, one launch (start us, length us, event | category | flops | bytes accessed | tf_op | source)
XLA Modules:
  0.0 95.8 jit_solution(4808447030509523430)
XLA Ops:
  0.6 0.7 reshape.33.embed
  1.3 0.9 copy-done
  2.2 0.9 copy-done.2
  3.1 0.7 copy-done.5
  3.8 0.3 joined.1
  4.2 0.8 collective-permute-start.5
  4.9 3.4 %collective-permute-start = (bf16[64,256]{1,0:T(8,128)(2,1)S(1)}, bf16[64,256]{1,0:T(8,128)(2,1)S(1)}, u32[]{:S(2)}, u32[]{:S(2)}) collective-permute-start(bf16[64,256]{1,0:T(8,128)(2,1)S(1)} %get-tuple-element.22), channel_id=1, source_target_pairs={{0,1},{1,2},{2,3},{3,4},{4,5},{5,6},{6,7},{8,9},{9,10},{10,11},{11... | collective-permute-start | bytes 98312 | tf_op jit(solution)/shard_map/ppermute | solution.py:334
  8.4 1.9 %collective-permute-start.1 = (bf16[64,256]{1,0:T(8,128)(2,1)S(1)}, bf16[64,256]{1,0:T(8,128)(2,1)S(1)}, u32[]{:S(2)}, u32[]{:S(2)}) collective-permute-start(bf16[64,256]{1,0:T(8,128)(2,1)S(1)} %get-tuple-element.23), channel_id=1, source_target_pairs={{1,0},{2,1},{3,2},{4,3},{5,4},{6,5},{7,6},{9,8},{10,9},{11,10},{12... | collective-permute-start | bytes 98312 | tf_op jit(solution)/shard_map/ppermute | solution.py:335
  10.3 0.1 pad_add_fusion.3.refs_0_
  10.4 0.9 copy.17.w_out
  11.3 0.0 collective-permute-done.above
  11.3 2.3 %collective-permute-done.1.below = bf16[64,256]{1,0:T(8,128)(2,1)S(1)} collective-permute-done((bf16[64,256]{1,0:T(8,128)(2,1)S(1)}, bf16[64,256]{1,0:T(8,128)(2,1)S(1)}, u32[]{:S(2)}, u32[]{:S(2)}) %collective-permute-start.1) | collective-permute-done | bytes 32800 | tf_op jit(solution)/shard_map/ppermute | solution.py:335
  13.6 1.3 %copy-done.6 = bf16[3,3,256,256]{3,2,1,0:T(8,128)(2,1)S(1)} copy-done((bf16[3,3,256,256]{3,2,1,0:T(8,128)(2,1)S(1)}, bf16[3,3,256,256]{3,2,1,0:T(8,128)(2,1)}, u32[]{:S(2)}) %copy-start.6) | copy-done | bytes 1179672
  14.9 2.5 %conv.1 = (bf16[8,4096]{1,0:T(8,128)(2,1)}, bf16[256,128]{1,0:T(8,128)(2,1)S(1)}) custom-call(bf16[512,256]{1,0:T(8,128)(2,1)S(1)} %get-tuple-element.21.joined, bf16[64,256]{1,0:T(8,128)(2,1)S(1)} %collective-permute-done.above, bf16[64,256]{1,0:T(8,128)(2,1)S(1)} %collective-permute-done.1.below, bf16[3,768,256]{2,1,0:T(8,128)(2,1)S(1)} %bitcast.19, ...), custom_call_target="tpu_custom_call" | custom-call | flops 640000000 | bytes 1048576 | tf_op jit(solution)/shard_map/conv/pallas_call | solution.py:29
  17.4 3.0 %collective-permute-start.2 = (bf16[256,128]{1,0:T(8,128)(2,1)S(1)}, bf16[256,128]{1,0:T(8,128)(2,1)S(1)}, u32[]{:S(2)}, u32[]{:S(2)}) collective-permute-start(bf16[256,128]{1,0:T(8,128)(2,1)S(1)} %get-tuple-element.24), channel_id=1, source_target_pairs={{0,8},{1,9},{2,10},{3,11},{4,12},{5,13},{6,14},{7,15},{8,16},{9,17... | collective-permute-start | bytes 196616 | tf_op jit(solution)/shard_map/ppermute | solution.py:362
  20.4 4.3 %collective-permute-start.3 = (bf16[256,128]{1,0:T(8,128)(2,1)S(1)}, bf16[256,128]{1,0:T(8,128)(2,1)S(1)}, u32[]{:S(2)}, u32[]{:S(2)}) collective-permute-start(bf16[256,128]{1,0:T(8,128)(2,1)S(1)} %get-tuple-element.24), channel_id=1, source_target_pairs={{0,16},{1,17},{2,18},{3,19},{4,20},{5,21},{6,22},{7,23},{8,24},{9,... | collective-permute-start | bytes 196616 | tf_op jit(solution)/shard_map/ppermute | solution.py:362
  24.7 4.0 %collective-permute-start.4 = (bf16[256,128]{1,0:T(8,128)(2,1)S(1)}, bf16[256,128]{1,0:T(8,128)(2,1)S(1)}, u32[]{:S(2)}, u32[]{:S(2)}) collective-permute-start(bf16[256,128]{1,0:T(8,128)(2,1)S(1)} %get-tuple-element.24), channel_id=1, source_target_pairs={{0,24},{1,25},{2,26},{3,27},{4,28},{5,29},{6,30},{7,31},{14,32},{1... | collective-permute-start | bytes 196616 | tf_op jit(solution)/shard_map/ppermute | solution.py:362
  28.7 0.1 pad_add_fusion.2.refs_0_
  28.8 0.0 collective-permute-done.5
  28.8 3.5 %collective-permute-start.6 = (f32[1,256]{1,0:T(1,128)S(1)}, f32[1,256]{1,0:T(1,128)S(1)}, u32[]{:S(2)}, u32[]{:S(2)}) collective-permute-start(f32[1,256]{1,0:T(1,128)S(1)} %add.18), channel_id=1, source_target_pairs={{0,2},{1,3},{2,0},{3,1},{4,6},{5,7},{6,4},{7,5},{8,10},{9,11},{10,... | collective-permute-start | bytes 3080 | tf_op jit(solution)/shard_map/ppermute | solution.py:292
  32.3 0.4 query.1.refs_1_
  32.7 1.3 %collective-permute-done.6 = f32[1,256]{1,0:T(1,128)S(1)} collective-permute-done((f32[1,256]{1,0:T(1,128)S(1)}, f32[1,256]{1,0:T(1,128)S(1)}, u32[]{:S(2)}, u32[]{:S(2)}) %collective-permute-start.6) | collective-permute-done | bytes 1056 | tf_op jit(solution)/shard_map/ppermute | solution.py:292
  34.0 2.5 %collective-permute-start.7 = (f32[1,256]{1,0:T(1,128)S(1)}, f32[1,256]{1,0:T(1,128)S(1)}, u32[]{:S(2)}, u32[]{:S(2)}) collective-permute-start(f32[1,256]{1,0:T(1,128)S(1)} %add.19.mine), channel_id=1, source_target_pairs={{0,6},{1,7},{2,4},{3,5},{4,2},{5,3},{6,0},{7,1},{8,14},{9,15},{10,... | collective-permute-start | bytes 3080 | tf_op jit(solution)/shard_map/ppermute | solution.py:292
  36.5 1.8 %collective-permute-done.7.other = f32[1,256]{1,0:T(1,128)S(1)} collective-permute-done((f32[1,256]{1,0:T(1,128)S(1)}, f32[1,256]{1,0:T(1,128)S(1)}, u32[]{:S(2)}, u32[]{:S(2)}) %collective-permute-start.7) | collective-permute-done | bytes 1056 | tf_op jit(solution)/shard_map/ppermute | solution.py:292
  38.3 0.8 pointer.1
  39.1 5.4 %collective-permute-start.8 = (bf16[1,256]{1,0:T(2,128)(2,1)}, bf16[1,256]{1,0:T(2,128)(2,1)S(1)}, u32[]{:S(2)}, u32[]{:S(2)}) collective-permute-start(bf16[1,256]{1,0:T(2,128)(2,1)} %pointer.1), channel_id=1, source_target_pairs={{0,8},{8,16},{16,24},{1,25},{24,32},{9,33},{32,40},{17,41},{2,42},... | collective-permute-start | bytes 1544 | tf_op jit(solution)/shard_map/ppermute | solution.py:360
  44.5 6.3 %collective-permute-start.9 = (bf16[1,256]{1,0:T(2,128)(2,1)}, bf16[1,256]{1,0:T(2,128)(2,1)S(1)}, u32[]{:S(2)}, u32[]{:S(2)}) collective-permute-start(bf16[1,256]{1,0:T(2,128)(2,1)} %pointer.1), channel_id=1, source_target_pairs={{0,16},{8,24},{16,32},{1,33},{24,40},{9,41},{32,48},{17,49},{2,50}... | collective-permute-start | bytes 1544 | tf_op jit(solution)/shard_map/ppermute | solution.py:361
  50.8 3.0 %collective-permute-done.9.far = bf16[1,256]{1,0:T(2,128)(2,1)S(1)} collective-permute-done((bf16[1,256]{1,0:T(2,128)(2,1)}, bf16[1,256]{1,0:T(2,128)(2,1)S(1)}, u32[]{:S(2)}, u32[]{:S(2)}) %collective-permute-start.9) | collective-permute-done | bytes 544 | tf_op jit(solution)/shard_map/ppermute | solution.py:361
  53.8 0.0 collective-permute-done.3.second
  53.8 0.0 collective-permute-done.4.third
  53.8 0.1 collective-permute-start.16
  53.9 7.2 %collective-permute-start.14 = (bf16[784,128]{1,0:T(8,128)(2,1)S(1)}, bf16[784,128]{1,0:T(8,128)(2,1)S(1)}, u32[]{:S(2)}, u32[]{:S(2)}) collective-permute-start(bf16[784,128]{1,0:T(8,128)(2,1)S(1)} %payload.1.refs_6_), channel_id=1, source_target_pairs={{0,2},{1,3},{2,0},{3,1},{4,6},{5,7},{6,4},{7,5},{8,10},{9,11},{10,... | collective-permute-start | bytes 602120 | tf_op jit(solution)/shard_map/ppermute | solution.py:292
  61.1 0.0 collective-permute-start.10
  61.1 0.1 pad_add_fusion.1.refs_0_
  61.2 0.1 pad_add_fusion.refs_0_
  61.2 8.5 %collective-permute-done.10.refs_6_ = bf16[784,128]{1,0:T(8,128)(2,1)S(1)} collective-permute-done((bf16[784,128]{1,0:T(8,128)(2,1)S(1)}, bf16[784,128]{1,0:T(8,128)(2,1)S(1)}, u32[]{:S(2)}, u32[]{:S(2)}) %collective-permute-start.10) | collective-permute-done | bytes 200736 | tf_op jit(solution)/shard_map/ppermute | solution.py:292
  69.7 0.9 collective-permute-start.13
  70.6 2.2 %collective-permute-start.11 = (bf16[784,128]{1,0:T(8,128)(2,1)S(1)}, bf16[784,128]{1,0:T(8,128)(2,1)S(1)}, u32[]{:S(2)}, u32[]{:S(2)}) collective-permute-start(bf16[784,128]{1,0:T(8,128)(2,1)S(1)} %collective-permute-done.10.refs_6_), channel_id=1, source_target_pairs={{0,2},{1,3},{2,0},{3,1},{4,6},{5,7},{6,4},{7,5},{8,10},{9,11},{10,... | collective-permute-start | bytes 602120 | tf_op jit(solution)/shard_map/ppermute | solution.py:292
  72.8 0.3 collective-permute-start.15
  73.1 0.0 collective-permute-done.16.refs_7_
  73.1 4.8 %attention.4 = (f32[512,1]{1,0:T(8,128)S(1)}, f32[512,1]{1,0:T(8,128)S(1)}, f32[512,256]{1,0:T(8,128)S(1)}, f32[64,128]{1,0:T(8,128)S(1)}) custom-call(s32[3]{0:T(128)S(1)} %pad_add_fusion.3.refs_0_, bf16[512,256]{1,0:T(8,128)(2,1)S(1)} %query.1.refs_1_, bf16[64,256]{1,0:T(8,128)(2,1)S(1)} %copy-done.8, bf16[64,256]{1,0:T(8,128)(2,1)S(1)} %copy-done.9, ...), custom_call_target="tpu_custom_call" | custom-call | flops 2400000000 | bytes 1048576 | tf_op jit(solution)/shard_map/attention/pallas_call | solution.py:29
  77.9 0.2 collective-permute-done.11.refs_6_
  78.1 0.6 collective-permute-start.12
  78.7 4.7 %attention.5 = (f32[512,1]{1,0:T(8,128)S(1)}, f32[512,1]{1,0:T(8,128)S(1)}, f32[512,256]{1,0:T(8,128)S(1)}, f32[64,128]{1,0:T(8,128)S(1)}) custom-call(s32[3]{0:T(128)S(1)} %pad_add_fusion.2.refs_0_, bf16[512,256]{1,0:T(8,128)(2,1)S(1)} %query.1.refs_1_, bf16[64,256]{1,0:T(8,128)(2,1)S(1)} %copy-done.8, bf16[64,256]{1,0:T(8,128)(2,1)S(1)} %copy-done.9, ...), custom_call_target="tpu_custom_call" | custom-call | flops 2400000000 | bytes 1048576 | tf_op jit(solution)/shard_map/attention/pallas_call | solution.py:29
  83.4 0.0 collective-permute-done.13.refs_7_
  83.4 0.0 copy-start.7
  83.4 4.7 %attention.6 = (f32[512,1]{1,0:T(8,128)S(1)}, f32[512,1]{1,0:T(8,128)S(1)}, f32[512,256]{1,0:T(8,128)S(1)}, f32[64,128]{1,0:T(8,128)S(1)}) custom-call(s32[3]{0:T(128)S(1)} %pad_add_fusion.1.refs_0_, bf16[512,256]{1,0:T(8,128)(2,1)S(1)} %query.1.refs_1_, bf16[64,256]{1,0:T(8,128)(2,1)S(1)} %copy-done.8, bf16[64,256]{1,0:T(8,128)(2,1)S(1)} %copy-done.9, ...), custom_call_target="tpu_custom_call" | custom-call | flops 2400000000 | bytes 1048576 | tf_op jit(solution)/shard_map/attention/pallas_call | solution.py:29
  88.1 7.7 %attention.7 = bf16[512,256]{1,0:T(8,128)(2,1)} custom-call(s32[3]{0:T(128)S(1)} %pad_add_fusion.refs_0_, bf16[512,256]{1,0:T(8,128)(2,1)S(1)} %query.1.refs_1_, bf16[64,256]{1,0:T(8,128)(2,1)S(1)} %copy-done.8, bf16[64,256]{1,0:T(8,128)(2,1)S(1)} %copy-done.9, bf16[3,64]{1,0:T(4,128)(2,1)S(1)} %copy-done.10, bf16[1,64]{1,0:T(2,128)(2,1)S(1)} %bitcast.23, ...), custom_call_target="tpu_custom_call" | custom-call | flops 2400000000 | bytes 1048576 | tf_op jit(solution)/shard_map/attention/pallas_call | solution.py:29
  (30 shorter events, 0.1 us)
Async XLA Ops:
  1.3 0.9 copy-start
  2.2 0.9 copy-start.2
  3.1 0.7 copy-start.5
  4.2 24.6 %collective-permute-start.5 = (f32[1,256]{1,0:T(1,128)S(1)}, f32[1,256]{1,0:T(1,128)S(1)}, u32[]{:S(2)}, u32[]{:S(2)}) collective-permute-start(f32[1,256]{1,0:T(1,128)S(1)} %get-tuple-element.25), channel_id=1, source_target_pairs={{0,1},{1,0},{2,3},{3,2},{4,5},{5,4},{6,7},{7,6},{8,9},{9,8},{10,11... | collective-permute-start | bytes 3080 | tf_op jit(solution)/shard_map/ppermute | solution.py:292
  4.9 6.3 %collective-permute-start = (bf16[64,256]{1,0:T(8,128)(2,1)S(1)}, bf16[64,256]{1,0:T(8,128)(2,1)S(1)}, u32[]{:S(2)}, u32[]{:S(2)}) collective-permute-start(bf16[64,256]{1,0:T(8,128)(2,1)S(1)} %get-tuple-element.22), channel_id=1, source_target_pairs={{0,1},{1,2},{2,3},{3,4},{4,5},{5,6},{6,7},{8,9},{9,10},{10,11},{11... | collective-permute-start | bytes 98312 | tf_op jit(solution)/shard_map/ppermute | solution.py:334
  8.4 5.2 %collective-permute-start.1 = (bf16[64,256]{1,0:T(8,128)(2,1)S(1)}, bf16[64,256]{1,0:T(8,128)(2,1)S(1)}, u32[]{:S(2)}, u32[]{:S(2)}) collective-permute-start(bf16[64,256]{1,0:T(8,128)(2,1)S(1)} %get-tuple-element.23), channel_id=1, source_target_pairs={{1,0},{2,1},{3,2},{4,3},{5,4},{6,5},{7,6},{9,8},{10,9},{11,10},{12... | collective-permute-start | bytes 98312 | tf_op jit(solution)/shard_map/ppermute | solution.py:335
  13.6 1.3 %copy-start.6 = (bf16[3,3,256,256]{3,2,1,0:T(8,128)(2,1)S(1)}, bf16[3,3,256,256]{3,2,1,0:T(8,128)(2,1)}, u32[]{:S(2)}) copy-start(bf16[3,3,256,256]{3,2,1,0:T(8,128)(2,1)} %param.18) | copy-start | bytes 3538948
  14.9 17.4 %copy-start.1 = (bf16[1,8,64,256]{3,2,1,0:T(8,128)(2,1)S(1)}, bf16[1,8,64,256]{3,2,1,0:T(8,128)(2,1)}, u32[]{:S(2)}) copy-start(bf16[1,8,64,256]{3,2,1,0:T(8,128)(2,1)} %param.14) | copy-start | bytes 786436
  14.9 17.4 %copy-start.3 = (bf16[256,256]{1,0:T(8,128)(2,1)S(1)}, bf16[256,256]{1,0:T(8,128)(2,1)}, u32[]{:S(2)}) copy-start(bf16[256,256]{1,0:T(8,128)(2,1)} %w_query.1) | copy-start | bytes 393220
  14.9 23.4 %copy-start.4 = (bf16[256,256]{1,0:T(8,128)(2,1)S(1)}, bf16[256,256]{1,0:T(8,128)(2,1)}, u32[]{:S(2)}) copy-start(bf16[256,256]{1,0:T(8,128)(2,1)} %w_ptr.1) | copy-start | bytes 393220
  14.9 35.8 %copy-start.12 = (bf16[16,256]{1,0:T(8,128)(2,1)S(1)}, bf16[16,256]{1,0:T(8,128)(2,1)}, u32[]{:S(2)}) copy-start(bf16[16,256]{1,0:T(8,128)(2,1)} %param.26) | copy-start | bytes 24580
  17.4 55.7 %copy-start.8 = (bf16[64,256]{1,0:T(8,128)(2,1)S(1)}, bf16[64,256]{1,0:T(8,128)(2,1)}, u32[]{:S(2)}) copy-start(bf16[64,256]{1,0:T(8,128)(2,1)} %refs_2_.7) | copy-start | bytes 98308
  17.4 55.7 %copy-start.9 = (bf16[64,256]{1,0:T(8,128)(2,1)S(1)}, bf16[64,256]{1,0:T(8,128)(2,1)}, u32[]{:S(2)}) copy-start(bf16[64,256]{1,0:T(8,128)(2,1)} %refs_3_.7) | copy-start | bytes 98308
  17.4 55.7 %copy-start.10 = (bf16[3,64]{1,0:T(4,128)(2,1)S(1)}, bf16[3,64]{1,0:T(4,128)(2,1)}, u32[]{:S(2)}) copy-start(bf16[3,64]{1,0:T(4,128)(2,1)} %refs_4_.7) | copy-start | bytes 1156
  17.4 55.7 %copy-start.11 = (bf16[64]{0:T(256)(128)(2,1)S(1)}, bf16[64]{0:T(256)(128)(2,1)}, u32[]{:S(2)}) copy-start(bf16[64]{0:T(256)(128)(2,1)} %param.27) | copy-start | bytes 388
  17.4 36.4 %collective-permute-start.2 = (bf16[256,128]{1,0:T(8,128)(2,1)S(1)}, bf16[256,128]{1,0:T(8,128)(2,1)S(1)}, u32[]{:S(2)}, u32[]{:S(2)}) collective-permute-start(bf16[256,128]{1,0:T(8,128)(2,1)S(1)} %get-tuple-element.24), channel_id=1, source_target_pairs={{0,8},{1,9},{2,10},{3,11},{4,12},{5,13},{6,14},{7,15},{8,16},{9,17... | collective-permute-start | bytes 196616 | tf_op jit(solution)/shard_map/ppermute | solution.py:362
  20.4 33.4 %collective-permute-start.3 = (bf16[256,128]{1,0:T(8,128)(2,1)S(1)}, bf16[256,128]{1,0:T(8,128)(2,1)S(1)}, u32[]{:S(2)}, u32[]{:S(2)}) collective-permute-start(bf16[256,128]{1,0:T(8,128)(2,1)S(1)} %get-tuple-element.24), channel_id=1, source_target_pairs={{0,16},{1,17},{2,18},{3,19},{4,20},{5,21},{6,22},{7,23},{8,24},{9,... | collective-permute-start | bytes 196616 | tf_op jit(solution)/shard_map/ppermute | solution.py:362
  24.7 29.1 %collective-permute-start.4 = (bf16[256,128]{1,0:T(8,128)(2,1)S(1)}, bf16[256,128]{1,0:T(8,128)(2,1)S(1)}, u32[]{:S(2)}, u32[]{:S(2)}) collective-permute-start(bf16[256,128]{1,0:T(8,128)(2,1)S(1)} %get-tuple-element.24), channel_id=1, source_target_pairs={{0,24},{1,25},{2,26},{3,27},{4,28},{5,29},{6,30},{7,31},{14,32},{1... | collective-permute-start | bytes 196616 | tf_op jit(solution)/shard_map/ppermute | solution.py:362
  28.8 5.2 %collective-permute-start.6 = (f32[1,256]{1,0:T(1,128)S(1)}, f32[1,256]{1,0:T(1,128)S(1)}, u32[]{:S(2)}, u32[]{:S(2)}) collective-permute-start(f32[1,256]{1,0:T(1,128)S(1)} %add.18), channel_id=1, source_target_pairs={{0,2},{1,3},{2,0},{3,1},{4,6},{5,7},{6,4},{7,5},{8,10},{9,11},{10,... | collective-permute-start | bytes 3080 | tf_op jit(solution)/shard_map/ppermute | solution.py:292
  34.0 4.3 %collective-permute-start.7 = (f32[1,256]{1,0:T(1,128)S(1)}, f32[1,256]{1,0:T(1,128)S(1)}, u32[]{:S(2)}, u32[]{:S(2)}) collective-permute-start(f32[1,256]{1,0:T(1,128)S(1)} %add.19.mine), channel_id=1, source_target_pairs={{0,6},{1,7},{2,4},{3,5},{4,2},{5,3},{6,0},{7,1},{8,14},{9,15},{10,... | collective-permute-start | bytes 3080 | tf_op jit(solution)/shard_map/ppermute | solution.py:292
  39.1 11.7 %collective-permute-start.8 = (bf16[1,256]{1,0:T(2,128)(2,1)}, bf16[1,256]{1,0:T(2,128)(2,1)S(1)}, u32[]{:S(2)}, u32[]{:S(2)}) collective-permute-start(bf16[1,256]{1,0:T(2,128)(2,1)} %pointer.1), channel_id=1, source_target_pairs={{0,8},{8,16},{16,24},{1,25},{24,32},{9,33},{32,40},{17,41},{2,42},... | collective-permute-start | bytes 1544 | tf_op jit(solution)/shard_map/ppermute | solution.py:360
  44.5 9.3 %collective-permute-start.9 = (bf16[1,256]{1,0:T(2,128)(2,1)}, bf16[1,256]{1,0:T(2,128)(2,1)S(1)}, u32[]{:S(2)}, u32[]{:S(2)}) collective-permute-start(bf16[1,256]{1,0:T(2,128)(2,1)} %pointer.1), channel_id=1, source_target_pairs={{0,16},{8,24},{16,32},{1,33},{24,40},{9,41},{32,48},{17,49},{2,50}... | collective-permute-start | bytes 1544 | tf_op jit(solution)/shard_map/ppermute | solution.py:361
  53.8 19.2 %collective-permute-start.16 = (bf16[784,128]{1,0:T(8,128)(2,1)S(1)}, bf16[784,128]{1,0:T(8,128)(2,1)S(1)}, u32[]{:S(2)}, u32[]{:S(2)}) collective-permute-start(bf16[784,128]{1,0:T(8,128)(2,1)S(1)} %payload.1.refs_6_), channel_id=1, source_target_pairs={{0,1},{1,0},{2,3},{3,2},{4,5},{5,4},{6,7},{7,6},{8,9},{9,8},{10,11... | collective-permute-start | bytes 602120 | tf_op jit(solution)/shard_map/ppermute | solution.py:292
  53.9 18.9 %collective-permute-start.14 = (bf16[784,128]{1,0:T(8,128)(2,1)S(1)}, bf16[784,128]{1,0:T(8,128)(2,1)S(1)}, u32[]{:S(2)}, u32[]{:S(2)}) collective-permute-start(bf16[784,128]{1,0:T(8,128)(2,1)S(1)} %payload.1.refs_6_), channel_id=1, source_target_pairs={{0,2},{1,3},{2,0},{3,1},{4,6},{5,7},{6,4},{7,5},{8,10},{9,11},{10,... | collective-permute-start | bytes 602120 | tf_op jit(solution)/shard_map/ppermute | solution.py:292
  61.1 8.6 %collective-permute-start.10 = (bf16[784,128]{1,0:T(8,128)(2,1)S(1)}, bf16[784,128]{1,0:T(8,128)(2,1)S(1)}, u32[]{:S(2)}, u32[]{:S(2)}) collective-permute-start(bf16[784,128]{1,0:T(8,128)(2,1)S(1)} %payload.1.refs_6_), channel_id=1, source_target_pairs={{0,6},{1,7},{2,4},{3,5},{4,2},{5,3},{6,0},{7,1},{8,14},{9,15},{10,... | collective-permute-start | bytes 602120 | tf_op jit(solution)/shard_map/ppermute | solution.py:292
  69.7 13.7 %collective-permute-start.13 = (bf16[784,128]{1,0:T(8,128)(2,1)S(1)}, bf16[784,128]{1,0:T(8,128)(2,1)S(1)}, u32[]{:S(2)}, u32[]{:S(2)}) collective-permute-start(bf16[784,128]{1,0:T(8,128)(2,1)S(1)} %collective-permute-done.10.refs_6_), channel_id=1, source_target_pairs={{0,1},{1,0},{2,3},{3,2},{4,5},{5,4},{6,7},{7,6},{8,9},{9,8},{10,11... | collective-permute-start | bytes 602120 | tf_op jit(solution)/shard_map/ppermute | solution.py:292
  70.6 7.5 %collective-permute-start.11 = (bf16[784,128]{1,0:T(8,128)(2,1)S(1)}, bf16[784,128]{1,0:T(8,128)(2,1)S(1)}, u32[]{:S(2)}, u32[]{:S(2)}) collective-permute-start(bf16[784,128]{1,0:T(8,128)(2,1)S(1)} %collective-permute-done.10.refs_6_), channel_id=1, source_target_pairs={{0,2},{1,3},{2,0},{3,1},{4,6},{5,7},{6,4},{7,5},{8,10},{9,11},{10,... | collective-permute-start | bytes 602120 | tf_op jit(solution)/shard_map/ppermute | solution.py:292
  72.8 5.9 %collective-permute-start.15 = (bf16[784,128]{1,0:T(8,128)(2,1)S(1)}, bf16[784,128]{1,0:T(8,128)(2,1)S(1)}, u32[]{:S(2)}, u32[]{:S(2)}) collective-permute-start(bf16[784,128]{1,0:T(8,128)(2,1)S(1)} %collective-permute-done.14.refs_6_), channel_id=1, source_target_pairs={{0,1},{1,0},{2,3},{3,2},{4,5},{5,4},{6,7},{7,6},{8,9},{9,8},{10,11... | collective-permute-start | bytes 602120 | tf_op jit(solution)/shard_map/ppermute | solution.py:292
  78.1 9.9 %collective-permute-start.12 = (bf16[784,128]{1,0:T(8,128)(2,1)S(1)}, bf16[784,128]{1,0:T(8,128)(2,1)S(1)}, u32[]{:S(2)}, u32[]{:S(2)}) collective-permute-start(bf16[784,128]{1,0:T(8,128)(2,1)S(1)} %collective-permute-done.11.refs_6_), channel_id=1, source_target_pairs={{0,1},{1,0},{2,3},{3,2},{4,5},{5,4},{6,7},{7,6},{8,9},{9,8},{10,11... | collective-permute-start | bytes 602120 | tf_op jit(solution)/shard_map/ppermute | solution.py:292
  83.4 4.7 %copy-start.7 = (bf16[256,256]{1,0:T(8,128)(2,1)S(1)}, bf16[256,256]{1,0:T(8,128)(2,1)}, u32[]{:S(2)}) copy-start(bf16[256,256]{1,0:T(8,128)(2,1)} %refs_13_.1) | copy-start | bytes 393220

commit v2 on v1

v2 whole, which is shorter than its diff:
```python
import functools

import jax
import jax.numpy as jnp
from jax import lax
from jax.experimental import pallas as pl
from jax.experimental.pallas import tpu as pltpu
from jax.sharding import PartitionSpec as P

MEMS = 3
POINTERS = 16
FRAMES = 32
BANDS = 8
ROWS = 8
COLS = 64
TOK = ROWS * COLS
HALF = TOK // 2
D = 256
MEM = 64
PAY = MEMS * HALF
BOTH = ("tm", "space")
bf16 = jnp.bfloat16
f32 = jnp.float32
NT = (((1,), (1,)), ((), ()))


def call(
    kernel, out_shape, *args, scratch=(), in_specs=None, aliases=None, flops=0, limit=48, any_out=False, name=None
):
    vmem = pl.BlockSpec(memory_space=pltpu.VMEM)
    return pl.pallas_call(
        kernel,
        out_shape=out_shape,
        in_specs=[vmem] * len(args) if in_specs is None else in_specs,
        out_specs=jax.tree.map(
            lambda _: pl.BlockSpec(memory_space=pl.ANY) if any_out else vmem, out_shape
        ),
        scratch_shapes=list(scratch),
        input_output_aliases=aliases or {},
        compiler_params=pltpu.CompilerParams(vmem_limit_bytes=limit << 20),
        cost_estimate=pl.CostEstimate(flops=flops, bytes_accessed=1 << 20, transcendentals=0),
        name=name,
    )(*args)


def sds(shape, dtype):
    return jax.ShapeDtypeStruct(shape, dtype)


def fetch(pairs, sems):
    copies = [pltpu.make_async_copy(a, b, sems.at[i]) for i, (a, b) in enumerate(pairs)]
    for copy in copies:
        copy.start()
    return copies


def joined_kernel(*refs):
    sources, outputs, refs = refs[:5], refs[5:10], refs[10:]
    joined, top, bottom, pooled, query = outputs
    feat, w_pix, mask, embed, w_query, sems = refs
    copies = fetch(zip(sources, refs[:5]), sems)
    for copy in copies[:4]:
        copy.wait()
    columns = mask[...].astype(f32).T
    row = embed[...].reshape(1, D).astype(f32)
    total = jnp.zeros((8, D), f32)
    for r in range(ROWS):
        rows = feat[r * COLS : (r + 1) * COLS, :]
        column = columns[:, r : r + 1]
        value = jnp.dot(rows, w_pix[...], preferred_element_type=f32) + column * row
        value = value.astype(bf16)
        joined[r * COLS : (r + 1) * COLS, :] = value
        if r == 0:
            top[...] = value
        if r == ROWS - 1:
            bottom[...] = value
        picked = rows.astype(f32) * column
        for k in range(COLS // 8):
            total = total + picked[k * 8 : (k + 1) * 8, :]
    pooled[...] = jnp.sum(total, axis=0, keepdims=True)
    copies[4].wait()
    for r in range(0, TOK, 128):
        x = feat[r : r + 128, :].astype(f32)
        x = x - jnp.mean(x, axis=1, keepdims=True)
        x = x * lax.rsqrt(jnp.mean(x * x, axis=1, keepdims=True) + 1e-05)
        y = jnp.dot(x.astype(bf16), w_query[...], preferred_element_type=f32)
        query[r : r + 128, :] = (y * D ** (-0.5)).astype(bf16)


def conv_kernel(*refs):
    sources, (memory, pairs), refs = refs[:5], refs[5:7], refs[7:]
    joined, above, below, w_conv, w_out, wide, tokens, sems = refs
    near = fetch(zip(sources[:3], refs[:3]), sems)
    taps = [(sources[3].at[a], w_conv.at[a]) for a in range(3)]
    copies = fetch(taps + [(sources[4], w_out)], sems.at[pl.ds(3, 4)])
    for copy in near:
        copy.wait()
    side = lax.broadcasted_iota(jnp.int32, (COLS, D), 0)
    for r in range(ROWS + 2):
        if r == 0:
            row = above[...]
        elif r == ROWS + 1:
            row = below[...]
        else:
            row = joined[(r - 1) * COLS : r * COLS, :]
        value = row.astype(f32)
        left = jnp.where(side == 0, 0.0, pltpu.roll(value, 1, 0))
        right = jnp.where(side == COLS - 1, 0.0, pltpu.roll(value, COLS - 1, 0))
        here = slice(r * COLS, (r + 1) * COLS)
        wide[here, 0:D] = left.astype(bf16)
        wide[here, D : 2 * D] = row
        wide[here, 2 * D : 3 * D] = right.astype(bf16)
    for copy in copies:
        copy.wait()
    w_twice = jnp.concatenate([w_out[...], w_out[...]], axis=0)
    for part in range(4):
        start = part * 2 * COLS
        total = None
        for a in range(3):
            window = wide[start + a * COLS : start + a * COLS + 2 * COLS, :]
            term = jnp.dot(window, w_conv[a], preferred_element_type=f32)
            total = term if total is None else total + term
        hidden = 0.5 * total * (
            1.0 + jnp.tanh(0.7978845608028654 * (total + 0.044715 * (total * total * total)))
        )
        tokens[start : start + 2 * COLS, :] = lax.dot_general(
            hidden.astype(bf16), w_twice, NT, preferred_element_type=f32
        )
    lane = lax.broadcasted_iota(jnp.int32, (8, 128), 1)
    for k in range(COLS // 2):
        even = tokens[pl.ds(2 * k, ROWS, stride=COLS), :]
        odd = tokens[pl.ds(2 * k + 1, ROWS, stride=COLS), :]
        memory[:, k * 128 : (k + 1) * 128] = jnp.where(lane < MEM, even, odd).astype(bf16)
    lane = lax.broadcasted_iota(jnp.int32, (HALF, 128), 1)
    pairs[...] = jnp.where(lane < MEM, tokens[0:HALF, :], tokens[HALF:TOK, :]).astype(bf16)


def place_rows(pieces):
    row = lax.broadcasted_iota(jnp.int32, (16, 128), 0)
    out = jnp.zeros((16, 128), f32)
    for i, piece in enumerate(pieces):
        for half in range(2):
            out = jnp.where(row == 2 * i + half, piece[:, half * 128 : (half + 1) * 128], out)
    return out


def pair_kernel(mine, other, w_ptr, own, pointer, out):
    pooled = mine[...] + other[...]
    scale = lax.rsqrt(jnp.mean(pooled * pooled, axis=1, keepdims=True) + 1e-06)
    normed = jnp.broadcast_to(pooled * scale, (8, D)).astype(bf16)
    y = jnp.dot(normed, w_ptr[...], preferred_element_type=f32)[0:1, :].astype(bf16)
    pointer[...] = y
    out[0:HALF, :] = own[...]
    out[HALF : HALF + 16, :] = place_rows([y.astype(f32)]).astype(bf16)


def payload_kernel(couple, first, second, third, out, window):
    out[0:HALF, :] = first[...]
    out[HALF : 2 * HALF, :] = second[0:HALF, :]
    out[2 * HALF : 3 * HALF, :] = third[...]
    row = lax.broadcasted_iota(jnp.int32, (16, 128), 0)
    behind = second[HALF : HALF + 16, :].astype(f32)
    mine = couple[HALF : HALF + 16, :].astype(f32)
    behind = jnp.where((row == 2) | (row == 3), pltpu.roll(behind, 2, 0), 0.0)
    window[...] = (mine + behind).astype(bf16)


def twice(w):
    zero = jnp.zeros_like(w)
    return jnp.concatenate(
        [jnp.concatenate([w, zero], axis=1), jnp.concatenate([zero, w], axis=1)], axis=0
    )


QT = 256
HOLDERS = (0, 1, 2, 3, 6, 7, 4, 5)


def attention_kernel(count, first, last, *refs):
    refs = list(refs)
    query, w_key, w_value, mem_tpos, empty = refs[:5]
    refs = refs[5:]
    blocks, refs = refs[:count], refs[count:]
    if first:
        state_in = None
    else:
        state_in, refs = refs[:3], refs[3:]
    if last:
        tails, refs = refs[:BANDS], refs[BANDS:]
        feat, w_proj, ptr_tpos, attended, keys, values, shifts, top, norm, mixed, ptr_tok = refs
    else:
        top, norm, mixed, keys, values, shifts = refs
    frame = lax.axis_index("tm")
    wk = twice(w_key[...])
    wv = twice(w_value[...])
    padded = jnp.concatenate([mem_tpos[...], jnp.zeros((8 - MEMS, MEM), bf16)], axis=0)
    tpos_keys = jnp.dot(padded, w_key[...], preferred_element_type=f32)
    if first:
        token = jnp.broadcast_to(empty[...], (8, MEM))
        null_key = jnp.dot(token, w_key[...], preferred_element_type=f32).astype(bf16)
        null_value = jnp.dot(token, w_value[...], preferred_element_type=f32).astype(bf16)
        score = jnp.sum(
            query[...].astype(f32) * null_key[0:1, :].astype(f32), axis=1, keepdims=True
        )
        top[...] = score
        norm[...] = jnp.ones_like(score)
        mixed[...] = jnp.broadcast_to(null_value[0:1, :].astype(f32), (TOK, D))
    else:
        for source, target in zip(state_in, (top, norm, mixed)):
            target[...] = source[...]

    def update(rows, scores, value_rows):
        old = top[rows, :]
        new = jnp.maximum(old, jnp.max(scores, axis=1, keepdims=True))
        weights = jnp.exp(scores - new)
        fade = jnp.exp(old - new)
        norm[rows, :] = norm[rows, :] * fade + jnp.sum(weights, axis=1, keepdims=True)
        mixed[rows, :] = mixed[rows, :] * fade + jnp.dot(
            weights.astype(bf16), value_rows, preferred_element_type=f32
        )
        top[rows, :] = new

    tiles = [slice(q * QT, (q + 1) * QT) for q in range(TOK // QT)]
    shifts[...] = tpos_keys

    @pl.loop(0, jnp.minimum(frame, MEMS))
    def _(d):
        shift = shifts[pl.ds(d, 1), :]
        for b, block in enumerate(blocks):
            x = block[pl.ds(pl.multiple_of(d * HALF, HALF), HALF), :]
            base = b * TOK
            k = jnp.dot(x, wk, preferred_element_type=f32)
            v = jnp.dot(x, wv, preferred_element_type=f32).astype(bf16)
            keys[base : base + HALF, :] = (k[:, :D] + shift).astype(bf16)
            keys[base + HALF : base + TOK, :] = (k[:, D:] + shift).astype(bf16)
            values[base : base + HALF, :] = v[:, :D]
            values[base + HALF : base + TOK, :] = v[:, D:]
        found = [
            lax.dot_general(query[rows, :], keys[...], NT, preferred_element_type=f32)
            for rows in tiles
        ]
        for rows, scores in zip(tiles, found):
            update(rows, scores, values[...])

    if last:
        widened = jnp.dot(ptr_tpos[...], wk, preferred_element_type=f32)
        lane = lax.broadcasted_iota(jnp.int32, (1, POINTERS * 4), 1)
        here = lax.axis_index("space")
        for tail, holder in zip(tails, HOLDERS):
            at = pl.ds(pl.multiple_of((here ^ holder) * 8, 8), 8)
            ptr_tok[at, :] = tail[...].astype(f32)[0:8, :]
        rows = [(2 * (i // 4) + i % 2) * 8 + 2 * (i % 4 // 2) for i in range(POINTERS)]
        tok = jnp.concatenate([ptr_tok[r : r + 2, :] for r in rows], axis=0).astype(bf16)
        k = (jnp.dot(tok, wk, preferred_element_type=f32) + widened).astype(bf16)
        v = jnp.dot(tok, wv, preferred_element_type=f32).astype(bf16)
        valid = frame >= (lane % (POINTERS * 2)) // 2 + 1
        k = jnp.concatenate([k[:, :D], k[:, D:]], axis=0)
        v = jnp.concatenate([v[:, :D], v[:, D:]], axis=0)
        for rows in tiles:
            scores = lax.dot_general(query[rows, :], k, NT, preferred_element_type=f32)
            update(rows, jnp.where(valid, scores, -jnp.inf), v)
        for rows in tiles:
            final = (mixed[rows, :] / norm[rows, :]).astype(bf16)
            attended[rows, :] = (
                feat[rows, :].astype(f32)
                + jnp.dot(final, w_proj[...], preferred_element_type=f32)
            ).astype(bf16)


def order_kernel(value, earlier, out):
    pass


def after(value, earlier):
    return call(
        order_kernel,
        sds(value.shape, value.dtype),
        value,
        earlier,
        in_specs=[pl.BlockSpec(memory_space=pl.ANY)] * 2,
        aliases={0: 0},
        any_out=True,
        name="order",
    )


def attend(query, weights, blocks, state=None, final=None):
    vmem = pl.BlockSpec(memory_space=pltpu.VMEM)
    args = [query, *weights, *blocks]
    specs = [vmem] * len(args)
    if state is not None:
        args += list(state)
        specs += [vmem] * 3
    state_shape = [((TOK, 1), f32), ((TOK, 1), f32), ((TOK, D), f32)]
    scratch = [pltpu.VMEM((len(blocks) * TOK, D), bf16)] * 2 + [pltpu.VMEM((8, D), f32)]
    if final is None:
        out = tuple(sds(*s) for s in state_shape)
    else:
        args += final
        specs += [vmem] * len(final)
        out = sds((TOK, D), bf16)
        scratch += [pltpu.VMEM(*s) for s in state_shape] + [pltpu.VMEM((BANDS * 8, 128), f32)]
    return call(
        functools.partial(attention_kernel, len(blocks), state is None, final is not None),
        out,
        *args,
        in_specs=specs,
        scratch=scratch,
        flops=len(blocks) * 1_200_000_000,
        name="attention",
    )


def mirrored(source, target, s):
    if (source // 4) % 2 == (target // 4) % 2:
        return s
    return across(s)


def later(distance):
    return [
        ((t - distance) * BANDS + mirrored(t - distance, t, s), t * BANDS + s)
        for t in range(distance, FRAMES)
        for s in range(BANDS)
    ]


def pointer_distance(s):
    return 4 * (s // 2) + s % 2 + 1


def pointer_route():
    pairs = []
    for t in range(FRAMES):
        for s in range(BANDS):
            source = t - pointer_distance(s)
            if source >= 0:
                pairs.append((source * BANDS + s, t * BANDS + s))
    return pairs


def over_space(x, target):
    return lax.ppermute(x, "space", [(i, target(i)) for i in range(BANDS)])


def sibling(i):
    return i ^ 1


def beside(i):
    return i ^ 2


def opposite(i):
    return i ^ 4


def across(i):
    return i ^ 6


def body(
    features,
    masks,
    w_pix,
    mask_embed,
    w_conv,
    w_out,
    w_ptr,
    w_query,
    w_key,
    w_value,
    w_proj,
    mem_tpos,
    ptr_tpos,
    empty_memory,
):
    feat = features.reshape(TOK, D)
    far = pl.BlockSpec(memory_space=pl.ANY)
    vmem = pl.BlockSpec(memory_space=pltpu.VMEM)
    joined, top, bottom, pooled, query = call(
        joined_kernel,
        (
            sds((TOK, D), bf16),
            sds((COLS, D), bf16),
            sds((COLS, D), bf16),
            sds((1, D), f32),
            sds((TOK, D), bf16),
        ),
        feat,
        w_pix,
        masks.reshape(ROWS, COLS),
        mask_embed,
        w_query,
        in_specs=[far] * 5,
        scratch=[
            pltpu.VMEM((TOK, D), bf16),
            pltpu.VMEM((D, D), bf16),
            pltpu.VMEM((ROWS, COLS), jnp.int32),
            pltpu.VMEM((D,), bf16),
            pltpu.VMEM((D, D), bf16),
            pltpu.SemaphoreType.DMA((5,)),
        ],
        flops=140_000_000,
        limit=60,
        name="joined",
    )
    above = lax.ppermute(bottom, "space", [(i, i + 1) for i in range(BANDS - 1)])
    below = lax.ppermute(top, "space", [(i + 1, i) for i in range(BANDS - 1)])
    pooled = pooled + over_space(pooled, sibling)
    pooled = pooled + over_space(pooled, beside)
    above = after(above, pooled)
    memory, pairs = call(
        conv_kernel,
        (sds((ROWS, COLS * MEM), bf16), sds((HALF, 128), bf16)),
        joined,
        above,
        below,
        w_conv.reshape(3, 3 * D, D),
        w_out.T,
        in_specs=[far] * 5,
        scratch=[
            pltpu.VMEM((TOK, D), bf16),
            pltpu.VMEM((COLS, D), bf16),
            pltpu.VMEM((COLS, D), bf16),
            pltpu.VMEM((3, 3 * D, D), bf16),
            pltpu.VMEM((MEM, D), bf16),
            pltpu.VMEM(((ROWS + 2) * COLS, 3 * D), bf16),
            pltpu.VMEM((TOK, 128), f32),
            pltpu.SemaphoreType.DMA((7,)),
        ],
        flops=640_000_000,
        limit=60,
        name="conv",
    )
    first = lax.ppermute(pairs, BOTH, later(1))
    third = lax.ppermute(pairs, BOTH, later(3))
    pointer, couple = call(
        pair_kernel,
        (sds((1, D), bf16), sds((HALF + 16, 128), bf16)),
        pooled,
        over_space(pooled, opposite),
        w_ptr,
        pairs,
        flops=1_000_000,
        name="pair",
    )
    second = lax.ppermute(couple, BOTH, later(2))
    own, window = call(
        payload_kernel,
        (sds((PAY, 128), bf16), sds((16, 128), bf16)),
        couple,
        first,
        second,
        third,
        name="payload",
    )

    weights = (w_key, w_value, mem_tpos, empty_memory.reshape(1, MEM))

    one = over_space(own, beside)
    two = over_space(own, across)
    tail = lax.ppermute(window, BOTH, pointer_route())
    state = attend(query, weights, [own, over_space(own, sibling)])
    two = after(two, state[2])
    tail = after(tail, state[2])
    three = over_space(two, beside)
    tails = [tail, over_space(tail, beside), over_space(tail, across)]
    state = attend(query, weights, [one, over_space(one, sibling)], state)
    three = after(three, state[2])
    tails[2] = after(tails[2], state[2])
    tails.append(over_space(tails[2], beside))
    state = attend(query, weights, [two, over_space(two, sibling)], state)
    attended = attend(
        query,
        weights,
        [three, over_space(three, sibling)],
        state,
        [
            *(x for t in tails for x in (t, over_space(t, sibling))),
            feat,
            w_proj,
            ptr_tpos.reshape(POINTERS * 2, 128),
        ],
    )
    return (
        attended.reshape(1, ROWS, COLS, D),
        memory.reshape(1, ROWS, COLS * MEM),
        pointer,
    )


def solution(mesh):
    return jax.shard_map(
        body,
        mesh=mesh,
        in_specs=(
            P("tm", "space", None, None),
            P("tm", "space", None),
            P(),
            P(),
            P(),
            P(),
            P(),
            P(),
            P(),
            P(),
            P(),
            P(),
            P(),
            P(),
        ),
        out_specs=(P("tm", "space", None, None), P("tm", "space", None), P("tm", None)),
        check_vma=False,
    )
```

time: 97.1 us -> 83 us (0.85)
  waiting for transfers between devices: 17.2 us -> 9.3 us
  local copies, waits for them, and re-layouts: 5.39 us -> 2.08 us
  starting transfers between devices: 46.2 us -> 43.5 us
    ppermute x5 -> x4, starting transfers between devices: 22.9 us -> 13 us  [the longest x1 5.42 us: body(): second = lax.ppermute(couple, BOTH, later(2))]
    ppermute x10 -> x17, waiting for transfers between devices: 11.8 us -> 2.65 us  [over_space(): return lax.ppermute(x, 'space', [(i, target(i)) for i in range(BANDS)])]
    ppermute x10 -> x17, starting transfers between devices: 18 us -> 24.4 us  [over_space(): return lax.ppermute(x, 'space', [(i, target(i)) for i in range(BANDS)])]
    ppermute x5 -> x4, waiting for transfers between devices: 3.02 us -> 6.65 us  [the longest x1 6.64 us: body(): third = lax.ppermute(pairs, BOTH, later(3))]
    unnamed x27 -> x24, local copies, waits for them, and re-layouts: 4.72 us -> 2.07 us
    ppermute x1, waiting for transfers between devices: 2.33 us -> 0.01 us  [body(): below = lax.ppermute(top, 'space', [(i + 1, i) for i in range(BANDS - 1)])]
    pallas_call x9 -> x13, Pallas kernels: 25.9 us -> 25.7 us  [call(): pl.pallas_call(kernel, out_shape=out_shape, in_specs=[vmem] * len(args) i...]
  transfers between devices with their start and end apart: 17 -> 23, of which waited for: 6 -> 4; matrix products, arithmetic and copies ran while one was open for 1% -> 1% of each run, Pallas kernels for 19% -> 20%
where the time goes in v2:
time: 83 us; the launch traced here: 82.1 us
  starting transfers between devices  43.5 us (52%)
  Pallas kernels  25.7 us (31%)
  waiting for transfers between devices  9.3 us (11%)
  local copies, waits for them, and re-layouts  2.08 us (3%)
  between operations  0.92 us (1%)
    pallas_call x13, Pallas kernels, call(): pl.pallas_call(kernel, out_shape=out_shape, in_specs=[vmem] * len(args) i...  25.7 us
    ppermute x17, starting transfers between devices, over_space(): return lax.ppermute(x, 'space', [(i, target(i)) for i in range(BANDS)])  24.4 us
    ppermute x1, waiting for transfers between devices, body(): third = lax.ppermute(pairs, BOTH, later(3))  6.64 us
    ppermute x1, starting transfers between devices, body(): second = lax.ppermute(couple, BOTH, later(2))  5.42 us
    ppermute x1, starting transfers between devices, body(): lax.ppermute(bottom, 'space', [(i, i + 1) for i in range(BANDS - 1)])  4.11 us
    ppermute x1, starting transfers between devices, body(): first = lax.ppermute(pairs, BOTH, later(1))  3.72 us
    ppermute x17, waiting for transfers between devices, over_space(): return lax.ppermute(x, 'space', [(i, target(i)) for i in range(BANDS)])  2.65 us
    unnamed x24, local copies, waits for them, and re-layouts  2.07 us
  transfers between devices with their start and end apart: 23, of which 4 were waited for; matrix products, arithmetic and copies ran while one was open for 1% of the time, Pallas kernels for 20%

profile of v2, /device:TPU:13, one launch (start us, length us, event | category | flops | bytes accessed | tf_op | source)
XLA Modules:
  0.0 82.1 jit_solution(4374743910765699125)
XLA Ops:
  0.6 2.5 %joined.1 = (bf16[512,256]{1,0:T(8,128)(2,1)}, bf16[64,256]{1,0:T(8,128)(2,1)}, bf16[64,256]{1,0:T(8,128)(2,1)}, f32[1,256]{1,0:T(1,128)}, bf16[512,256]{1,0:T(8,128)(2,1)}) custom-call(bf16[512,256]{1,0:T(8,128)(2,1)} %bitcast.7, bf16[256,256]{1,0:T(8,128)(2,1)} %refs_1_.5, s32[8,64]{1,0:T(8,128)} %bitcast.13, bf16[256]{0:T(256)(128)(2,1)} %refs_3_.5, ...), custom_call_target="tpu_custom_call" | custom-call | flops 140000000 | bytes 1048576 | tf_op jit(solution)/shard_map/joined/pallas_call | solution.py:31
  3.1 4.1 %collective-permute-start.3 = (bf16[64,256]{1,0:T(8,128)(2,1)}, bf16[64,256]{1,0:T(8,128)(2,1)S(1)}, u32[]{:S(2)}, u32[]{:S(2)}) collective-permute-start(bf16[64,256]{1,0:T(8,128)(2,1)} %get-tuple-element.26), channel_id=1, source_target_pairs={{0,1},{1,2},{2,3},{3,4},{4,5},{5,6},{6,7},{8,9},{9,10},{10,11},{11... | collective-permute-start | bytes 98312 | tf_op jit(solution)/shard_map/ppermute | solution.py:408
  7.2 1.9 %collective-permute-start.4 = (bf16[64,256]{1,0:T(8,128)(2,1)}, bf16[64,256]{1,0:T(8,128)(2,1)S(1)}, u32[]{:S(2)}, u32[]{:S(2)}) collective-permute-start(bf16[64,256]{1,0:T(8,128)(2,1)} %get-tuple-element.27), channel_id=1, source_target_pairs={{1,0},{2,1},{3,2},{4,3},{5,4},{6,5},{7,6},{9,8},{10,9},{11,10},{12... | collective-permute-start | bytes 98312 | tf_op jit(solution)/shard_map/ppermute | solution.py:409
  9.2 0.1 collective-permute-start
  9.3 1.3 %collective-permute-done = f32[1,256]{1,0:T(1,128)S(1)} collective-permute-done((f32[1,256]{1,0:T(1,128)}, f32[1,256]{1,0:T(1,128)S(1)}, u32[]{:S(2)}, u32[]{:S(2)}) %collective-permute-start) | collective-permute-done | bytes 1056 | tf_op jit(solution)/shard_map/ppermute | solution.py:343
  10.6 0.7 add.6
  11.3 1.6 %collective-permute-start.1 = (f32[1,256]{1,0:T(1,128)S(1)}, f32[1,256]{1,0:T(1,128)S(1)}, u32[]{:S(2)}, u32[]{:S(2)}) collective-permute-start(f32[1,256]{1,0:T(1,128)S(1)} %add.6), channel_id=1, source_target_pairs={{0,2},{1,3},{2,0},{3,1},{4,6},{5,7},{6,4},{7,5},{8,10},{9,11},{10,... | collective-permute-start | bytes 3080 | tf_op jit(solution)/shard_map/ppermute | solution.py:343
  12.9 1.0 %collective-permute-done.1 = f32[1,256]{1,0:T(1,128)S(1)} collective-permute-done((f32[1,256]{1,0:T(1,128)S(1)}, f32[1,256]{1,0:T(1,128)S(1)}, u32[]{:S(2)}, u32[]{:S(2)}) %collective-permute-start.1) | collective-permute-done | bytes 1056 | tf_op jit(solution)/shard_map/ppermute | solution.py:343
  13.9 2.9 %collective-permute-start.2 = (f32[1,256]{1,0:T(1,128)S(1)}, f32[1,256]{1,0:T(1,128)S(1)}, u32[]{:S(2)}, u32[]{:S(2)}) collective-permute-start(f32[1,256]{1,0:T(1,128)S(1)} %add.7.earlier.mine), channel_id=1, source_target_pairs={{0,4},{1,5},{2,6},{3,7},{4,0},{5,1},{6,2},{7,3},{8,12},{9,13},{10,... | collective-permute-start | bytes 3080 | tf_op jit(solution)/shard_map/ppermute | solution.py:343
  16.8 0.6 copy-done.3
  17.4 0.6 copy-done.11
  18.0 0.0 copy-start.8
  18.0 0.0 copy-start.9
  18.0 4.1 %conv.1 = (bf16[8,4096]{1,0:T(8,128)(2,1)}, bf16[256,128]{1,0:T(8,128)(2,1)}) custom-call(bf16[512,256]{1,0:T(8,128)(2,1)} %get-tuple-element.25.refs_0_, bf16[64,256]{1,0:T(8,128)(2,1)} %copy-done.3, bf16[64,256]{1,0:T(8,128)(2,1)} %copy-done.11, bf16[3,768,256]{2,1,0:T(8,128)(2,1)} %bitcast.14, bf16[64,256]{1,0:T(8,128)(2,1)} %bitcast.15), custom_call_target="tpu_custom_call" | custom-call | flops 640000000 | bytes 1048576 | tf_op jit(solution)/shard_map/conv/pallas_call | solution.py:31
  22.1 0.0 collective-permute-done.2.other
  22.1 0.8 %copy-done.2 = bf16[256,128]{1,0:T(8,128)(2,1)S(1)} copy-done((bf16[256,128]{1,0:T(8,128)(2,1)S(1)}, bf16[256,128]{1,0:T(8,128)(2,1)}, u32[]{:S(2)}) %copy-start.2) | copy-done | bytes 65560
  23.0 0.8 pair.1
  23.7 5.4 %collective-permute-start.6 = (bf16[272,128]{1,0:T(8,128)(2,1)S(1)}, bf16[272,128]{1,0:T(8,128)(2,1)S(1)}, u32[]{:S(2)}, u32[]{:S(2)}) collective-permute-start(bf16[272,128]{1,0:T(8,128)(2,1)S(1)} %get-tuple-element.29.couple), channel_id=1, source_target_pairs={{0,16},{1,17},{2,18},{3,19},{4,20},{5,21},{6,22},{7,23},{8,24},{9,... | collective-permute-start | bytes 208904 | tf_op jit(solution)/shard_map/ppermute | solution.py:448
  29.2 3.7 %collective-permute-start.5 = (bf16[256,128]{1,0:T(8,128)(2,1)}, bf16[256,128]{1,0:T(8,128)(2,1)S(1)}, u32[]{:S(2)}, u32[]{:S(2)}) collective-permute-start(bf16[256,128]{1,0:T(8,128)(2,1)} %get-tuple-element.28.own), channel_id=1, source_target_pairs={{0,8},{1,9},{2,10},{3,11},{4,12},{5,13},{6,14},{7,15},{8,16},{9,17... | collective-permute-start | bytes 196616 | tf_op jit(solution)/shard_map/ppermute | solution.py:436
  32.9 2.0 %collective-permute-start.7 = (bf16[256,128]{1,0:T(8,128)(2,1)}, bf16[256,128]{1,0:T(8,128)(2,1)S(1)}, u32[]{:S(2)}, u32[]{:S(2)}) collective-permute-start(bf16[256,128]{1,0:T(8,128)(2,1)} %get-tuple-element.28.own), channel_id=1, source_target_pairs={{0,24},{1,25},{2,26},{3,27},{4,28},{5,29},{6,30},{7,31},{14,32},{1... | collective-permute-start | bytes 196616 | tf_op jit(solution)/shard_map/ppermute | solution.py:437
  34.9 6.6 %collective-permute-done.7.third = bf16[256,128]{1,0:T(8,128)(2,1)S(1)} collective-permute-done((bf16[256,128]{1,0:T(8,128)(2,1)}, bf16[256,128]{1,0:T(8,128)(2,1)S(1)}, u32[]{:S(2)}, u32[]{:S(2)}) %collective-permute-start.7) | collective-permute-done | bytes 65568 | tf_op jit(solution)/shard_map/ppermute | solution.py:437
  41.5 0.0 collective-permute-done.6.second
  41.6 2.4 %collective-permute-start.11 = (bf16[768,128]{1,0:T(8,128)(2,1)S(1)}, bf16[768,128]{1,0:T(8,128)(2,1)S(1)}, u32[]{:S(2)}, u32[]{:S(2)}) collective-permute-start(bf16[768,128]{1,0:T(8,128)(2,1)S(1)} %get-tuple-element.30.refs_5_), channel_id=1, source_target_pairs={{0,2},{1,3},{2,0},{3,1},{4,6},{5,7},{6,4},{7,5},{8,10},{9,11},{10,... | collective-permute-start | bytes 589832 | tf_op jit(solution)/shard_map/ppermute | solution.py:343
  43.9 4.2 %collective-permute-start.9 = (bf16[768,128]{1,0:T(8,128)(2,1)S(1)}, bf16[768,128]{1,0:T(8,128)(2,1)S(1)}, u32[]{:S(2)}, u32[]{:S(2)}) collective-permute-start(bf16[768,128]{1,0:T(8,128)(2,1)S(1)} %get-tuple-element.30.refs_5_), channel_id=1, source_target_pairs={{0,1},{1,0},{2,3},{3,2},{4,5},{5,4},{6,7},{7,6},{8,9},{9,8},{10,11... | collective-permute-start | bytes 589832 | tf_op jit(solution)/shard_map/ppermute | solution.py:343
  48.1 2.7 %collective-permute-start.8 = (bf16[768,128]{1,0:T(8,128)(2,1)S(1)}, bf16[768,128]{1,0:T(8,128)(2,1)S(1)}, u32[]{:S(2)}, u32[]{:S(2)}) collective-permute-start(bf16[768,128]{1,0:T(8,128)(2,1)S(1)} %get-tuple-element.30.refs_5_), channel_id=1, source_target_pairs={{0,6},{1,7},{2,4},{3,5},{4,2},{5,3},{6,0},{7,1},{8,14},{9,15},{10,... | collective-permute-start | bytes 589832 | tf_op jit(solution)/shard_map/ppermute | solution.py:343
  50.8 1.9 %collective-permute-start.15 = (bf16[16,128]{1,0:T(8,128)(2,1)S(1)}, bf16[16,128]{1,0:T(8,128)(2,1)S(1)}, u32[]{:S(2)}, u32[]{:S(2)}) collective-permute-start(bf16[16,128]{1,0:T(8,128)(2,1)S(1)} %get-tuple-element.40), channel_id=1, source_target_pairs={{0,8},{8,16},{1,17},{16,24},{9,25},{24,32},{17,33},{32,40},{25,41}... | collective-permute-start | bytes 12296 | tf_op jit(solution)/shard_map/ppermute | solution.py:463
  52.7 0.4 collective-permute-start.12
  53.1 0.0 collective-permute-done.9.refs_6_
  53.1 4.2 %attention.4 = (f32[512,1]{1,0:T(8,128)S(1)}, f32[512,1]{1,0:T(8,128)S(1)}, f32[512,256]{1,0:T(8,128)S(1)}) custom-call(bf16[512,256]{1,0:T(8,128)(2,1)S(1)} %copy-done.4, bf16[64,256]{1,0:T(8,128)(2,1)S(1)} %copy-done.6, bf16[64,256]{1,0:T(8,128)(2,1)S(1)} %copy-done.7, bf16[3,64]{1,0:T(4,128)(2,1)S(1)} %copy-done.8, bf16[1,64]{1,0:T(2,128)(2,1)S(1)} %bitcast.9, ...), custom_call_target="tpu_custom_call" | custom-call | flops 2400000000 | bytes 1048576 | tf_op jit(solution)/shard_map/attention/pallas_call | solution.py:31
  57.3 0.0 collective-permute-done.8.value
  57.3 1.7 %collective-permute-start.14 = (bf16[768,128]{1,0:T(8,128)(2,1)S(1)}, bf16[768,128]{1,0:T(8,128)(2,1)S(1)}, u32[]{:S(2)}, u32[]{:S(2)}) collective-permute-start(bf16[768,128]{1,0:T(8,128)(2,1)S(1)} %order.6.refs_5_), channel_id=1, source_target_pairs={{0,1},{1,0},{2,3},{3,2},{4,5},{5,4},{6,7},{7,6},{8,9},{9,8},{10,11... | collective-permute-start | bytes 589832 | tf_op jit(solution)/shard_map/ppermute | solution.py:343
  59.0 0.8 %collective-permute-start.10 = (bf16[768,128]{1,0:T(8,128)(2,1)S(1)}, bf16[768,128]{1,0:T(8,128)(2,1)S(1)}, u32[]{:S(2)}, u32[]{:S(2)}) collective-permute-start(bf16[768,128]{1,0:T(8,128)(2,1)S(1)} %order.6.refs_5_), channel_id=1, source_target_pairs={{0,2},{1,3},{2,0},{3,1},{4,6},{5,7},{6,4},{7,5},{8,10},{9,11},{10,... | collective-permute-start | bytes 589832 | tf_op jit(solution)/shard_map/ppermute | solution.py:343
  59.9 0.0 collective-permute-done.15.value
  59.9 2.5 %collective-permute-start.19 = (bf16[16,128]{1,0:T(8,128)(2,1)S(1)}, bf16[16,128]{1,0:T(8,128)(2,1)S(1)}, u32[]{:S(2)}, u32[]{:S(2)}) collective-permute-start(bf16[16,128]{1,0:T(8,128)(2,1)S(1)} %order.8.refs_10_), channel_id=1, source_target_pairs={{0,6},{1,7},{2,4},{3,5},{4,2},{5,3},{6,0},{7,1},{8,14},{9,15},{10,... | collective-permute-start | bytes 12296 | tf_op jit(solution)/shard_map/ppermute | solution.py:343
  62.4 4.1 %attention.5 = (f32[512,1]{1,0:T(8,128)S(1)}, f32[512,1]{1,0:T(8,128)S(1)}, f32[512,256]{1,0:T(8,128)S(1)}) custom-call(bf16[512,256]{1,0:T(8,128)(2,1)S(1)} %copy-done.4, bf16[64,256]{1,0:T(8,128)(2,1)S(1)} %copy-done.6, bf16[64,256]{1,0:T(8,128)(2,1)S(1)} %copy-done.7, bf16[3,64]{1,0:T(4,128)(2,1)S(1)} %copy-done.8, bf16[1,64]{1,0:T(2,128)(2,1)S(1)} %bitcast.10, ...), custom_call_target="tpu_custom_call" | custom-call | flops 2400000000 | bytes 1048576 | tf_op jit(solution)/shard_map/attention/pallas_call | solution.py:31
  66.5 0.3 collective-permute-done.19.value
  66.8 1.2 %collective-permute-start.21 = (bf16[16,128]{1,0:T(8,128)(2,1)S(1)}, bf16[16,128]{1,0:T(8,128)(2,1)S(1)}, u32[]{:S(2)}, u32[]{:S(2)}) collective-permute-start(bf16[16,128]{1,0:T(8,128)(2,1)S(1)} %order.9.refs_14_), channel_id=1, source_target_pairs={{0,2},{1,3},{2,0},{3,1},{4,6},{5,7},{6,4},{7,5},{8,10},{9,11},{10,... | collective-permute-start | bytes 12296 | tf_op jit(solution)/shard_map/ppermute | solution.py:343
  68.0 1.8 %collective-permute-start.16 = (bf16[16,128]{1,0:T(8,128)(2,1)S(1)}, bf16[16,128]{1,0:T(8,128)(2,1)S(1)}, u32[]{:S(2)}, u32[]{:S(2)}) collective-permute-start(bf16[16,128]{1,0:T(8,128)(2,1)S(1)} %order.8.refs_10_), channel_id=1, source_target_pairs={{0,1},{1,0},{2,3},{3,2},{4,5},{5,4},{6,7},{7,6},{8,9},{9,8},{10,11... | collective-permute-start | bytes 12296 | tf_op jit(solution)/shard_map/ppermute | solution.py:343
  69.8 0.0 collective-permute-done.17.refs_12_
  69.8 0.1 collective-permute-start.18
  69.9 0.0 collective-permute-done.10.value
  69.9 0.4 collective-permute-start.20
  70.3 0.0 collective-permute-done.14.refs_6_
  70.3 0.1 collective-permute-start.13
  70.5 1.5 %collective-permute-start.22 = (bf16[16,128]{1,0:T(8,128)(2,1)S(1)}, bf16[16,128]{1,0:T(8,128)(2,1)S(1)}, u32[]{:S(2)}, u32[]{:S(2)}) collective-permute-start(bf16[16,128]{1,0:T(8,128)(2,1)S(1)} %collective-permute-done.21.refs_16_), channel_id=1, source_target_pairs={{0,1},{1,0},{2,3},{3,2},{4,5},{5,4},{6,7},{7,6},{8,9},{9,8},{10,11... | collective-permute-start | bytes 12296 | tf_op jit(solution)/shard_map/ppermute | solution.py:343
  72.0 4.0 %attention.6 = (f32[512,1]{1,0:T(8,128)S(1)}, f32[512,1]{1,0:T(8,128)S(1)}, f32[512,256]{1,0:T(8,128)S(1)}) custom-call(bf16[512,256]{1,0:T(8,128)(2,1)S(1)} %copy-done.4, bf16[64,256]{1,0:T(8,128)(2,1)S(1)} %copy-done.6, bf16[64,256]{1,0:T(8,128)(2,1)S(1)} %copy-done.7, bf16[3,64]{1,0:T(4,128)(2,1)S(1)} %copy-done.8, bf16[1,64]{1,0:T(2,128)(2,1)S(1)} %bitcast.11, ...), custom_call_target="tpu_custom_call" | custom-call | flops 2400000000 | bytes 1048576 | tf_op jit(solution)/shard_map/attention/pallas_call | solution.py:31
  76.0 0.0 collective-permute-done.18.refs_13_
  76.1 6.0 %attention.7 = bf16[512,256]{1,0:T(8,128)(2,1)} custom-call(bf16[512,256]{1,0:T(8,128)(2,1)S(1)} %copy-done.4, bf16[64,256]{1,0:T(8,128)(2,1)S(1)} %copy-done.6, bf16[64,256]{1,0:T(8,128)(2,1)S(1)} %copy-done.7, bf16[3,64]{1,0:T(4,128)(2,1)S(1)} %copy-done.8, bf16[1,64]{1,0:T(2,128)(2,1)S(1)} %bitcast.12, bf16[768,128]{1,0:T(8,128)(2,1)S(1)} %order.7.refs_5_, ...), custom_call_target="tpu_custom_call" | custom-call | flops 2400000000 | bytes 1048576 | tf_op jit(solution)/shard_map/attention/pallas_call | solution.py:31
  (38 shorter events, 0.1 us)
Async XLA Ops:
  3.1 13.6 %collective-permute-start.3 = (bf16[64,256]{1,0:T(8,128)(2,1)}, bf16[64,256]{1,0:T(8,128)(2,1)S(1)}, u32[]{:S(2)}, u32[]{:S(2)}) collective-permute-start(bf16[64,256]{1,0:T(8,128)(2,1)} %get-tuple-element.26), channel_id=1, source_target_pairs={{0,1},{1,2},{2,3},{3,4},{4,5},{5,6},{6,7},{8,9},{9,10},{10,11},{11... | collective-permute-start | bytes 98312 | tf_op jit(solution)/shard_map/ppermute | solution.py:408
  7.2 10.1 %collective-permute-start.4 = (bf16[64,256]{1,0:T(8,128)(2,1)}, bf16[64,256]{1,0:T(8,128)(2,1)S(1)}, u32[]{:S(2)}, u32[]{:S(2)}) collective-permute-start(bf16[64,256]{1,0:T(8,128)(2,1)} %get-tuple-element.27), channel_id=1, source_target_pairs={{1,0},{2,1},{3,2},{4,3},{5,4},{6,5},{7,6},{9,8},{10,9},{11,10},{12... | collective-permute-start | bytes 98312 | tf_op jit(solution)/shard_map/ppermute | solution.py:409
  9.2 1.4 %collective-permute-start = (f32[1,256]{1,0:T(1,128)}, f32[1,256]{1,0:T(1,128)S(1)}, u32[]{:S(2)}, u32[]{:S(2)}) collective-permute-start(f32[1,256]{1,0:T(1,128)} %get-tuple-element.24), channel_id=1, source_target_pairs={{0,1},{1,0},{2,3},{3,2},{4,5},{5,4},{6,7},{7,6},{8,9},{9,8},{10,11... | collective-permute-start | bytes 3080 | tf_op jit(solution)/shard_map/ppermute | solution.py:343
  11.3 2.6 %collective-permute-start.1 = (f32[1,256]{1,0:T(1,128)S(1)}, f32[1,256]{1,0:T(1,128)S(1)}, u32[]{:S(2)}, u32[]{:S(2)}) collective-permute-start(f32[1,256]{1,0:T(1,128)S(1)} %add.6), channel_id=1, source_target_pairs={{0,2},{1,3},{2,0},{3,1},{4,6},{5,7},{6,4},{7,5},{8,10},{9,11},{10,... | collective-permute-start | bytes 3080 | tf_op jit(solution)/shard_map/ppermute | solution.py:343
  13.9 8.2 %collective-permute-start.2 = (f32[1,256]{1,0:T(1,128)S(1)}, f32[1,256]{1,0:T(1,128)S(1)}, u32[]{:S(2)}, u32[]{:S(2)}) collective-permute-start(f32[1,256]{1,0:T(1,128)S(1)} %add.7.earlier.mine), channel_id=1, source_target_pairs={{0,4},{1,5},{2,6},{3,7},{4,0},{5,1},{6,2},{7,3},{8,12},{9,13},{10,... | collective-permute-start | bytes 3080 | tf_op jit(solution)/shard_map/ppermute | solution.py:343
  16.8 0.6 copy-start.3
  17.4 0.6 copy-start.11
  18.0 4.1 %copy-start.1 = (bf16[256,256]{1,0:T(8,128)(2,1)S(1)}, bf16[256,256]{1,0:T(8,128)(2,1)}, u32[]{:S(2)}) copy-start(bf16[256,256]{1,0:T(8,128)(2,1)} %w_ptr.1) | copy-start | bytes 393220
  18.0 35.1 %copy-start.4 = (bf16[512,256]{1,0:T(8,128)(2,1)S(1)}, bf16[512,256]{1,0:T(8,128)(2,1)}, u32[]{:S(2)}) copy-start(bf16[512,256]{1,0:T(8,128)(2,1)} %get-tuple-element.23.refs_0_) | copy-start | bytes 786436
  18.0 35.1 %copy-start.6 = (bf16[64,256]{1,0:T(8,128)(2,1)S(1)}, bf16[64,256]{1,0:T(8,128)(2,1)}, u32[]{:S(2)}) copy-start(bf16[64,256]{1,0:T(8,128)(2,1)} %refs_1_.9) | copy-start | bytes 98308
  18.0 35.1 %copy-start.7 = (bf16[64,256]{1,0:T(8,128)(2,1)S(1)}, bf16[64,256]{1,0:T(8,128)(2,1)}, u32[]{:S(2)}) copy-start(bf16[64,256]{1,0:T(8,128)(2,1)} %refs_2_.7) | copy-start | bytes 98308
  18.0 35.1 %copy-start.8 = (bf16[3,64]{1,0:T(4,128)(2,1)S(1)}, bf16[3,64]{1,0:T(4,128)(2,1)}, u32[]{:S(2)}) copy-start(bf16[3,64]{1,0:T(4,128)(2,1)} %refs_3_.9) | copy-start | bytes 1156
  18.0 35.1 %copy-start.9 = (bf16[64]{0:T(256)(128)(2,1)S(1)}, bf16[64]{0:T(256)(128)(2,1)}, u32[]{:S(2)}) copy-start(bf16[64]{0:T(256)(128)(2,1)} %param.27) | copy-start | bytes 388
  22.1 0.8 %copy-start.2 = (bf16[256,128]{1,0:T(8,128)(2,1)S(1)}, bf16[256,128]{1,0:T(8,128)(2,1)}, u32[]{:S(2)}) copy-start(bf16[256,128]{1,0:T(8,128)(2,1)} %get-tuple-element.28.own) | copy-start | bytes 196612
  23.7 17.8 %collective-permute-start.6 = (bf16[272,128]{1,0:T(8,128)(2,1)S(1)}, bf16[272,128]{1,0:T(8,128)(2,1)S(1)}, u32[]{:S(2)}, u32[]{:S(2)}) collective-permute-start(bf16[272,128]{1,0:T(8,128)(2,1)S(1)} %get-tuple-element.29.couple), channel_id=1, source_target_pairs={{0,16},{1,17},{2,18},{3,19},{4,20},{5,21},{6,22},{7,23},{8,24},{9,... | collective-permute-start | bytes 208904 | tf_op jit(solution)/shard_map/ppermute | solution.py:448
  29.2 5.7 %collective-permute-start.5 = (bf16[256,128]{1,0:T(8,128)(2,1)}, bf16[256,128]{1,0:T(8,128)(2,1)S(1)}, u32[]{:S(2)}, u32[]{:S(2)}) collective-permute-start(bf16[256,128]{1,0:T(8,128)(2,1)} %get-tuple-element.28.own), channel_id=1, source_target_pairs={{0,8},{1,9},{2,10},{3,11},{4,12},{5,13},{6,14},{7,15},{8,16},{9,17... | collective-permute-start | bytes 196616 | tf_op jit(solution)/shard_map/ppermute | solution.py:436
  32.9 8.6 %collective-permute-start.7 = (bf16[256,128]{1,0:T(8,128)(2,1)}, bf16[256,128]{1,0:T(8,128)(2,1)S(1)}, u32[]{:S(2)}, u32[]{:S(2)}) collective-permute-start(bf16[256,128]{1,0:T(8,128)(2,1)} %get-tuple-element.28.own), channel_id=1, source_target_pairs={{0,24},{1,25},{2,26},{3,27},{4,28},{5,29},{6,30},{7,31},{14,32},{1... | collective-permute-start | bytes 196616 | tf_op jit(solution)/shard_map/ppermute | solution.py:437
  41.6 11.1 %collective-permute-start.11 = (bf16[768,128]{1,0:T(8,128)(2,1)S(1)}, bf16[768,128]{1,0:T(8,128)(2,1)S(1)}, u32[]{:S(2)}, u32[]{:S(2)}) collective-permute-start(bf16[768,128]{1,0:T(8,128)(2,1)S(1)} %get-tuple-element.30.refs_5_), channel_id=1, source_target_pairs={{0,2},{1,3},{2,0},{3,1},{4,6},{5,7},{6,4},{7,5},{8,10},{9,11},{10,... | collective-permute-start | bytes 589832 | tf_op jit(solution)/shard_map/ppermute | solution.py:343
  43.9 9.1 %collective-permute-start.9 = (bf16[768,128]{1,0:T(8,128)(2,1)S(1)}, bf16[768,128]{1,0:T(8,128)(2,1)S(1)}, u32[]{:S(2)}, u32[]{:S(2)}) collective-permute-start(bf16[768,128]{1,0:T(8,128)(2,1)S(1)} %get-tuple-element.30.refs_5_), channel_id=1, source_target_pairs={{0,1},{1,0},{2,3},{3,2},{4,5},{5,4},{6,7},{7,6},{8,9},{9,8},{10,11... | collective-permute-start | bytes 589832 | tf_op jit(solution)/shard_map/ppermute | solution.py:343
  48.1 9.2 %collective-permute-start.8 = (bf16[768,128]{1,0:T(8,128)(2,1)S(1)}, bf16[768,128]{1,0:T(8,128)(2,1)S(1)}, u32[]{:S(2)}, u32[]{:S(2)}) collective-permute-start(bf16[768,128]{1,0:T(8,128)(2,1)S(1)} %get-tuple-element.30.refs_5_), channel_id=1, source_target_pairs={{0,6},{1,7},{2,4},{3,5},{4,2},{5,3},{6,0},{7,1},{8,14},{9,15},{10,... | collective-permute-start | bytes 589832 | tf_op jit(solution)/shard_map/ppermute | solution.py:343
  50.8 9.1 %collective-permute-start.15 = (bf16[16,128]{1,0:T(8,128)(2,1)S(1)}, bf16[16,128]{1,0:T(8,128)(2,1)S(1)}, u32[]{:S(2)}, u32[]{:S(2)}) collective-permute-start(bf16[16,128]{1,0:T(8,128)(2,1)S(1)} %get-tuple-element.40), channel_id=1, source_target_pairs={{0,8},{8,16},{1,17},{16,24},{9,25},{24,32},{17,33},{32,40},{25,41}... | collective-permute-start | bytes 12296 | tf_op jit(solution)/shard_map/ppermute | solution.py:463
  52.7 9.7 %collective-permute-start.12 = (bf16[768,128]{1,0:T(8,128)(2,1)S(1)}, bf16[768,128]{1,0:T(8,128)(2,1)S(1)}, u32[]{:S(2)}, u32[]{:S(2)}) collective-permute-start(bf16[768,128]{1,0:T(8,128)(2,1)S(1)} %collective-permute-done.11.refs_5_), channel_id=1, source_target_pairs={{0,1},{1,0},{2,3},{3,2},{4,5},{5,4},{6,7},{7,6},{8,9},{9,8},{10,11... | collective-permute-start | bytes 589832 | tf_op jit(solution)/shard_map/ppermute | solution.py:343
  57.3 13.0 %collective-permute-start.14 = (bf16[768,128]{1,0:T(8,128)(2,1)S(1)}, bf16[768,128]{1,0:T(8,128)(2,1)S(1)}, u32[]{:S(2)}, u32[]{:S(2)}) collective-permute-start(bf16[768,128]{1,0:T(8,128)(2,1)S(1)} %order.6.refs_5_), channel_id=1, source_target_pairs={{0,1},{1,0},{2,3},{3,2},{4,5},{5,4},{6,7},{7,6},{8,9},{9,8},{10,11... | collective-permute-start | bytes 589832 | tf_op jit(solution)/shard_map/ppermute | solution.py:343
  59.0 10.9 %collective-permute-start.10 = (bf16[768,128]{1,0:T(8,128)(2,1)S(1)}, bf16[768,128]{1,0:T(8,128)(2,1)S(1)}, u32[]{:S(2)}, u32[]{:S(2)}) collective-permute-start(bf16[768,128]{1,0:T(8,128)(2,1)S(1)} %order.6.refs_5_), channel_id=1, source_target_pairs={{0,2},{1,3},{2,0},{3,1},{4,6},{5,7},{6,4},{7,5},{8,10},{9,11},{10,... | collective-permute-start | bytes 589832 | tf_op jit(solution)/shard_map/ppermute | solution.py:343
  59.9 6.9 %collective-permute-start.19 = (bf16[16,128]{1,0:T(8,128)(2,1)S(1)}, bf16[16,128]{1,0:T(8,128)(2,1)S(1)}, u32[]{:S(2)}, u32[]{:S(2)}) collective-permute-start(bf16[16,128]{1,0:T(8,128)(2,1)S(1)} %order.8.refs_10_), channel_id=1, source_target_pairs={{0,6},{1,7},{2,4},{3,5},{4,2},{5,3},{6,0},{7,1},{8,14},{9,15},{10,... | collective-permute-start | bytes 12296 | tf_op jit(solution)/shard_map/ppermute | solution.py:343
  62.4 7.5 %collective-permute-start.17 = (bf16[16,128]{1,0:T(8,128)(2,1)S(1)}, bf16[16,128]{1,0:T(8,128)(2,1)S(1)}, u32[]{:S(2)}, u32[]{:S(2)}) collective-permute-start(bf16[16,128]{1,0:T(8,128)(2,1)S(1)} %order.8.refs_10_), channel_id=1, source_target_pairs={{0,2},{1,3},{2,0},{3,1},{4,6},{5,7},{6,4},{7,5},{8,10},{9,11},{10,... | collective-permute-start | bytes 12296 | tf_op jit(solution)/shard_map/ppermute | solution.py:343
  62.4 5.6 %copy-start.10 = (bf16[16,256]{1,0:T(8,128)(2,1)S(1)}, bf16[16,256]{1,0:T(8,128)(2,1)}, u32[]{:S(2)}) copy-start(bf16[16,256]{1,0:T(8,128)(2,1)} %param.26) | copy-start | bytes 24580
  66.8 3.7 %collective-permute-start.21 = (bf16[16,128]{1,0:T(8,128)(2,1)S(1)}, bf16[16,128]{1,0:T(8,128)(2,1)S(1)}, u32[]{:S(2)}, u32[]{:S(2)}) collective-permute-start(bf16[16,128]{1,0:T(8,128)(2,1)S(1)} %order.9.refs_14_), channel_id=1, source_target_pairs={{0,2},{1,3},{2,0},{3,1},{4,6},{5,7},{6,4},{7,5},{8,10},{9,11},{10,... | collective-permute-start | bytes 12296 | tf_op jit(solution)/shard_map/ppermute | solution.py:343
  68.0 8.0 %collective-permute-start.16 = (bf16[16,128]{1,0:T(8,128)(2,1)S(1)}, bf16[16,128]{1,0:T(8,128)(2,1)S(1)}, u32[]{:S(2)}, u32[]{:S(2)}) collective-permute-start(bf16[16,128]{1,0:T(8,128)(2,1)S(1)} %order.8.refs_10_), channel_id=1, source_target_pairs={{0,1},{1,0},{2,3},{3,2},{4,5},{5,4},{6,7},{7,6},{8,9},{9,8},{10,11... | collective-permute-start | bytes 12296 | tf_op jit(solution)/shard_map/ppermute | solution.py:343
  69.8 6.2 %collective-permute-start.18 = (bf16[16,128]{1,0:T(8,128)(2,1)S(1)}, bf16[16,128]{1,0:T(8,128)(2,1)S(1)}, u32[]{:S(2)}, u32[]{:S(2)}) collective-permute-start(bf16[16,128]{1,0:T(8,128)(2,1)S(1)} %collective-permute-done.17.refs_12_), channel_id=1, source_target_pairs={{0,1},{1,0},{2,3},{3,2},{4,5},{5,4},{6,7},{7,6},{8,9},{9,8},{10,11... | collective-permute-start | bytes 12296 | tf_op jit(solution)/shard_map/ppermute | solution.py:343
  69.9 6.1 %collective-permute-start.20 = (bf16[16,128]{1,0:T(8,128)(2,1)S(1)}, bf16[16,128]{1,0:T(8,128)(2,1)S(1)}, u32[]{:S(2)}, u32[]{:S(2)}) collective-permute-start(bf16[16,128]{1,0:T(8,128)(2,1)S(1)} %order.9.refs_14_), channel_id=1, source_target_pairs={{0,1},{1,0},{2,3},{3,2},{4,5},{5,4},{6,7},{7,6},{8,9},{9,8},{10,11... | collective-permute-start | bytes 12296 | tf_op jit(solution)/shard_map/ppermute | solution.py:343
  70.3 5.7 %collective-permute-start.13 = (bf16[768,128]{1,0:T(8,128)(2,1)S(1)}, bf16[768,128]{1,0:T(8,128)(2,1)S(1)}, u32[]{:S(2)}, u32[]{:S(2)}) collective-permute-start(bf16[768,128]{1,0:T(8,128)(2,1)S(1)} %order.7.refs_5_), channel_id=1, source_target_pairs={{0,1},{1,0},{2,3},{3,2},{4,5},{5,4},{6,7},{7,6},{8,9},{9,8},{10,11... | collective-permute-start | bytes 589832 | tf_op jit(solution)/shard_map/ppermute | solution.py:343
  70.5 5.6 %collective-permute-start.22 = (bf16[16,128]{1,0:T(8,128)(2,1)S(1)}, bf16[16,128]{1,0:T(8,128)(2,1)S(1)}, u32[]{:S(2)}, u32[]{:S(2)}) collective-permute-start(bf16[16,128]{1,0:T(8,128)(2,1)S(1)} %collective-permute-done.21.refs_16_), channel_id=1, source_target_pairs={{0,1},{1,0},{2,3},{3,2},{4,5},{5,4},{6,7},{7,6},{8,9},{9,8},{10,11... | collective-permute-start | bytes 12296 | tf_op jit(solution)/shard_map/ppermute | solution.py:343
  72.0 4.1 %copy-start = (bf16[1,8,64,256]{3,2,1,0:T(8,128)(2,1)S(1)}, bf16[1,8,64,256]{3,2,1,0:T(8,128)(2,1)}, u32[]{:S(2)}) copy-start(bf16[1,8,64,256]{3,2,1,0:T(8,128)(2,1)} %param.14) | copy-start | bytes 786436
  72.0 4.1 %copy-start.5 = (bf16[256,256]{1,0:T(8,128)(2,1)S(1)}, bf16[256,256]{1,0:T(8,128)(2,1)}, u32[]{:S(2)}) copy-start(bf16[256,256]{1,0:T(8,128)(2,1)} %refs_19_.1) | copy-start | bytes 393220

commit v3 on v2

--- a/solution.py
+++ b/solution.py
@@ -56,7 +56,7 @@
 
 def joined_kernel(*refs):
     sources, outputs, refs = refs[:5], refs[5:10], refs[10:]
-    joined, top, bottom, pooled, query = outputs
+    joined, outer, inner, pooled, query = outputs
     feat, w_pix, mask, embed, w_query, sems = refs
     copies = fetch(zip(sources, refs[:5]), sems)
     for copy in copies[:4]:
@@ -71,12 +71,22 @@
         value = value.astype(bf16)
         joined[r * COLS : (r + 1) * COLS, :] = value
         if r == 0:
-            top[...] = value
-        if r == ROWS - 1:
-            bottom[...] = value
+            top = value
         picked = rows.astype(f32) * column
         for k in range(COLS // 8):
             total = total + picked[k * 8 : (k + 1) * 8, :]
+    odd = lax.axis_index("space") % 2 == 1
+
+    @pl.when(odd)
+    def _():
+        outer[...] = value
+        inner[...] = top
+
+    @pl.when(jnp.logical_not(odd))
+    def _():
+        outer[...] = top
+        inner[...] = value
+
     pooled[...] = jnp.sum(total, axis=0, keepdims=True)
     copies[4].wait()
     for r in range(0, TOK, 128):
@@ -89,26 +99,26 @@
 
 def conv_kernel(*refs):
     sources, (memory, pairs), refs = refs[:5], refs[5:7], refs[7:]
-    joined, above, below, w_conv, w_out, wide, tokens, sems = refs
+    joined, outer, inner, w_conv, w_out, wide, tokens, sems = refs
     near = fetch(zip(sources[:3], refs[:3]), sems)
     taps = [(sources[3].at[a], w_conv.at[a]) for a in range(3)]
     copies = fetch(taps + [(sources[4], w_out)], sems.at[pl.ds(3, 4)])
     for copy in near:
         copy.wait()
+    odd = lax.axis_index("space") % 2 == 1
     side = lax.broadcasted_iota(jnp.int32, (COLS, D), 0)
     for r in range(ROWS + 2):
         if r == 0:
-            row = above[...]
+            value = jnp.where(odd, inner[...].astype(f32), outer[...].astype(f32))
         elif r == ROWS + 1:
-            row = below[...]
+            value = jnp.where(odd, outer[...].astype(f32), inner[...].astype(f32))
         else:
-            row = joined[(r - 1) * COLS : r * COLS, :]
-        value = row.astype(f32)
+            value = joined[(r - 1) * COLS : r * COLS, :].astype(f32)
         left = jnp.where(side == 0, 0.0, pltpu.roll(value, 1, 0))
         right = jnp.where(side == COLS - 1, 0.0, pltpu.roll(value, COLS - 1, 0))
         here = slice(r * COLS, (r + 1) * COLS)
         wide[here, 0:D] = left.astype(bf16)
-        wide[here, D : 2 * D] = row
+        wide[here, D : 2 * D] = value.astype(bf16)
         wide[here, 2 * D : 3 * D] = right.astype(bf16)
     for copy in copies:
         copy.wait()
@@ -173,7 +183,7 @@
 
 
 QT = 256
-HOLDERS = (0, 1, 2, 3, 6, 7, 4, 5)
+HOLDERS = (0, 1, 2, 3, 4, 5, 6, 7)
 
 
 def attention_kernel(count, first, last, *refs):
@@ -187,9 +197,9 @@
         state_in, refs = refs[:3], refs[3:]
     if last:
         tails, refs = refs[:BANDS], refs[BANDS:]
-        feat, w_proj, ptr_tpos, attended, keys, values, shifts, top, norm, mixed, ptr_tok = refs
+        feat, w_proj, ptr_tpos, attended, keys, values, top, norm, mixed, ptr_tok = refs
     else:
-        top, norm, mixed, keys, values, shifts = refs
+        top, norm, mixed, keys, values = refs
     frame = lax.axis_index("tm")
     wk = twice(w_key[...])
     wv = twice(w_value[...])
@@ -209,10 +219,14 @@
         for source, target in zip(state_in, (top, norm, mixed)):
             target[...] = source[...]
 
-    def update(rows, scores, value_rows):
+    def update(rows, scores, value_rows, valid=None):
         old = top[rows, :]
         new = jnp.maximum(old, jnp.max(scores, axis=1, keepdims=True))
-        weights = jnp.exp(scores - new)
+        level = new
+        if valid is not None:
+            level = jnp.where(valid, new, jnp.inf)
+            new = jnp.where(valid, new, old)
+        weights = jnp.exp(scores - level)
         fade = jnp.exp(old - new)
         norm[rows, :] = norm[rows, :] * fade + jnp.sum(weights, axis=1, keepdims=True)
         mixed[rows, :] = mixed[rows, :] * fade + jnp.dot(
@@ -221,26 +235,31 @@
         top[rows, :] = new
 
     tiles = [slice(q * QT, (q + 1) * QT) for q in range(TOK // QT)]
-    shifts[...] = tpos_keys
-
-    @pl.loop(0, jnp.minimum(frame, MEMS))
-    def _(d):
-        shift = shifts[pl.ds(d, 1), :]
+    span = count * TOK
+    for d in range(MEMS):
+        shift = tpos_keys[d : d + 1, :]
         for b, block in enumerate(blocks):
-            x = block[pl.ds(pl.multiple_of(d * HALF, HALF), HALF), :]
-            base = b * TOK
+            x = block[d * HALF : (d + 1) * HALF, :]
+            base = d * span + b * TOK
             k = jnp.dot(x, wk, preferred_element_type=f32)
             v = jnp.dot(x, wv, preferred_element_type=f32).astype(bf16)
             keys[base : base + HALF, :] = (k[:, :D] + shift).astype(bf16)
             keys[base + HALF : base + TOK, :] = (k[:, D:] + shift).astype(bf16)
             values[base : base + HALF, :] = v[:, :D]
             values[base + HALF : base + TOK, :] = v[:, D:]
-        found = [
-            lax.dot_general(query[rows, :], keys[...], NT, preferred_element_type=f32)
-            for rows in tiles
-        ]
-        for rows, scores in zip(tiles, found):
-            update(rows, scores, values[...])
+
+    def score(step):
+        d, rows = step
+        cols = slice(d * span, (d + 1) * span)
+        return lax.dot_general(query[rows, :], keys[cols, :], NT, preferred_element_type=f32)
+
+    steps = [(d, rows) for d in range(MEMS) for rows in tiles]
+    coming = score(steps[0])
+    for i, (d, rows) in enumerate(steps):
+        scores = coming
+        if i + 1 < len(steps):
+            coming = score(steps[i + 1])
+        update(rows, scores, values[d * span : (d + 1) * span, :], frame >= d + 1)
 
     if last:
         widened = jnp.dot(ptr_tpos[...], wk, preferred_element_type=f32)
@@ -292,7 +311,7 @@
         args += list(state)
         specs += [vmem] * 3
     state_shape = [((TOK, 1), f32), ((TOK, 1), f32), ((TOK, D), f32)]
-    scratch = [pltpu.VMEM((len(blocks) * TOK, D), bf16)] * 2 + [pltpu.VMEM((8, D), f32)]
+    scratch = [pltpu.VMEM((MEMS * len(blocks) * TOK, D), bf16)] * 2
     if final is None:
         out = tuple(sds(*s) for s in state_shape)
     else:
@@ -311,15 +330,15 @@
     )
 
 
-def mirrored(source, target, s):
+def shifted(source, target, s):
     if (source // 4) % 2 == (target // 4) % 2:
         return s
-    return across(s)
+    return opposite(s)
 
 
 def later(distance):
     return [
-        ((t - distance) * BANDS + mirrored(t - distance, t, s), t * BANDS + s)
+        ((t - distance) * BANDS + shifted(t - distance, t, s), t * BANDS + s)
         for t in range(distance, FRAMES)
         for s in range(BANDS)
     ]
@@ -335,7 +354,7 @@
         for s in range(BANDS):
             source = t - pointer_distance(s)
             if source >= 0:
-                pairs.append((source * BANDS + s, t * BANDS + s))
+                pairs.append((source * BANDS + shifted(source, t, s), t * BANDS + s))
     return pairs
 
 
@@ -353,10 +372,6 @@
 
 def opposite(i):
     return i ^ 4
-
-
-def across(i):
-    return i ^ 6
 
 
 def body(
@@ -378,7 +393,7 @@
     feat = features.reshape(TOK, D)
     far = pl.BlockSpec(memory_space=pl.ANY)
     vmem = pl.BlockSpec(memory_space=pltpu.VMEM)
-    joined, top, bottom, pooled, query = call(
+    joined, outer, inner, pooled, query = call(
         joined_kernel,
         (
             sds((TOK, D), bf16),
@@ -405,17 +420,18 @@
         limit=60,
         name="joined",
     )
-    above = lax.ppermute(bottom, "space", [(i, i + 1) for i in range(BANDS - 1)])
-    below = lax.ppermute(top, "space", [(i + 1, i) for i in range(BANDS - 1)])
+    links = [(i, i + 1) for i in range(1, BANDS - 1, 2)]
+    outer = lax.ppermute(outer, "space", links + [(b, a) for a, b in links])
+    inner = over_space(inner, sibling)
     pooled = pooled + over_space(pooled, sibling)
     pooled = pooled + over_space(pooled, beside)
-    above = after(above, pooled)
+    outer = after(outer, pooled)
     memory, pairs = call(
         conv_kernel,
         (sds((ROWS, COLS * MEM), bf16), sds((HALF, 128), bf16)),
         joined,
-        above,
-        below,
+        outer,
+        inner,
         w_conv.reshape(3, 3 * D, D),
         w_out.T,
         in_specs=[far] * 5,
@@ -459,13 +475,13 @@
     weights = (w_key, w_value, mem_tpos, empty_memory.reshape(1, MEM))
 
     one = over_space(own, beside)
-    two = over_space(own, across)
+    two = over_space(own, opposite)
     tail = lax.ppermute(window, BOTH, pointer_route())
     state = attend(query, weights, [own, over_space(own, sibling)])
     two = after(two, state[2])
     tail = after(tail, state[2])
     three = over_space(two, beside)
-    tails = [tail, over_space(tail, beside), over_space(tail, across)]
+    tails = [tail, over_space(tail, beside), over_space(tail, opposite)]
     state = attend(query, weights, [one, over_space(one, sibling)], state)
     three = after(three, state[2])
     tails[2] = after(tails[2], state[2])

time: 83 us -> 75.9 us (0.914)
  starting transfers between devices: 43.5 us -> 39.3 us
  Pallas kernels: 25.7 us -> 22.2 us
  waiting for transfers between devices: 9.3 us -> 10.3 us
    ppermute x17 -> x18, starting transfers between devices: 24.4 us -> 20.5 us  [over_space(): return lax.ppermute(x, 'space', [(i, target(i)) for i in range(BANDS)])]
    pallas_call x13, Pallas kernels: 25.7 us -> 22.2 us  [call(): pl.pallas_call(kernel, out_shape=out_shape, in_specs=[vmem] * len(args) i...]
    ppermute x2 -> x1, starting transfers between devices: 6.03 us -> 4.11 us  [body(): outer = lax.ppermute(outer, 'space', links + [(b, a) for a, b in links])]
    ppermute x1, starting transfers between devices: 1.91 us -> 3.27 us  [body(): tail = lax.ppermute(window, BOTH, pointer_route())]
    ppermute x17 -> x18, waiting for transfers between devices: 2.65 us -> 3.66 us  [over_space(): return lax.ppermute(x, 'space', [(i, target(i)) for i in range(BANDS)])]
  transfers between devices with their start and end apart: 23 -> 23, of which waited for: 4 -> 4; matrix products, arithmetic and copies ran while one was open for 1% -> 1% of each run, Pallas kernels for 20% -> 19%
where the time goes in v3:
time: 75.9 us; the launch traced here: 75.5 us
  starting transfers between devices  39.3 us (52%)
  Pallas kernels  22.2 us (29%)
  waiting for transfers between devices  10.3 us (14%)
  local copies, waits for them, and re-layouts  2.08 us (3%)
  between operations  0.9 us (1%)
    pallas_call x13, Pallas kernels, call(): pl.pallas_call(kernel, out_shape=out_shape, in_specs=[vmem] * len(args) i...  22.2 us
    ppermute x18, starting transfers between devices, over_space(): return lax.ppermute(x, 'space', [(i, target(i)) for i in range(BANDS)])  20.5 us
    ppermute x1, waiting for transfers between devices, body(): third = lax.ppermute(pairs, BOTH, later(3))  6.65 us
    ppermute x1, starting transfers between devices, body(): second = lax.ppermute(couple, BOTH, later(2))  5.14 us
    ppermute x1, starting transfers between devices, body(): outer = lax.ppermute(outer, 'space', links + [(b, a) for a, b in links])  4.11 us
    ppermute x1, starting transfers between devices, body(): first = lax.ppermute(pairs, BOTH, later(1))  3.72 us
    ppermute x18, waiting for transfers between devices, over_space(): return lax.ppermute(x, 'space', [(i, target(i)) for i in range(BANDS)])  3.66 us
    ppermute x1, starting transfers between devices, body(): tail = lax.ppermute(window, BOTH, pointer_route())  3.27 us
  transfers between devices with their start and end apart: 23, of which 4 were waited for; matrix products, arithmetic and copies ran while one was open for 1% of the time, Pallas kernels for 19%

profile of v3, /device:TPU:13, one launch (start us, length us, event | category | flops | bytes accessed | tf_op | source)
XLA Modules:
  0.0 75.5 jit_solution(2713010369236045679)
XLA Ops:
  0.6 2.5 %joined.1 = (bf16[512,256]{1,0:T(8,128)(2,1)}, bf16[64,256]{1,0:T(8,128)(2,1)}, bf16[64,256]{1,0:T(8,128)(2,1)}, f32[1,256]{1,0:T(1,128)}, bf16[512,256]{1,0:T(8,128)(2,1)}) custom-call(bf16[512,256]{1,0:T(8,128)(2,1)} %bitcast.7, bf16[256,256]{1,0:T(8,128)(2,1)} %refs_1_.5, s32[8,64]{1,0:T(8,128)} %bitcast.13, bf16[256]{0:T(256)(128)(2,1)} %refs_3_.5, ...), custom_call_target="tpu_custom_call" | custom-call | flops 140000000 | bytes 1048576 | tf_op jit(solution)/shard_map/joined/pallas_call | solution.py:31
  3.1 4.1 %collective-permute-start.3 = (bf16[64,256]{1,0:T(8,128)(2,1)}, bf16[64,256]{1,0:T(8,128)(2,1)S(1)}, u32[]{:S(2)}, u32[]{:S(2)}) collective-permute-start(bf16[64,256]{1,0:T(8,128)(2,1)} %get-tuple-element.26), channel_id=1, source_target_pairs={{1,2},{3,4},{5,6},{2,1},{4,3},{6,5},{9,10},{11,12},{13,14},{10,9},... | collective-permute-start | bytes 98312 | tf_op jit(solution)/shard_map/ppermute | solution.py:424
  7.2 0.1 collective-permute-start.4
  7.3 0.5 collective-permute-start
  7.8 1.0 %collective-permute-done = f32[1,256]{1,0:T(1,128)S(1)} collective-permute-done((f32[1,256]{1,0:T(1,128)}, f32[1,256]{1,0:T(1,128)S(1)}, u32[]{:S(2)}, u32[]{:S(2)}) %collective-permute-start) | collective-permute-done | bytes 1056 | tf_op jit(solution)/shard_map/ppermute | solution.py:362
  8.9 0.7 add.6
  9.5 1.6 %collective-permute-start.1 = (f32[1,256]{1,0:T(1,128)S(1)}, f32[1,256]{1,0:T(1,128)S(1)}, u32[]{:S(2)}, u32[]{:S(2)}) collective-permute-start(f32[1,256]{1,0:T(1,128)S(1)} %add.6), channel_id=1, source_target_pairs={{0,2},{1,3},{2,0},{3,1},{4,6},{5,7},{6,4},{7,5},{8,10},{9,11},{10,... | collective-permute-start | bytes 3080 | tf_op jit(solution)/shard_map/ppermute | solution.py:362
  11.2 1.0 %collective-permute-done.1 = f32[1,256]{1,0:T(1,128)S(1)} collective-permute-done((f32[1,256]{1,0:T(1,128)S(1)}, f32[1,256]{1,0:T(1,128)S(1)}, u32[]{:S(2)}, u32[]{:S(2)}) %collective-permute-start.1) | collective-permute-done | bytes 1056 | tf_op jit(solution)/shard_map/ppermute | solution.py:362
  12.1 2.8 %collective-permute-start.2 = (f32[1,256]{1,0:T(1,128)S(1)}, f32[1,256]{1,0:T(1,128)S(1)}, u32[]{:S(2)}, u32[]{:S(2)}) collective-permute-start(f32[1,256]{1,0:T(1,128)S(1)} %add.7.earlier.mine), channel_id=1, source_target_pairs={{0,4},{1,5},{2,6},{3,7},{4,0},{5,1},{6,2},{7,3},{8,12},{9,13},{10,... | collective-permute-start | bytes 3080 | tf_op jit(solution)/shard_map/ppermute | solution.py:362
  15.0 0.6 copy-done.3
  15.6 0.0 collective-permute-done.4.refs_2_
  15.6 0.6 copy-done.11
  16.2 0.0 copy-start.8
  16.2 0.0 copy-start.9
  16.2 4.1 %conv.1 = (bf16[8,4096]{1,0:T(8,128)(2,1)}, bf16[256,128]{1,0:T(8,128)(2,1)}) custom-call(bf16[512,256]{1,0:T(8,128)(2,1)} %get-tuple-element.25.refs_0_, bf16[64,256]{1,0:T(8,128)(2,1)} %copy-done.3, bf16[64,256]{1,0:T(8,128)(2,1)} %copy-done.11, bf16[3,768,256]{2,1,0:T(8,128)(2,1)} %bitcast.14, bf16[64,256]{1,0:T(8,128)(2,1)} %bitcast.15), custom_call_target="tpu_custom_call" | custom-call | flops 640000000 | bytes 1048576 | tf_op jit(solution)/shard_map/conv/pallas_call | solution.py:31
  20.3 0.8 %copy-done.2 = bf16[256,128]{1,0:T(8,128)(2,1)S(1)} copy-done((bf16[256,128]{1,0:T(8,128)(2,1)S(1)}, bf16[256,128]{1,0:T(8,128)(2,1)}, u32[]{:S(2)}) %copy-start.2) | copy-done | bytes 65560
  21.2 0.8 %pair.1 = (bf16[1,256]{1,0:T(2,128)(2,1)}, bf16[272,128]{1,0:T(8,128)(2,1)S(1)}) custom-call(f32[1,256]{1,0:T(1,128)S(1)} %add.7.earlier.mine, f32[1,256]{1,0:T(1,128)S(1)} %collective-permute-done.2.other, bf16[256,256]{1,0:T(8,128)(2,1)S(1)} %copy-done.1, bf16[256,128]{1,0:T(8,128)(2,1)S(1)} %copy-done.2), custom_call_target="tpu_custom_call" | custom-call | flops 1000000 | bytes 1048576 | tf_op jit(solution)/shard_map/pair/pallas_call | solution.py:31
  21.9 5.1 %collective-permute-start.6 = (bf16[272,128]{1,0:T(8,128)(2,1)S(1)}, bf16[272,128]{1,0:T(8,128)(2,1)S(1)}, u32[]{:S(2)}, u32[]{:S(2)}) collective-permute-start(bf16[272,128]{1,0:T(8,128)(2,1)S(1)} %get-tuple-element.29.couple), channel_id=1, source_target_pairs={{0,16},{1,17},{2,18},{3,19},{4,20},{5,21},{6,22},{7,23},{8,24},{9,... | collective-permute-start | bytes 208904 | tf_op jit(solution)/shard_map/ppermute | solution.py:464
  27.1 3.7 %collective-permute-start.5 = (bf16[256,128]{1,0:T(8,128)(2,1)}, bf16[256,128]{1,0:T(8,128)(2,1)S(1)}, u32[]{:S(2)}, u32[]{:S(2)}) collective-permute-start(bf16[256,128]{1,0:T(8,128)(2,1)} %get-tuple-element.28.own), channel_id=1, source_target_pairs={{0,8},{1,9},{2,10},{3,11},{4,12},{5,13},{6,14},{7,15},{8,16},{9,17... | collective-permute-start | bytes 196616 | tf_op jit(solution)/shard_map/ppermute | solution.py:452
  30.8 2.6 %collective-permute-start.7 = (bf16[256,128]{1,0:T(8,128)(2,1)}, bf16[256,128]{1,0:T(8,128)(2,1)S(1)}, u32[]{:S(2)}, u32[]{:S(2)}) collective-permute-start(bf16[256,128]{1,0:T(8,128)(2,1)} %get-tuple-element.28.own), channel_id=1, source_target_pairs={{0,24},{1,25},{2,26},{3,27},{4,28},{5,29},{6,30},{7,31},{12,32},{1... | collective-permute-start | bytes 196616 | tf_op jit(solution)/shard_map/ppermute | solution.py:453
  33.4 6.6 %collective-permute-done.7.third = bf16[256,128]{1,0:T(8,128)(2,1)S(1)} collective-permute-done((bf16[256,128]{1,0:T(8,128)(2,1)}, bf16[256,128]{1,0:T(8,128)(2,1)S(1)}, u32[]{:S(2)}, u32[]{:S(2)}) %collective-permute-start.7) | collective-permute-done | bytes 65568 | tf_op jit(solution)/shard_map/ppermute | solution.py:453
  40.1 1.4 %collective-permute-start.11 = (bf16[768,128]{1,0:T(8,128)(2,1)S(1)}, bf16[768,128]{1,0:T(8,128)(2,1)S(1)}, u32[]{:S(2)}, u32[]{:S(2)}) collective-permute-start(bf16[768,128]{1,0:T(8,128)(2,1)S(1)} %get-tuple-element.30.refs_5_), channel_id=1, source_target_pairs={{0,2},{1,3},{2,0},{3,1},{4,6},{5,7},{6,4},{7,5},{8,10},{9,11},{10,... | collective-permute-start | bytes 589832 | tf_op jit(solution)/shard_map/ppermute | solution.py:362
  41.5 3.4 %collective-permute-start.9 = (bf16[768,128]{1,0:T(8,128)(2,1)S(1)}, bf16[768,128]{1,0:T(8,128)(2,1)S(1)}, u32[]{:S(2)}, u32[]{:S(2)}) collective-permute-start(bf16[768,128]{1,0:T(8,128)(2,1)S(1)} %get-tuple-element.30.refs_5_), channel_id=1, source_target_pairs={{0,1},{1,0},{2,3},{3,2},{4,5},{5,4},{6,7},{7,6},{8,9},{9,8},{10,11... | collective-permute-start | bytes 589832 | tf_op jit(solution)/shard_map/ppermute | solution.py:362
  44.9 0.7 collective-permute-start.8
  45.6 3.3 %collective-permute-start.15 = (bf16[16,128]{1,0:T(8,128)(2,1)S(1)}, bf16[16,128]{1,0:T(8,128)(2,1)S(1)}, u32[]{:S(2)}, u32[]{:S(2)}) collective-permute-start(bf16[16,128]{1,0:T(8,128)(2,1)S(1)} %get-tuple-element.40), channel_id=1, source_target_pairs={{0,8},{8,16},{1,17},{16,24},{9,25},{28,32},{21,33},{32,40},{29,41}... | collective-permute-start | bytes 12296 | tf_op jit(solution)/shard_map/ppermute | solution.py:479
  48.9 0.0 collective-permute-done.11.refs_5_
  48.9 2.6 %collective-permute-start.12 = (bf16[768,128]{1,0:T(8,128)(2,1)S(1)}, bf16[768,128]{1,0:T(8,128)(2,1)S(1)}, u32[]{:S(2)}, u32[]{:S(2)}) collective-permute-start(bf16[768,128]{1,0:T(8,128)(2,1)S(1)} %collective-permute-done.11.refs_5_), channel_id=1, source_target_pairs={{0,1},{1,0},{2,3},{3,2},{4,5},{5,4},{6,7},{7,6},{8,9},{9,8},{10,11... | collective-permute-start | bytes 589832 | tf_op jit(solution)/shard_map/ppermute | solution.py:362
  51.5 0.0 collective-permute-done.9.refs_6_
  51.5 3.4 %attention.4 = (f32[512,1]{1,0:T(8,128)S(1)}, f32[512,1]{1,0:T(8,128)S(1)}, f32[512,256]{1,0:T(8,128)S(1)}) custom-call(bf16[512,256]{1,0:T(8,128)(2,1)S(1)} %copy-done.4, bf16[64,256]{1,0:T(8,128)(2,1)S(1)} %copy-done.6, bf16[64,256]{1,0:T(8,128)(2,1)S(1)} %copy-done.7, bf16[3,64]{1,0:T(4,128)(2,1)S(1)} %copy-done.8, bf16[1,64]{1,0:T(2,128)(2,1)S(1)} %bitcast.9, ...), custom_call_target="tpu_custom_call" | custom-call | flops 2400000000 | bytes 1048576 | tf_op jit(solution)/shard_map/attention/pallas_call | solution.py:31
  54.9 1.6 %collective-permute-done.8.value = bf16[768,128]{1,0:T(8,128)(2,1)S(1)} collective-permute-done((bf16[768,128]{1,0:T(8,128)(2,1)S(1)}, bf16[768,128]{1,0:T(8,128)(2,1)S(1)}, u32[]{:S(2)}, u32[]{:S(2)}) %collective-permute-start.8) | collective-permute-done | bytes 196640 | tf_op jit(solution)/shard_map/ppermute | solution.py:362
  56.5 0.8 %collective-permute-start.14 = (bf16[768,128]{1,0:T(8,128)(2,1)S(1)}, bf16[768,128]{1,0:T(8,128)(2,1)S(1)}, u32[]{:S(2)}, u32[]{:S(2)}) collective-permute-start(bf16[768,128]{1,0:T(8,128)(2,1)S(1)} %order.6.refs_5_), channel_id=1, source_target_pairs={{0,1},{1,0},{2,3},{3,2},{4,5},{5,4},{6,7},{7,6},{8,9},{9,8},{10,11... | collective-permute-start | bytes 589832 | tf_op jit(solution)/shard_map/ppermute | solution.py:362
  57.3 0.0 collective-permute-start.10
  57.3 2.1 %collective-permute-start.19 = (bf16[16,128]{1,0:T(8,128)(2,1)S(1)}, bf16[16,128]{1,0:T(8,128)(2,1)S(1)}, u32[]{:S(2)}, u32[]{:S(2)}) collective-permute-start(bf16[16,128]{1,0:T(8,128)(2,1)S(1)} %order.8.refs_10_), channel_id=1, source_target_pairs={{0,4},{1,5},{2,6},{3,7},{4,0},{5,1},{6,2},{7,3},{8,12},{9,13},{10,... | collective-permute-start | bytes 12296 | tf_op jit(solution)/shard_map/ppermute | solution.py:362
  59.4 0.1 collective-permute-start.17
  59.5 3.3 %attention.5 = (f32[512,1]{1,0:T(8,128)S(1)}, f32[512,1]{1,0:T(8,128)S(1)}, f32[512,256]{1,0:T(8,128)S(1)}) custom-call(bf16[512,256]{1,0:T(8,128)(2,1)S(1)} %copy-done.4, bf16[64,256]{1,0:T(8,128)(2,1)S(1)} %copy-done.6, bf16[64,256]{1,0:T(8,128)(2,1)S(1)} %copy-done.7, bf16[3,64]{1,0:T(4,128)(2,1)S(1)} %copy-done.8, bf16[1,64]{1,0:T(2,128)(2,1)S(1)} %bitcast.10, ...), custom_call_target="tpu_custom_call" | custom-call | flops 2400000000 | bytes 1048576 | tf_op jit(solution)/shard_map/attention/pallas_call | solution.py:31
  62.8 1.6 %collective-permute-start.21 = (bf16[16,128]{1,0:T(8,128)(2,1)S(1)}, bf16[16,128]{1,0:T(8,128)(2,1)S(1)}, u32[]{:S(2)}, u32[]{:S(2)}) collective-permute-start(bf16[16,128]{1,0:T(8,128)(2,1)S(1)} %order.9.refs_14_), channel_id=1, source_target_pairs={{0,2},{1,3},{2,0},{3,1},{4,6},{5,7},{6,4},{7,5},{8,10},{9,11},{10,... | collective-permute-start | bytes 12296 | tf_op jit(solution)/shard_map/ppermute | solution.py:362
  64.5 1.3 %collective-permute-start.16 = (bf16[16,128]{1,0:T(8,128)(2,1)S(1)}, bf16[16,128]{1,0:T(8,128)(2,1)S(1)}, u32[]{:S(2)}, u32[]{:S(2)}) collective-permute-start(bf16[16,128]{1,0:T(8,128)(2,1)S(1)} %order.8.refs_10_), channel_id=1, source_target_pairs={{0,1},{1,0},{2,3},{3,2},{4,5},{5,4},{6,7},{7,6},{8,9},{9,8},{10,11... | collective-permute-start | bytes 12296 | tf_op jit(solution)/shard_map/ppermute | solution.py:362
  65.8 0.0 collective-permute-done.17.refs_12_
  65.8 0.1 collective-permute-start.18
  65.9 0.4 collective-permute-start.20
  66.3 0.1 collective-permute-start.13
  66.4 0.0 collective-permute-done.21.refs_16_
  66.4 0.9 %collective-permute-start.22 = (bf16[16,128]{1,0:T(8,128)(2,1)S(1)}, bf16[16,128]{1,0:T(8,128)(2,1)S(1)}, u32[]{:S(2)}, u32[]{:S(2)}) collective-permute-start(bf16[16,128]{1,0:T(8,128)(2,1)S(1)} %collective-permute-done.21.refs_16_), channel_id=1, source_target_pairs={{0,1},{1,0},{2,3},{3,2},{4,5},{5,4},{6,7},{7,6},{8,9},{9,8},{10,11... | collective-permute-start | bytes 12296 | tf_op jit(solution)/shard_map/ppermute | solution.py:362
  67.3 3.3 %attention.6 = (f32[512,1]{1,0:T(8,128)S(1)}, f32[512,1]{1,0:T(8,128)S(1)}, f32[512,256]{1,0:T(8,128)S(1)}) custom-call(bf16[512,256]{1,0:T(8,128)(2,1)S(1)} %copy-done.4, bf16[64,256]{1,0:T(8,128)(2,1)S(1)} %copy-done.6, bf16[64,256]{1,0:T(8,128)(2,1)S(1)} %copy-done.7, bf16[3,64]{1,0:T(4,128)(2,1)S(1)} %copy-done.8, bf16[1,64]{1,0:T(2,128)(2,1)S(1)} %bitcast.11, ...), custom_call_target="tpu_custom_call" | custom-call | flops 2400000000 | bytes 1048576 | tf_op jit(solution)/shard_map/attention/pallas_call | solution.py:31
  70.6 0.0 collective-permute-done.18.refs_13_
  70.6 0.0 collective-permute-done.20.refs_15_
  70.6 0.0 collective-permute-done.13.refs_6_
  70.6 4.8 %attention.7 = bf16[512,256]{1,0:T(8,128)(2,1)} custom-call(bf16[512,256]{1,0:T(8,128)(2,1)S(1)} %copy-done.4, bf16[64,256]{1,0:T(8,128)(2,1)S(1)} %copy-done.6, bf16[64,256]{1,0:T(8,128)(2,1)S(1)} %copy-done.7, bf16[3,64]{1,0:T(4,128)(2,1)S(1)} %copy-done.8, bf16[1,64]{1,0:T(2,128)(2,1)S(1)} %bitcast.12, bf16[768,128]{1,0:T(8,128)(2,1)S(1)} %order.7.refs_5_, ...), custom_call_target="tpu_custom_call" | custom-call | flops 2400000000 | bytes 1048576 | tf_op jit(solution)/shard_map/attention/pallas_call | solution.py:31
  (38 shorter events, 0.1 us)
Async XLA Ops:
  3.1 11.8 %collective-permute-start.3 = (bf16[64,256]{1,0:T(8,128)(2,1)}, bf16[64,256]{1,0:T(8,128)(2,1)S(1)}, u32[]{:S(2)}, u32[]{:S(2)}) collective-permute-start(bf16[64,256]{1,0:T(8,128)(2,1)} %get-tuple-element.26), channel_id=1, source_target_pairs={{1,2},{3,4},{5,6},{2,1},{4,3},{6,5},{9,10},{11,12},{13,14},{10,9},... | collective-permute-start | bytes 98312 | tf_op jit(solution)/shard_map/ppermute | solution.py:424
  7.2 8.3 %collective-permute-start.4 = (bf16[64,256]{1,0:T(8,128)(2,1)}, bf16[64,256]{1,0:T(8,128)(2,1)S(1)}, u32[]{:S(2)}, u32[]{:S(2)}) collective-permute-start(bf16[64,256]{1,0:T(8,128)(2,1)} %get-tuple-element.27), channel_id=1, source_target_pairs={{0,1},{1,0},{2,3},{3,2},{4,5},{5,4},{6,7},{7,6},{8,9},{9,8},{10,11... | collective-permute-start | bytes 98312 | tf_op jit(solution)/shard_map/ppermute | solution.py:362
  7.3 1.5 %collective-permute-start = (f32[1,256]{1,0:T(1,128)}, f32[1,256]{1,0:T(1,128)S(1)}, u32[]{:S(2)}, u32[]{:S(2)}) collective-permute-start(f32[1,256]{1,0:T(1,128)} %get-tuple-element.24), channel_id=1, source_target_pairs={{0,1},{1,0},{2,3},{3,2},{4,5},{5,4},{6,7},{7,6},{8,9},{9,8},{10,11... | collective-permute-start | bytes 3080 | tf_op jit(solution)/shard_map/ppermute | solution.py:362
  9.5 2.6 %collective-permute-start.1 = (f32[1,256]{1,0:T(1,128)S(1)}, f32[1,256]{1,0:T(1,128)S(1)}, u32[]{:S(2)}, u32[]{:S(2)}) collective-permute-start(f32[1,256]{1,0:T(1,128)S(1)} %add.6), channel_id=1, source_target_pairs={{0,2},{1,3},{2,0},{3,1},{4,6},{5,7},{6,4},{7,5},{8,10},{9,11},{10,... | collective-permute-start | bytes 3080 | tf_op jit(solution)/shard_map/ppermute | solution.py:362
  12.1 8.2 %collective-permute-start.2 = (f32[1,256]{1,0:T(1,128)S(1)}, f32[1,256]{1,0:T(1,128)S(1)}, u32[]{:S(2)}, u32[]{:S(2)}) collective-permute-start(f32[1,256]{1,0:T(1,128)S(1)} %add.7.earlier.mine), channel_id=1, source_target_pairs={{0,4},{1,5},{2,6},{3,7},{4,0},{5,1},{6,2},{7,3},{8,12},{9,13},{10,... | collective-permute-start | bytes 3080 | tf_op jit(solution)/shard_map/ppermute | solution.py:362
  15.0 0.6 copy-start.3
  15.6 0.6 copy-start.11
  16.2 4.1 %copy-start.1 = (bf16[256,256]{1,0:T(8,128)(2,1)S(1)}, bf16[256,256]{1,0:T(8,128)(2,1)}, u32[]{:S(2)}) copy-start(bf16[256,256]{1,0:T(8,128)(2,1)} %w_ptr.1) | copy-start | bytes 393220
  16.2 35.3 %copy-start.4 = (bf16[512,256]{1,0:T(8,128)(2,1)S(1)}, bf16[512,256]{1,0:T(8,128)(2,1)}, u32[]{:S(2)}) copy-start(bf16[512,256]{1,0:T(8,128)(2,1)} %get-tuple-element.23.refs_0_) | copy-start | bytes 786436
  16.2 35.3 %copy-start.6 = (bf16[64,256]{1,0:T(8,128)(2,1)S(1)}, bf16[64,256]{1,0:T(8,128)(2,1)}, u32[]{:S(2)}) copy-start(bf16[64,256]{1,0:T(8,128)(2,1)} %refs_1_.9) | copy-start | bytes 98308
  16.2 35.3 %copy-start.7 = (bf16[64,256]{1,0:T(8,128)(2,1)S(1)}, bf16[64,256]{1,0:T(8,128)(2,1)}, u32[]{:S(2)}) copy-start(bf16[64,256]{1,0:T(8,128)(2,1)} %refs_2_.7) | copy-start | bytes 98308
  16.2 35.3 %copy-start.8 = (bf16[3,64]{1,0:T(4,128)(2,1)S(1)}, bf16[3,64]{1,0:T(4,128)(2,1)}, u32[]{:S(2)}) copy-start(bf16[3,64]{1,0:T(4,128)(2,1)} %refs_3_.9) | copy-start | bytes 1156
  16.2 35.3 %copy-start.9 = (bf16[64]{0:T(256)(128)(2,1)S(1)}, bf16[64]{0:T(256)(128)(2,1)}, u32[]{:S(2)}) copy-start(bf16[64]{0:T(256)(128)(2,1)} %param.27) | copy-start | bytes 388
  20.3 0.8 %copy-start.2 = (bf16[256,128]{1,0:T(8,128)(2,1)S(1)}, bf16[256,128]{1,0:T(8,128)(2,1)}, u32[]{:S(2)}) copy-start(bf16[256,128]{1,0:T(8,128)(2,1)} %get-tuple-element.28.own) | copy-start | bytes 196612
  21.9 18.1 %collective-permute-start.6 = (bf16[272,128]{1,0:T(8,128)(2,1)S(1)}, bf16[272,128]{1,0:T(8,128)(2,1)S(1)}, u32[]{:S(2)}, u32[]{:S(2)}) collective-permute-start(bf16[272,128]{1,0:T(8,128)(2,1)S(1)} %get-tuple-element.29.couple), channel_id=1, source_target_pairs={{0,16},{1,17},{2,18},{3,19},{4,20},{5,21},{6,22},{7,23},{8,24},{9,... | collective-permute-start | bytes 208904 | tf_op jit(solution)/shard_map/ppermute | solution.py:464
  27.1 6.3 %collective-permute-start.5 = (bf16[256,128]{1,0:T(8,128)(2,1)}, bf16[256,128]{1,0:T(8,128)(2,1)S(1)}, u32[]{:S(2)}, u32[]{:S(2)}) collective-permute-start(bf16[256,128]{1,0:T(8,128)(2,1)} %get-tuple-element.28.own), channel_id=1, source_target_pairs={{0,8},{1,9},{2,10},{3,11},{4,12},{5,13},{6,14},{7,15},{8,16},{9,17... | collective-permute-start | bytes 196616 | tf_op jit(solution)/shard_map/ppermute | solution.py:452
  30.8 9.2 %collective-permute-start.7 = (bf16[256,128]{1,0:T(8,128)(2,1)}, bf16[256,128]{1,0:T(8,128)(2,1)S(1)}, u32[]{:S(2)}, u32[]{:S(2)}) collective-permute-start(bf16[256,128]{1,0:T(8,128)(2,1)} %get-tuple-element.28.own), channel_id=1, source_target_pairs={{0,24},{1,25},{2,26},{3,27},{4,28},{5,29},{6,30},{7,31},{12,32},{1... | collective-permute-start | bytes 196616 | tf_op jit(solution)/shard_map/ppermute | solution.py:453
  40.1 8.8 %collective-permute-start.11 = (bf16[768,128]{1,0:T(8,128)(2,1)S(1)}, bf16[768,128]{1,0:T(8,128)(2,1)S(1)}, u32[]{:S(2)}, u32[]{:S(2)}) collective-permute-start(bf16[768,128]{1,0:T(8,128)(2,1)S(1)} %get-tuple-element.30.refs_5_), channel_id=1, source_target_pairs={{0,2},{1,3},{2,0},{3,1},{4,6},{5,7},{6,4},{7,5},{8,10},{9,11},{10,... | collective-permute-start | bytes 589832 | tf_op jit(solution)/shard_map/ppermute | solution.py:362
  41.5 10.0 %collective-permute-start.9 = (bf16[768,128]{1,0:T(8,128)(2,1)S(1)}, bf16[768,128]{1,0:T(8,128)(2,1)S(1)}, u32[]{:S(2)}, u32[]{:S(2)}) collective-permute-start(bf16[768,128]{1,0:T(8,128)(2,1)S(1)} %get-tuple-element.30.refs_5_), channel_id=1, source_target_pairs={{0,1},{1,0},{2,3},{3,2},{4,5},{5,4},{6,7},{7,6},{8,9},{9,8},{10,11... | collective-permute-start | bytes 589832 | tf_op jit(solution)/shard_map/ppermute | solution.py:362
  44.9 11.6 %collective-permute-start.8 = (bf16[768,128]{1,0:T(8,128)(2,1)S(1)}, bf16[768,128]{1,0:T(8,128)(2,1)S(1)}, u32[]{:S(2)}, u32[]{:S(2)}) collective-permute-start(bf16[768,128]{1,0:T(8,128)(2,1)S(1)} %get-tuple-element.30.refs_5_), channel_id=1, source_target_pairs={{0,4},{1,5},{2,6},{3,7},{4,0},{5,1},{6,2},{7,3},{8,12},{9,13},{10,... | collective-permute-start | bytes 589832 | tf_op jit(solution)/shard_map/ppermute | solution.py:362
  45.6 11.7 %collective-permute-start.15 = (bf16[16,128]{1,0:T(8,128)(2,1)S(1)}, bf16[16,128]{1,0:T(8,128)(2,1)S(1)}, u32[]{:S(2)}, u32[]{:S(2)}) collective-permute-start(bf16[16,128]{1,0:T(8,128)(2,1)S(1)} %get-tuple-element.40), channel_id=1, source_target_pairs={{0,8},{8,16},{1,17},{16,24},{9,25},{28,32},{21,33},{32,40},{29,41}... | collective-permute-start | bytes 12296 | tf_op jit(solution)/shard_map/ppermute | solution.py:479
  48.9 10.6 %collective-permute-start.12 = (bf16[768,128]{1,0:T(8,128)(2,1)S(1)}, bf16[768,128]{1,0:T(8,128)(2,1)S(1)}, u32[]{:S(2)}, u32[]{:S(2)}) collective-permute-start(bf16[768,128]{1,0:T(8,128)(2,1)S(1)} %collective-permute-done.11.refs_5_), channel_id=1, source_target_pairs={{0,1},{1,0},{2,3},{3,2},{4,5},{5,4},{6,7},{7,6},{8,9},{9,8},{10,11... | collective-permute-start | bytes 589832 | tf_op jit(solution)/shard_map/ppermute | solution.py:362
  56.5 9.8 %collective-permute-start.14 = (bf16[768,128]{1,0:T(8,128)(2,1)S(1)}, bf16[768,128]{1,0:T(8,128)(2,1)S(1)}, u32[]{:S(2)}, u32[]{:S(2)}) collective-permute-start(bf16[768,128]{1,0:T(8,128)(2,1)S(1)} %order.6.refs_5_), channel_id=1, source_target_pairs={{0,1},{1,0},{2,3},{3,2},{4,5},{5,4},{6,7},{7,6},{8,9},{9,8},{10,11... | collective-permute-start | bytes 589832 | tf_op jit(solution)/shard_map/ppermute | solution.py:362
  57.3 8.6 %collective-permute-start.10 = (bf16[768,128]{1,0:T(8,128)(2,1)S(1)}, bf16[768,128]{1,0:T(8,128)(2,1)S(1)}, u32[]{:S(2)}, u32[]{:S(2)}) collective-permute-start(bf16[768,128]{1,0:T(8,128)(2,1)S(1)} %order.6.refs_5_), channel_id=1, source_target_pairs={{0,2},{1,3},{2,0},{3,1},{4,6},{5,7},{6,4},{7,5},{8,10},{9,11},{10,... | collective-permute-start | bytes 589832 | tf_op jit(solution)/shard_map/ppermute | solution.py:362
  57.3 5.5 %collective-permute-start.19 = (bf16[16,128]{1,0:T(8,128)(2,1)S(1)}, bf16[16,128]{1,0:T(8,128)(2,1)S(1)}, u32[]{:S(2)}, u32[]{:S(2)}) collective-permute-start(bf16[16,128]{1,0:T(8,128)(2,1)S(1)} %order.8.refs_10_), channel_id=1, source_target_pairs={{0,4},{1,5},{2,6},{3,7},{4,0},{5,1},{6,2},{7,3},{8,12},{9,13},{10,... | collective-permute-start | bytes 12296 | tf_op jit(solution)/shard_map/ppermute | solution.py:362
  59.4 6.4 %collective-permute-start.17 = (bf16[16,128]{1,0:T(8,128)(2,1)S(1)}, bf16[16,128]{1,0:T(8,128)(2,1)S(1)}, u32[]{:S(2)}, u32[]{:S(2)}) collective-permute-start(bf16[16,128]{1,0:T(8,128)(2,1)S(1)} %order.8.refs_10_), channel_id=1, source_target_pairs={{0,2},{1,3},{2,0},{3,1},{4,6},{5,7},{6,4},{7,5},{8,10},{9,11},{10,... | collective-permute-start | bytes 12296 | tf_op jit(solution)/shard_map/ppermute | solution.py:362
  59.5 5.0 %copy-start.10 = (bf16[16,256]{1,0:T(8,128)(2,1)S(1)}, bf16[16,256]{1,0:T(8,128)(2,1)}, u32[]{:S(2)}) copy-start(bf16[16,256]{1,0:T(8,128)(2,1)} %param.26) | copy-start | bytes 24580
  62.8 3.6 %collective-permute-start.21 = (bf16[16,128]{1,0:T(8,128)(2,1)S(1)}, bf16[16,128]{1,0:T(8,128)(2,1)S(1)}, u32[]{:S(2)}, u32[]{:S(2)}) collective-permute-start(bf16[16,128]{1,0:T(8,128)(2,1)S(1)} %order.9.refs_14_), channel_id=1, source_target_pairs={{0,2},{1,3},{2,0},{3,1},{4,6},{5,7},{6,4},{7,5},{8,10},{9,11},{10,... | collective-permute-start | bytes 12296 | tf_op jit(solution)/shard_map/ppermute | solution.py:362
  64.5 6.1 %collective-permute-start.16 = (bf16[16,128]{1,0:T(8,128)(2,1)S(1)}, bf16[16,128]{1,0:T(8,128)(2,1)S(1)}, u32[]{:S(2)}, u32[]{:S(2)}) collective-permute-start(bf16[16,128]{1,0:T(8,128)(2,1)S(1)} %order.8.refs_10_), channel_id=1, source_target_pairs={{0,1},{1,0},{2,3},{3,2},{4,5},{5,4},{6,7},{7,6},{8,9},{9,8},{10,11... | collective-permute-start | bytes 12296 | tf_op jit(solution)/shard_map/ppermute | solution.py:362
  65.8 4.8 %collective-permute-start.18 = (bf16[16,128]{1,0:T(8,128)(2,1)S(1)}, bf16[16,128]{1,0:T(8,128)(2,1)S(1)}, u32[]{:S(2)}, u32[]{:S(2)}) collective-permute-start(bf16[16,128]{1,0:T(8,128)(2,1)S(1)} %collective-permute-done.17.refs_12_), channel_id=1, source_target_pairs={{0,1},{1,0},{2,3},{3,2},{4,5},{5,4},{6,7},{7,6},{8,9},{9,8},{10,11... | collective-permute-start | bytes 12296 | tf_op jit(solution)/shard_map/ppermute | solution.py:362
  65.9 4.7 %collective-permute-start.20 = (bf16[16,128]{1,0:T(8,128)(2,1)S(1)}, bf16[16,128]{1,0:T(8,128)(2,1)S(1)}, u32[]{:S(2)}, u32[]{:S(2)}) collective-permute-start(bf16[16,128]{1,0:T(8,128)(2,1)S(1)} %order.9.refs_14_), channel_id=1, source_target_pairs={{0,1},{1,0},{2,3},{3,2},{4,5},{5,4},{6,7},{7,6},{8,9},{9,8},{10,11... | collective-permute-start | bytes 12296 | tf_op jit(solution)/shard_map/ppermute | solution.py:362
  66.3 4.3 %collective-permute-start.13 = (bf16[768,128]{1,0:T(8,128)(2,1)S(1)}, bf16[768,128]{1,0:T(8,128)(2,1)S(1)}, u32[]{:S(2)}, u32[]{:S(2)}) collective-permute-start(bf16[768,128]{1,0:T(8,128)(2,1)S(1)} %order.7.refs_5_), channel_id=1, source_target_pairs={{0,1},{1,0},{2,3},{3,2},{4,5},{5,4},{6,7},{7,6},{8,9},{9,8},{10,11... | collective-permute-start | bytes 589832 | tf_op jit(solution)/shard_map/ppermute | solution.py:362
  66.4 4.2 %collective-permute-start.22 = (bf16[16,128]{1,0:T(8,128)(2,1)S(1)}, bf16[16,128]{1,0:T(8,128)(2,1)S(1)}, u32[]{:S(2)}, u32[]{:S(2)}) collective-permute-start(bf16[16,128]{1,0:T(8,128)(2,1)S(1)} %collective-permute-done.21.refs_16_), channel_id=1, source_target_pairs={{0,1},{1,0},{2,3},{3,2},{4,5},{5,4},{6,7},{7,6},{8,9},{9,8},{10,11... | collective-permute-start | bytes 12296 | tf_op jit(solution)/shard_map/ppermute | solution.py:362
  67.3 3.3 %copy-start = (bf16[1,8,64,256]{3,2,1,0:T(8,128)(2,1)S(1)}, bf16[1,8,64,256]{3,2,1,0:T(8,128)(2,1)}, u32[]{:S(2)}) copy-start(bf16[1,8,64,256]{3,2,1,0:T(8,128)(2,1)} %param.14) | copy-start | bytes 786436
  67.3 3.4 %copy-start.5 = (bf16[256,256]{1,0:T(8,128)(2,1)S(1)}, bf16[256,256]{1,0:T(8,128)(2,1)}, u32[]{:S(2)}) copy-start(bf16[256,256]{1,0:T(8,128)(2,1)} %refs_19_.1) | copy-start | bytes 393220

commit v4 on v3

--- a/solution.py
+++ b/solution.py
@@ -175,6 +175,12 @@
     window[...] = (mine + behind).astype(bf16)
 
 
+def join_kernel(block, tail, far, out):
+    out[0:PAY, :] = block[...]
+    out[PAY : PAY + 16, :] = tail[...]
+    out[PAY + 16 : PAY + 32, :] = far[...]
+
+
 def twice(w):
     zero = jnp.zeros_like(w)
     return jnp.concatenate(
@@ -183,7 +189,6 @@
 
 
 QT = 256
-HOLDERS = (0, 1, 2, 3, 4, 5, 6, 7)
 
 
 def attention_kernel(count, first, last, *refs):
@@ -196,7 +201,7 @@
     else:
         state_in, refs = refs[:3], refs[3:]
     if last:
-        tails, refs = refs[:BANDS], refs[BANDS:]
+        carriers, refs = refs[:2] + blocks, refs[2:]
         feat, w_proj, ptr_tpos, attended, keys, values, top, norm, mixed, ptr_tok = refs
     else:
         top, norm, mixed, keys, values = refs
@@ -265,9 +270,11 @@
         widened = jnp.dot(ptr_tpos[...], wk, preferred_element_type=f32)
         lane = lax.broadcasted_iota(jnp.int32, (1, POINTERS * 4), 1)
         here = lax.axis_index("space")
-        for tail, holder in zip(tails, HOLDERS):
-            at = pl.ds(pl.multiple_of((here ^ holder) * 8, 8), 8)
-            ptr_tok[at, :] = tail[...].astype(f32)[0:8, :]
+        for i, carrier in enumerate(carriers):
+            for half in range(2):
+                at = pl.ds(pl.multiple_of((here ^ (i + 4 * half)) * 8, 8), 8)
+                start = PAY + 16 * half
+                ptr_tok[at, :] = carrier[start : start + 16, :].astype(f32)[0:8, :]
         rows = [(2 * (i // 4) + i % 2) * 8 + 2 * (i % 4 // 2) for i in range(POINTERS)]
         tok = jnp.concatenate([ptr_tok[r : r + 2, :] for r in rows], axis=0).astype(bf16)
         k = (jnp.dot(tok, wk, preferred_element_type=f32) + widened).astype(bf16)
@@ -478,26 +485,26 @@
     two = over_space(own, opposite)
     tail = lax.ppermute(window, BOTH, pointer_route())
     state = attend(query, weights, [own, over_space(own, sibling)])
-    two = after(two, state[2])
     tail = after(tail, state[2])
+    two = call(
+        join_kernel,
+        sds((PAY + 32, 128), bf16),
+        two,
+        tail,
+        over_space(tail, opposite),
+        name="join",
+    )
     three = over_space(two, beside)
-    tails = [tail, over_space(tail, beside), over_space(tail, opposite)]
     state = attend(query, weights, [one, over_space(one, sibling)], state)
+    two_beside = over_space(two, sibling)
+    state = attend(query, weights, [two, two_beside], state)
     three = after(three, state[2])
-    tails[2] = after(tails[2], state[2])
-    tails.append(over_space(tails[2], beside))
-    state = attend(query, weights, [two, over_space(two, sibling)], state)
     attended = attend(
         query,
         weights,
         [three, over_space(three, sibling)],
         state,
-        [
-            *(x for t in tails for x in (t, over_space(t, sibling))),
-            feat,
-            w_proj,
-            ptr_tpos.reshape(POINTERS * 2, 128),
-        ],
+        [two, two_beside, feat, w_proj, ptr_tpos.reshape(POINTERS * 2, 128)],
     )
     return (
         attended.reshape(1, ROWS, COLS, D),

time: 75.9 us -> 75.6 us (level)
  starting transfers between devices: 39.3 us -> 36.6 us
  waiting for transfers between devices: 10.3 us -> 12.1 us
    ppermute x18 -> x12, starting transfers between devices: 20.5 us -> 17.8 us  [over_space(): return lax.ppermute(x, 'space', [(i, target(i)) for i in range(BANDS)])]
    ppermute x18 -> x12, waiting for transfers between devices: 3.66 us -> 5.46 us  [over_space(): return lax.ppermute(x, 'space', [(i, target(i)) for i in range(BANDS)])]
    pallas_call x13 -> x12, Pallas kernels: 22.2 us -> 22.9 us  [call(): pl.pallas_call(kernel, out_shape=out_shape, in_specs=[vmem] * len(args) i...]
  transfers between devices with their start and end apart: 23 -> 17, of which waited for: 4 -> 6; matrix products, arithmetic and copies ran while one was open for 1% -> 1% of each run, Pallas kernels for 19% -> 19%
where the time goes in v4:
time: 75.6 us; the launch traced here: 75.3 us
  starting transfers between devices  36.6 us (48%)
  Pallas kernels  22.9 us (30%)
  waiting for transfers between devices  12.1 us (16%)
  local copies, waits for them, and re-layouts  2.09 us (3%)
  between operations  0.89 us (1%)
    pallas_call x12, Pallas kernels, call(): pl.pallas_call(kernel, out_shape=out_shape, in_specs=[vmem] * len(args) i...  22.9 us
    ppermute x12, starting transfers between devices, over_space(): return lax.ppermute(x, 'space', [(i, target(i)) for i in range(BANDS)])  17.8 us
    ppermute x1, waiting for transfers between devices, body(): third = lax.ppermute(pairs, BOTH, later(3))  6.65 us
    ppermute x12, waiting for transfers between devices, over_space(): return lax.ppermute(x, 'space', [(i, target(i)) for i in range(BANDS)])  5.46 us
    ppermute x1, starting transfers between devices, body(): second = lax.ppermute(couple, BOTH, later(2))  5.14 us
    ppermute x1, starting transfers between devices, body(): outer = lax.ppermute(outer, 'space', links + [(b, a) for a, b in links])  4.11 us
    ppermute x1, starting transfers between devices, body(): first = lax.ppermute(pairs, BOTH, later(1))  3.72 us
    ppermute x1, starting transfers between devices, body(): tail = lax.ppermute(window, BOTH, pointer_route())  3.27 us
  transfers between devices with their start and end apart: 17, of which 6 were waited for; matrix products, arithmetic and copies ran while one was open for 1% of the time, Pallas kernels for 19%

profile of v4, /device:TPU:13, one launch (start us, length us, event | category | flops | bytes accessed | tf_op | source)
XLA Modules:
  0.0 75.3 jit_solution(6813242230947485363)
XLA Ops:
  0.6 2.5 %joined.1 = (bf16[512,256]{1,0:T(8,128)(2,1)}, bf16[64,256]{1,0:T(8,128)(2,1)}, bf16[64,256]{1,0:T(8,128)(2,1)}, f32[1,256]{1,0:T(1,128)}, bf16[512,256]{1,0:T(8,128)(2,1)}) custom-call(bf16[512,256]{1,0:T(8,128)(2,1)} %bitcast.7, bf16[256,256]{1,0:T(8,128)(2,1)} %refs_1_.5, s32[8,64]{1,0:T(8,128)} %bitcast.13, bf16[256]{0:T(256)(128)(2,1)} %refs_3_.5, ...), custom_call_target="tpu_custom_call" | custom-call | flops 140000000 | bytes 1048576 | tf_op jit(solution)/shard_map/joined/pallas_call | solution.py:31
  3.1 4.1 %collective-permute-start.3 = (bf16[64,256]{1,0:T(8,128)(2,1)}, bf16[64,256]{1,0:T(8,128)(2,1)S(1)}, u32[]{:S(2)}, u32[]{:S(2)}) collective-permute-start(bf16[64,256]{1,0:T(8,128)(2,1)} %get-tuple-element.26), channel_id=1, source_target_pairs={{1,2},{3,4},{5,6},{2,1},{4,3},{6,5},{9,10},{11,12},{13,14},{10,9},... | collective-permute-start | bytes 98312 | tf_op jit(solution)/shard_map/ppermute | solution.py:431
  7.2 0.1 collective-permute-start.4
  7.3 0.5 collective-permute-start
  7.8 1.0 %collective-permute-done = f32[1,256]{1,0:T(1,128)S(1)} collective-permute-done((f32[1,256]{1,0:T(1,128)}, f32[1,256]{1,0:T(1,128)S(1)}, u32[]{:S(2)}, u32[]{:S(2)}) %collective-permute-start) | collective-permute-done | bytes 1056 | tf_op jit(solution)/shard_map/ppermute | solution.py:369
  8.8 0.7 add.6
  9.5 1.6 %collective-permute-start.1 = (f32[1,256]{1,0:T(1,128)S(1)}, f32[1,256]{1,0:T(1,128)S(1)}, u32[]{:S(2)}, u32[]{:S(2)}) collective-permute-start(f32[1,256]{1,0:T(1,128)S(1)} %add.6), channel_id=1, source_target_pairs={{0,2},{1,3},{2,0},{3,1},{4,6},{5,7},{6,4},{7,5},{8,10},{9,11},{10,... | collective-permute-start | bytes 3080 | tf_op jit(solution)/shard_map/ppermute | solution.py:369
  11.2 1.0 %collective-permute-done.1 = f32[1,256]{1,0:T(1,128)S(1)} collective-permute-done((f32[1,256]{1,0:T(1,128)S(1)}, f32[1,256]{1,0:T(1,128)S(1)}, u32[]{:S(2)}, u32[]{:S(2)}) %collective-permute-start.1) | collective-permute-done | bytes 1056 | tf_op jit(solution)/shard_map/ppermute | solution.py:369
  12.1 2.8 %collective-permute-start.2 = (f32[1,256]{1,0:T(1,128)S(1)}, f32[1,256]{1,0:T(1,128)S(1)}, u32[]{:S(2)}, u32[]{:S(2)}) collective-permute-start(f32[1,256]{1,0:T(1,128)S(1)} %add.7.earlier.mine), channel_id=1, source_target_pairs={{0,4},{1,5},{2,6},{3,7},{4,0},{5,1},{6,2},{7,3},{8,12},{9,13},{10,... | collective-permute-start | bytes 3080 | tf_op jit(solution)/shard_map/ppermute | solution.py:369
  14.9 0.0 collective-permute-done.3.value
  14.9 0.6 copy-done.3
  15.6 0.0 collective-permute-done.4.refs_2_
  15.6 0.6 copy-done.11
  16.2 0.0 copy-start.8
  16.2 0.0 copy-start.9
  16.2 4.1 %conv.1 = (bf16[8,4096]{1,0:T(8,128)(2,1)}, bf16[256,128]{1,0:T(8,128)(2,1)}) custom-call(bf16[512,256]{1,0:T(8,128)(2,1)} %get-tuple-element.25.refs_0_, bf16[64,256]{1,0:T(8,128)(2,1)} %copy-done.3, bf16[64,256]{1,0:T(8,128)(2,1)} %copy-done.11, bf16[3,768,256]{2,1,0:T(8,128)(2,1)} %bitcast.14, bf16[64,256]{1,0:T(8,128)(2,1)} %bitcast.15), custom_call_target="tpu_custom_call" | custom-call | flops 640000000 | bytes 1048576 | tf_op jit(solution)/shard_map/conv/pallas_call | solution.py:31
  20.3 0.0 collective-permute-done.2.other
  20.3 0.8 %copy-done.2 = bf16[256,128]{1,0:T(8,128)(2,1)S(1)} copy-done((bf16[256,128]{1,0:T(8,128)(2,1)S(1)}, bf16[256,128]{1,0:T(8,128)(2,1)}, u32[]{:S(2)}) %copy-start.2) | copy-done | bytes 65560
  21.2 0.8 %pair.1 = (bf16[1,256]{1,0:T(2,128)(2,1)}, bf16[272,128]{1,0:T(8,128)(2,1)S(1)}) custom-call(f32[1,256]{1,0:T(1,128)S(1)} %add.7.earlier.mine, f32[1,256]{1,0:T(1,128)S(1)} %collective-permute-done.2.other, bf16[256,256]{1,0:T(8,128)(2,1)S(1)} %copy-done.1, bf16[256,128]{1,0:T(8,128)(2,1)S(1)} %copy-done.2), custom_call_target="tpu_custom_call" | custom-call | flops 1000000 | bytes 1048576 | tf_op jit(solution)/shard_map/pair/pallas_call | solution.py:31
  21.9 5.1 %collective-permute-start.6 = (bf16[272,128]{1,0:T(8,128)(2,1)S(1)}, bf16[272,128]{1,0:T(8,128)(2,1)S(1)}, u32[]{:S(2)}, u32[]{:S(2)}) collective-permute-start(bf16[272,128]{1,0:T(8,128)(2,1)S(1)} %get-tuple-element.29.couple), channel_id=1, source_target_pairs={{0,16},{1,17},{2,18},{3,19},{4,20},{5,21},{6,22},{7,23},{8,24},{9,... | collective-permute-start | bytes 208904 | tf_op jit(solution)/shard_map/ppermute | solution.py:471
  27.1 3.7 %collective-permute-start.5 = (bf16[256,128]{1,0:T(8,128)(2,1)}, bf16[256,128]{1,0:T(8,128)(2,1)S(1)}, u32[]{:S(2)}, u32[]{:S(2)}) collective-permute-start(bf16[256,128]{1,0:T(8,128)(2,1)} %get-tuple-element.28.own), channel_id=1, source_target_pairs={{0,8},{1,9},{2,10},{3,11},{4,12},{5,13},{6,14},{7,15},{8,16},{9,17... | collective-permute-start | bytes 196616 | tf_op jit(solution)/shard_map/ppermute | solution.py:459
  30.8 2.6 %collective-permute-start.7 = (bf16[256,128]{1,0:T(8,128)(2,1)}, bf16[256,128]{1,0:T(8,128)(2,1)S(1)}, u32[]{:S(2)}, u32[]{:S(2)}) collective-permute-start(bf16[256,128]{1,0:T(8,128)(2,1)} %get-tuple-element.28.own), channel_id=1, source_target_pairs={{0,24},{1,25},{2,26},{3,27},{4,28},{5,29},{6,30},{7,31},{12,32},{1... | collective-permute-start | bytes 196616 | tf_op jit(solution)/shard_map/ppermute | solution.py:460
  33.4 0.0 collective-permute-done.5.first
  33.4 6.6 %collective-permute-done.7.third = bf16[256,128]{1,0:T(8,128)(2,1)S(1)} collective-permute-done((bf16[256,128]{1,0:T(8,128)(2,1)}, bf16[256,128]{1,0:T(8,128)(2,1)S(1)}, u32[]{:S(2)}, u32[]{:S(2)}) %collective-permute-start.7) | collective-permute-done | bytes 65568 | tf_op jit(solution)/shard_map/ppermute | solution.py:460
  40.0 0.0 collective-permute-done.6.second
  40.1 1.4 %collective-permute-start.14 = (bf16[768,128]{1,0:T(8,128)(2,1)S(1)}, bf16[768,128]{1,0:T(8,128)(2,1)S(1)}, u32[]{:S(2)}, u32[]{:S(2)}) collective-permute-start(bf16[768,128]{1,0:T(8,128)(2,1)S(1)} %get-tuple-element.30.refs_5_), channel_id=1, source_target_pairs={{0,2},{1,3},{2,0},{3,1},{4,6},{5,7},{6,4},{7,5},{8,10},{9,11},{10,... | collective-permute-start | bytes 589832 | tf_op jit(solution)/shard_map/ppermute | solution.py:369
  41.5 3.4 %collective-permute-start.10 = (bf16[768,128]{1,0:T(8,128)(2,1)S(1)}, bf16[768,128]{1,0:T(8,128)(2,1)S(1)}, u32[]{:S(2)}, u32[]{:S(2)}) collective-permute-start(bf16[768,128]{1,0:T(8,128)(2,1)S(1)} %get-tuple-element.30.refs_5_), channel_id=1, source_target_pairs={{0,1},{1,0},{2,3},{3,2},{4,5},{5,4},{6,7},{7,6},{8,9},{9,8},{10,11... | collective-permute-start | bytes 589832 | tf_op jit(solution)/shard_map/ppermute | solution.py:369
  44.9 0.7 collective-permute-start.8
  45.6 3.3 %collective-permute-start.9 = (bf16[16,128]{1,0:T(8,128)(2,1)S(1)}, bf16[16,128]{1,0:T(8,128)(2,1)S(1)}, u32[]{:S(2)}, u32[]{:S(2)}) collective-permute-start(bf16[16,128]{1,0:T(8,128)(2,1)S(1)} %get-tuple-element.31), channel_id=1, source_target_pairs={{0,8},{8,16},{1,17},{16,24},{9,25},{28,32},{21,33},{32,40},{29,41}... | collective-permute-start | bytes 12296 | tf_op jit(solution)/shard_map/ppermute | solution.py:486
  48.9 0.0 collective-permute-done.14.refs_5_
  48.9 2.6 %collective-permute-start.15 = (bf16[768,128]{1,0:T(8,128)(2,1)S(1)}, bf16[768,128]{1,0:T(8,128)(2,1)S(1)}, u32[]{:S(2)}, u32[]{:S(2)}) collective-permute-start(bf16[768,128]{1,0:T(8,128)(2,1)S(1)} %collective-permute-done.14.refs_5_), channel_id=1, source_target_pairs={{0,1},{1,0},{2,3},{3,2},{4,5},{5,4},{6,7},{7,6},{8,9},{9,8},{10,11... | collective-permute-start | bytes 589832 | tf_op jit(solution)/shard_map/ppermute | solution.py:369
  51.4 0.0 collective-permute-done.10.refs_6_
  51.5 3.6 %attention.4 = (f32[512,1]{1,0:T(8,128)S(1)}, f32[512,1]{1,0:T(8,128)S(1)}, f32[512,256]{1,0:T(8,128)S(1)}) custom-call(bf16[512,256]{1,0:T(8,128)(2,1)S(1)} %copy-done.4, bf16[64,256]{1,0:T(8,128)(2,1)S(1)} %copy-done.6, bf16[64,256]{1,0:T(8,128)(2,1)S(1)} %copy-done.7, bf16[3,64]{1,0:T(4,128)(2,1)S(1)} %copy-done.8, bf16[1,64]{1,0:T(2,128)(2,1)S(1)} %bitcast.9, ...), custom_call_target="tpu_custom_call" | custom-call | flops 2400000000 | bytes 1048576 | tf_op jit(solution)/shard_map/attention/pallas_call | solution.py:31
  55.1 0.0 collective-permute-done.9.value
  55.1 1.1 %collective-permute-start.11 = (bf16[16,128]{1,0:T(8,128)(2,1)S(1)}, bf16[16,128]{1,0:T(8,128)(2,1)S(1)}, u32[]{:S(2)}, u32[]{:S(2)}) collective-permute-start(bf16[16,128]{1,0:T(8,128)(2,1)S(1)} %order.4.tail), channel_id=1, source_target_pairs={{0,4},{1,5},{2,6},{3,7},{4,0},{5,1},{6,2},{7,3},{8,12},{9,13},{10,... | collective-permute-start | bytes 12296 | tf_op jit(solution)/shard_map/ppermute | solution.py:369
  56.1 0.4 collective-permute-done.8.block
  56.5 2.0 %collective-permute-done.11.far = bf16[16,128]{1,0:T(8,128)(2,1)S(1)} collective-permute-done((bf16[16,128]{1,0:T(8,128)(2,1)S(1)}, bf16[16,128]{1,0:T(8,128)(2,1)S(1)}, u32[]{:S(2)}, u32[]{:S(2)}) %collective-permute-start.11) | collective-permute-done | bytes 4128 | tf_op jit(solution)/shard_map/ppermute | solution.py:369
  58.6 1.2 %collective-permute-start.13 = (bf16[800,128]{1,0:T(8,128)(2,1)S(1)}, bf16[800,128]{1,0:T(8,128)(2,1)S(1)}, u32[]{:S(2)}, u32[]{:S(2)}) collective-permute-start(bf16[800,128]{1,0:T(8,128)(2,1)S(1)} %join.1.refs_5_.refs_10_), channel_id=1, source_target_pairs={{0,1},{1,0},{2,3},{3,2},{4,5},{5,4},{6,7},{7,6},{8,9},{9,8},{10,11... | collective-permute-start | bytes 614408 | tf_op jit(solution)/shard_map/ppermute | solution.py:369
  59.8 1.7 %collective-permute-start.12 = (bf16[800,128]{1,0:T(8,128)(2,1)S(1)}, bf16[800,128]{1,0:T(8,128)(2,1)S(1)}, u32[]{:S(2)}, u32[]{:S(2)}) collective-permute-start(bf16[800,128]{1,0:T(8,128)(2,1)S(1)} %join.1.refs_5_.refs_10_), channel_id=1, source_target_pairs={{0,2},{1,3},{2,0},{3,1},{4,6},{5,7},{6,4},{7,5},{8,10},{9,11},{10,... | collective-permute-start | bytes 614408 | tf_op jit(solution)/shard_map/ppermute | solution.py:369
  61.5 3.5 %attention.5 = (f32[512,1]{1,0:T(8,128)S(1)}, f32[512,1]{1,0:T(8,128)S(1)}, f32[512,256]{1,0:T(8,128)S(1)}) custom-call(bf16[512,256]{1,0:T(8,128)(2,1)S(1)} %copy-done.4, bf16[64,256]{1,0:T(8,128)(2,1)S(1)} %copy-done.6, bf16[64,256]{1,0:T(8,128)(2,1)S(1)} %copy-done.7, bf16[3,64]{1,0:T(4,128)(2,1)S(1)} %copy-done.8, bf16[1,64]{1,0:T(2,128)(2,1)S(1)} %bitcast.10, ...), custom_call_target="tpu_custom_call" | custom-call | flops 2400000000 | bytes 1048576 | tf_op jit(solution)/shard_map/attention/pallas_call | solution.py:31
  65.0 0.0 copy-start.10
  65.0 0.0 copy-start
  65.0 0.0 copy-start.5
  65.1 3.5 %attention.6 = (f32[512,1]{1,0:T(8,128)S(1)}, f32[512,1]{1,0:T(8,128)S(1)}, f32[512,256]{1,0:T(8,128)S(1)}) custom-call(bf16[512,256]{1,0:T(8,128)(2,1)S(1)} %copy-done.4, bf16[64,256]{1,0:T(8,128)(2,1)S(1)} %copy-done.6, bf16[64,256]{1,0:T(8,128)(2,1)S(1)} %copy-done.7, bf16[3,64]{1,0:T(4,128)(2,1)S(1)} %copy-done.8, bf16[1,64]{1,0:T(2,128)(2,1)S(1)} %bitcast.11, ...), custom_call_target="tpu_custom_call" | custom-call | flops 2400000000 | bytes 1048576 | tf_op jit(solution)/shard_map/attention/pallas_call | solution.py:31
  68.5 0.0 collective-permute-done.12.value
  68.6 0.6 collective-permute-start.16
  69.2 1.1 %collective-permute-done.16.refs_6_ = bf16[800,128]{1,0:T(8,128)(2,1)S(1)} collective-permute-done((bf16[800,128]{1,0:T(8,128)(2,1)S(1)}, bf16[800,128]{1,0:T(8,128)(2,1)S(1)}, u32[]{:S(2)}, u32[]{:S(2)}) %collective-permute-start.16) | collective-permute-done | bytes 204832 | tf_op jit(solution)/shard_map/ppermute | solution.py:369
  70.3 5.0 %attention.7 = bf16[512,256]{1,0:T(8,128)(2,1)} custom-call(bf16[512,256]{1,0:T(8,128)(2,1)S(1)} %copy-done.4, bf16[64,256]{1,0:T(8,128)(2,1)S(1)} %copy-done.6, bf16[64,256]{1,0:T(8,128)(2,1)S(1)} %copy-done.7, bf16[3,64]{1,0:T(4,128)(2,1)S(1)} %copy-done.8, bf16[1,64]{1,0:T(2,128)(2,1)S(1)} %bitcast.12, bf16[800,128]{1,0:T(8,128)(2,1)S(1)} %order.5.refs_5_, ...), custom_call_target="tpu_custom_call" | custom-call | flops 2400000000 | bytes 1048576 | tf_op jit(solution)/shard_map/attention/pallas_call | solution.py:31
  (25 shorter events, 0.1 us)
Async XLA Ops:
  3.1 11.8 %collective-permute-start.3 = (bf16[64,256]{1,0:T(8,128)(2,1)}, bf16[64,256]{1,0:T(8,128)(2,1)S(1)}, u32[]{:S(2)}, u32[]{:S(2)}) collective-permute-start(bf16[64,256]{1,0:T(8,128)(2,1)} %get-tuple-element.26), channel_id=1, source_target_pairs={{1,2},{3,4},{5,6},{2,1},{4,3},{6,5},{9,10},{11,12},{13,14},{10,9},... | collective-permute-start | bytes 98312 | tf_op jit(solution)/shard_map/ppermute | solution.py:431
  7.2 8.3 %collective-permute-start.4 = (bf16[64,256]{1,0:T(8,128)(2,1)}, bf16[64,256]{1,0:T(8,128)(2,1)S(1)}, u32[]{:S(2)}, u32[]{:S(2)}) collective-permute-start(bf16[64,256]{1,0:T(8,128)(2,1)} %get-tuple-element.27), channel_id=1, source_target_pairs={{0,1},{1,0},{2,3},{3,2},{4,5},{5,4},{6,7},{7,6},{8,9},{9,8},{10,11... | collective-permute-start | bytes 98312 | tf_op jit(solution)/shard_map/ppermute | solution.py:369
  7.3 1.5 %collective-permute-start = (f32[1,256]{1,0:T(1,128)}, f32[1,256]{1,0:T(1,128)S(1)}, u32[]{:S(2)}, u32[]{:S(2)}) collective-permute-start(f32[1,256]{1,0:T(1,128)} %get-tuple-element.24), channel_id=1, source_target_pairs={{0,1},{1,0},{2,3},{3,2},{4,5},{5,4},{6,7},{7,6},{8,9},{9,8},{10,11... | collective-permute-start | bytes 3080 | tf_op jit(solution)/shard_map/ppermute | solution.py:369
  9.5 2.6 %collective-permute-start.1 = (f32[1,256]{1,0:T(1,128)S(1)}, f32[1,256]{1,0:T(1,128)S(1)}, u32[]{:S(2)}, u32[]{:S(2)}) collective-permute-start(f32[1,256]{1,0:T(1,128)S(1)} %add.6), channel_id=1, source_target_pairs={{0,2},{1,3},{2,0},{3,1},{4,6},{5,7},{6,4},{7,5},{8,10},{9,11},{10,... | collective-permute-start | bytes 3080 | tf_op jit(solution)/shard_map/ppermute | solution.py:369
  12.1 8.2 %collective-permute-start.2 = (f32[1,256]{1,0:T(1,128)S(1)}, f32[1,256]{1,0:T(1,128)S(1)}, u32[]{:S(2)}, u32[]{:S(2)}) collective-permute-start(f32[1,256]{1,0:T(1,128)S(1)} %add.7.earlier.mine), channel_id=1, source_target_pairs={{0,4},{1,5},{2,6},{3,7},{4,0},{5,1},{6,2},{7,3},{8,12},{9,13},{10,... | collective-permute-start | bytes 3080 | tf_op jit(solution)/shard_map/ppermute | solution.py:369
  14.9 0.6 copy-start.3
  15.6 0.6 copy-start.11
  16.2 4.1 %copy-start.1 = (bf16[256,256]{1,0:T(8,128)(2,1)S(1)}, bf16[256,256]{1,0:T(8,128)(2,1)}, u32[]{:S(2)}) copy-start(bf16[256,256]{1,0:T(8,128)(2,1)} %w_ptr.1) | copy-start | bytes 393220
  16.2 35.3 %copy-start.4 = (bf16[512,256]{1,0:T(8,128)(2,1)S(1)}, bf16[512,256]{1,0:T(8,128)(2,1)}, u32[]{:S(2)}) copy-start(bf16[512,256]{1,0:T(8,128)(2,1)} %get-tuple-element.23.refs_0_) | copy-start | bytes 786436
  16.2 35.3 %copy-start.6 = (bf16[64,256]{1,0:T(8,128)(2,1)S(1)}, bf16[64,256]{1,0:T(8,128)(2,1)}, u32[]{:S(2)}) copy-start(bf16[64,256]{1,0:T(8,128)(2,1)} %refs_1_.9) | copy-start | bytes 98308
  16.2 35.3 %copy-start.7 = (bf16[64,256]{1,0:T(8,128)(2,1)S(1)}, bf16[64,256]{1,0:T(8,128)(2,1)}, u32[]{:S(2)}) copy-start(bf16[64,256]{1,0:T(8,128)(2,1)} %refs_2_.7) | copy-start | bytes 98308
  16.2 35.3 %copy-start.8 = (bf16[3,64]{1,0:T(4,128)(2,1)S(1)}, bf16[3,64]{1,0:T(4,128)(2,1)}, u32[]{:S(2)}) copy-start(bf16[3,64]{1,0:T(4,128)(2,1)} %refs_3_.9) | copy-start | bytes 1156
  16.2 35.3 %copy-start.9 = (bf16[64]{0:T(256)(128)(2,1)S(1)}, bf16[64]{0:T(256)(128)(2,1)}, u32[]{:S(2)}) copy-start(bf16[64]{0:T(256)(128)(2,1)} %param.27) | copy-start | bytes 388
  20.3 0.8 %copy-start.2 = (bf16[256,128]{1,0:T(8,128)(2,1)S(1)}, bf16[256,128]{1,0:T(8,128)(2,1)}, u32[]{:S(2)}) copy-start(bf16[256,128]{1,0:T(8,128)(2,1)} %get-tuple-element.28.own) | copy-start | bytes 196612
  21.9 18.1 %collective-permute-start.6 = (bf16[272,128]{1,0:T(8,128)(2,1)S(1)}, bf16[272,128]{1,0:T(8,128)(2,1)S(1)}, u32[]{:S(2)}, u32[]{:S(2)}) collective-permute-start(bf16[272,128]{1,0:T(8,128)(2,1)S(1)} %get-tuple-element.29.couple), channel_id=1, source_target_pairs={{0,16},{1,17},{2,18},{3,19},{4,20},{5,21},{6,22},{7,23},{8,24},{9,... | collective-permute-start | bytes 208904 | tf_op jit(solution)/shard_map/ppermute | solution.py:471
  27.1 6.3 %collective-permute-start.5 = (bf16[256,128]{1,0:T(8,128)(2,1)}, bf16[256,128]{1,0:T(8,128)(2,1)S(1)}, u32[]{:S(2)}, u32[]{:S(2)}) collective-permute-start(bf16[256,128]{1,0:T(8,128)(2,1)} %get-tuple-element.28.own), channel_id=1, source_target_pairs={{0,8},{1,9},{2,10},{3,11},{4,12},{5,13},{6,14},{7,15},{8,16},{9,17... | collective-permute-start | bytes 196616 | tf_op jit(solution)/shard_map/ppermute | solution.py:459
  30.8 9.2 %collective-permute-start.7 = (bf16[256,128]{1,0:T(8,128)(2,1)}, bf16[256,128]{1,0:T(8,128)(2,1)S(1)}, u32[]{:S(2)}, u32[]{:S(2)}) collective-permute-start(bf16[256,128]{1,0:T(8,128)(2,1)} %get-tuple-element.28.own), channel_id=1, source_target_pairs={{0,24},{1,25},{2,26},{3,27},{4,28},{5,29},{6,30},{7,31},{12,32},{1... | collective-permute-start | bytes 196616 | tf_op jit(solution)/shard_map/ppermute | solution.py:460
  40.1 8.8 %collective-permute-start.14 = (bf16[768,128]{1,0:T(8,128)(2,1)S(1)}, bf16[768,128]{1,0:T(8,128)(2,1)S(1)}, u32[]{:S(2)}, u32[]{:S(2)}) collective-permute-start(bf16[768,128]{1,0:T(8,128)(2,1)S(1)} %get-tuple-element.30.refs_5_), channel_id=1, source_target_pairs={{0,2},{1,3},{2,0},{3,1},{4,6},{5,7},{6,4},{7,5},{8,10},{9,11},{10,... | collective-permute-start | bytes 589832 | tf_op jit(solution)/shard_map/ppermute | solution.py:369
  41.5 10.0 %collective-permute-start.10 = (bf16[768,128]{1,0:T(8,128)(2,1)S(1)}, bf16[768,128]{1,0:T(8,128)(2,1)S(1)}, u32[]{:S(2)}, u32[]{:S(2)}) collective-permute-start(bf16[768,128]{1,0:T(8,128)(2,1)S(1)} %get-tuple-element.30.refs_5_), channel_id=1, source_target_pairs={{0,1},{1,0},{2,3},{3,2},{4,5},{5,4},{6,7},{7,6},{8,9},{9,8},{10,11... | collective-permute-start | bytes 589832 | tf_op jit(solution)/shard_map/ppermute | solution.py:369
  44.9 11.6 %collective-permute-start.8 = (bf16[768,128]{1,0:T(8,128)(2,1)S(1)}, bf16[768,128]{1,0:T(8,128)(2,1)S(1)}, u32[]{:S(2)}, u32[]{:S(2)}) collective-permute-start(bf16[768,128]{1,0:T(8,128)(2,1)S(1)} %get-tuple-element.30.refs_5_), channel_id=1, source_target_pairs={{0,4},{1,5},{2,6},{3,7},{4,0},{5,1},{6,2},{7,3},{8,12},{9,13},{10,... | collective-permute-start | bytes 589832 | tf_op jit(solution)/shard_map/ppermute | solution.py:369
  45.6 9.5 %collective-permute-start.9 = (bf16[16,128]{1,0:T(8,128)(2,1)S(1)}, bf16[16,128]{1,0:T(8,128)(2,1)S(1)}, u32[]{:S(2)}, u32[]{:S(2)}) collective-permute-start(bf16[16,128]{1,0:T(8,128)(2,1)S(1)} %get-tuple-element.31), channel_id=1, source_target_pairs={{0,8},{8,16},{1,17},{16,24},{9,25},{28,32},{21,33},{32,40},{29,41}... | collective-permute-start | bytes 12296 | tf_op jit(solution)/shard_map/ppermute | solution.py:486
  48.9 12.6 %collective-permute-start.15 = (bf16[768,128]{1,0:T(8,128)(2,1)S(1)}, bf16[768,128]{1,0:T(8,128)(2,1)S(1)}, u32[]{:S(2)}, u32[]{:S(2)}) collective-permute-start(bf16[768,128]{1,0:T(8,128)(2,1)S(1)} %collective-permute-done.14.refs_5_), channel_id=1, source_target_pairs={{0,1},{1,0},{2,3},{3,2},{4,5},{5,4},{6,7},{7,6},{8,9},{9,8},{10,11... | collective-permute-start | bytes 589832 | tf_op jit(solution)/shard_map/ppermute | solution.py:369
  55.1 3.4 %collective-permute-start.11 = (bf16[16,128]{1,0:T(8,128)(2,1)S(1)}, bf16[16,128]{1,0:T(8,128)(2,1)S(1)}, u32[]{:S(2)}, u32[]{:S(2)}) collective-permute-start(bf16[16,128]{1,0:T(8,128)(2,1)S(1)} %order.4.tail), channel_id=1, source_target_pairs={{0,4},{1,5},{2,6},{3,7},{4,0},{5,1},{6,2},{7,3},{8,12},{9,13},{10,... | collective-permute-start | bytes 12296 | tf_op jit(solution)/shard_map/ppermute | solution.py:369
  58.6 6.5 %collective-permute-start.13 = (bf16[800,128]{1,0:T(8,128)(2,1)S(1)}, bf16[800,128]{1,0:T(8,128)(2,1)S(1)}, u32[]{:S(2)}, u32[]{:S(2)}) collective-permute-start(bf16[800,128]{1,0:T(8,128)(2,1)S(1)} %join.1.refs_5_.refs_10_), channel_id=1, source_target_pairs={{0,1},{1,0},{2,3},{3,2},{4,5},{5,4},{6,7},{7,6},{8,9},{9,8},{10,11... | collective-permute-start | bytes 614408 | tf_op jit(solution)/shard_map/ppermute | solution.py:369
  59.8 8.7 %collective-permute-start.12 = (bf16[800,128]{1,0:T(8,128)(2,1)S(1)}, bf16[800,128]{1,0:T(8,128)(2,1)S(1)}, u32[]{:S(2)}, u32[]{:S(2)}) collective-permute-start(bf16[800,128]{1,0:T(8,128)(2,1)S(1)} %join.1.refs_5_.refs_10_), channel_id=1, source_target_pairs={{0,2},{1,3},{2,0},{3,1},{4,6},{5,7},{6,4},{7,5},{8,10},{9,11},{10,... | collective-permute-start | bytes 614408 | tf_op jit(solution)/shard_map/ppermute | solution.py:369
  65.0 4.2 %copy-start.10 = (bf16[16,256]{1,0:T(8,128)(2,1)S(1)}, bf16[16,256]{1,0:T(8,128)(2,1)}, u32[]{:S(2)}) copy-start(bf16[16,256]{1,0:T(8,128)(2,1)} %param.26) | copy-start | bytes 24580
  65.0 5.3 %copy-start = (bf16[1,8,64,256]{3,2,1,0:T(8,128)(2,1)S(1)}, bf16[1,8,64,256]{3,2,1,0:T(8,128)(2,1)}, u32[]{:S(2)}) copy-start(bf16[1,8,64,256]{3,2,1,0:T(8,128)(2,1)} %param.14) | copy-start | bytes 786436
  65.0 5.2 %copy-start.5 = (bf16[256,256]{1,0:T(8,128)(2,1)S(1)}, bf16[256,256]{1,0:T(8,128)(2,1)}, u32[]{:S(2)}) copy-start(bf16[256,256]{1,0:T(8,128)(2,1)} %refs_13_.1) | copy-start | bytes 393220
  68.6 1.7 %collective-permute-start.16 = (bf16[800,128]{1,0:T(8,128)(2,1)S(1)}, bf16[800,128]{1,0:T(8,128)(2,1)S(1)}, u32[]{:S(2)}, u32[]{:S(2)}) collective-permute-start(bf16[800,128]{1,0:T(8,128)(2,1)S(1)} %order.5.refs_5_), channel_id=1, source_target_pairs={{0,1},{1,0},{2,3},{3,2},{4,5},{5,4},{6,7},{7,6},{8,9},{9,8},{10,11... | collective-permute-start | bytes 614408 | tf_op jit(solution)/shard_map/ppermute | solution.py:369

commit v5 on v4

--- a/solution.py
+++ b/solution.py
@@ -120,16 +120,18 @@
         wide[here, 0:D] = left.astype(bf16)
         wide[here, D : 2 * D] = value.astype(bf16)
         wide[here, 2 * D : 3 * D] = right.astype(bf16)
-    for copy in copies:
-        copy.wait()
-    w_twice = jnp.concatenate([w_out[...], w_out[...]], axis=0)
     for part in range(4):
         start = part * 2 * COLS
         total = None
         for a in range(3):
+            if part == 0:
+                copies[a].wait()
             window = wide[start + a * COLS : start + a * COLS + 2 * COLS, :]
             term = jnp.dot(window, w_conv[a], preferred_element_type=f32)
             total = term if total is None else total + term
+        if part == 0:
+            copies[3].wait()
+            w_twice = jnp.concatenate([w_out[...], w_out[...]], axis=0)
         hidden = 0.5 * total * (
             1.0 + jnp.tanh(0.7978845608028654 * (total + 0.044715 * (total * total * total)))
         )

time: 75.6 us -> 75.6 us (level)
  no operation moved by 1% of the time
where the time goes in v5:
time: 75.6 us; the launch traced here: 75.3 us
  starting transfers between devices  36.6 us (48%)
  Pallas kernels  22.9 us (30%)
  waiting for transfers between devices  12.1 us (16%)
  local copies, waits for them, and re-layouts  2.09 us (3%)
  between operations  0.89 us (1%)
    pallas_call x12, Pallas kernels, call(): pl.pallas_call(kernel, out_shape=out_shape, in_specs=[vmem] * len(args) i...  22.9 us
    ppermute x12, starting transfers between devices, over_space(): return lax.ppermute(x, 'space', [(i, target(i)) for i in range(BANDS)])  17.8 us
    ppermute x1, waiting for transfers between devices, body(): third = lax.ppermute(pairs, BOTH, later(3))  6.65 us
    ppermute x12, waiting for transfers between devices, over_space(): return lax.ppermute(x, 'space', [(i, target(i)) for i in range(BANDS)])  5.47 us
    ppermute x1, starting transfers between devices, body(): second = lax.ppermute(couple, BOTH, later(2))  5.14 us
    ppermute x1, starting transfers between devices, body(): outer = lax.ppermute(outer, 'space', links + [(b, a) for a, b in links])  4.11 us
    ppermute x1, starting transfers between devices, body(): first = lax.ppermute(pairs, BOTH, later(1))  3.72 us
    ppermute x1, starting transfers between devices, body(): tail = lax.ppermute(window, BOTH, pointer_route())  3.27 us
  transfers between devices with their start and end apart: 17, of which 6 were waited for; matrix products, arithmetic and copies ran while one was open for 1% of the time, Pallas kernels for 19%

profile of v5, /device:TPU:13, one launch (start us, length us, event | category | flops | bytes accessed | tf_op | source)
XLA Modules:
  0.0 75.3 jit_solution(5489978629814575406)
XLA Ops:
  0.6 2.5 %joined.1 = (bf16[512,256]{1,0:T(8,128)(2,1)}, bf16[64,256]{1,0:T(8,128)(2,1)}, bf16[64,256]{1,0:T(8,128)(2,1)}, f32[1,256]{1,0:T(1,128)}, bf16[512,256]{1,0:T(8,128)(2,1)}) custom-call(bf16[512,256]{1,0:T(8,128)(2,1)} %bitcast.7, bf16[256,256]{1,0:T(8,128)(2,1)} %refs_1_.5, s32[8,64]{1,0:T(8,128)} %bitcast.13, bf16[256]{0:T(256)(128)(2,1)} %refs_3_.5, ...), custom_call_target="tpu_custom_call" | custom-call | flops 140000000 | bytes 1048576 | tf_op jit(solution)/shard_map/joined/pallas_call | solution.py:31
  3.1 4.1 %collective-permute-start.3 = (bf16[64,256]{1,0:T(8,128)(2,1)}, bf16[64,256]{1,0:T(8,128)(2,1)S(1)}, u32[]{:S(2)}, u32[]{:S(2)}) collective-permute-start(bf16[64,256]{1,0:T(8,128)(2,1)} %get-tuple-element.26), channel_id=1, source_target_pairs={{1,2},{3,4},{5,6},{2,1},{4,3},{6,5},{9,10},{11,12},{13,14},{10,9},... | collective-permute-start | bytes 98312 | tf_op jit(solution)/shard_map/ppermute | solution.py:433
  7.2 0.1 collective-permute-start.4
  7.3 0.5 collective-permute-start
  7.8 1.0 %collective-permute-done = f32[1,256]{1,0:T(1,128)S(1)} collective-permute-done((f32[1,256]{1,0:T(1,128)}, f32[1,256]{1,0:T(1,128)S(1)}, u32[]{:S(2)}, u32[]{:S(2)}) %collective-permute-start) | collective-permute-done | bytes 1056 | tf_op jit(solution)/shard_map/ppermute | solution.py:371
  8.8 0.7 add.6
  9.5 1.6 %collective-permute-start.1 = (f32[1,256]{1,0:T(1,128)S(1)}, f32[1,256]{1,0:T(1,128)S(1)}, u32[]{:S(2)}, u32[]{:S(2)}) collective-permute-start(f32[1,256]{1,0:T(1,128)S(1)} %add.6), channel_id=1, source_target_pairs={{0,2},{1,3},{2,0},{3,1},{4,6},{5,7},{6,4},{7,5},{8,10},{9,11},{10,... | collective-permute-start | bytes 3080 | tf_op jit(solution)/shard_map/ppermute | solution.py:371
  11.2 1.0 %collective-permute-done.1 = f32[1,256]{1,0:T(1,128)S(1)} collective-permute-done((f32[1,256]{1,0:T(1,128)S(1)}, f32[1,256]{1,0:T(1,128)S(1)}, u32[]{:S(2)}, u32[]{:S(2)}) %collective-permute-start.1) | collective-permute-done | bytes 1056 | tf_op jit(solution)/shard_map/ppermute | solution.py:371
  12.1 2.8 %collective-permute-start.2 = (f32[1,256]{1,0:T(1,128)S(1)}, f32[1,256]{1,0:T(1,128)S(1)}, u32[]{:S(2)}, u32[]{:S(2)}) collective-permute-start(f32[1,256]{1,0:T(1,128)S(1)} %add.7.earlier.mine), channel_id=1, source_target_pairs={{0,4},{1,5},{2,6},{3,7},{4,0},{5,1},{6,2},{7,3},{8,12},{9,13},{10,... | collective-permute-start | bytes 3080 | tf_op jit(solution)/shard_map/ppermute | solution.py:371
  14.9 0.0 collective-permute-done.3.value
  14.9 0.6 copy-done.3
  15.6 0.0 collective-permute-done.4.refs_2_
  15.6 0.6 copy-done.11
  16.2 0.0 copy-start.8
  16.2 0.0 copy-start.9
  16.2 4.1 %conv.1 = (bf16[8,4096]{1,0:T(8,128)(2,1)}, bf16[256,128]{1,0:T(8,128)(2,1)}) custom-call(bf16[512,256]{1,0:T(8,128)(2,1)} %get-tuple-element.25.refs_0_, bf16[64,256]{1,0:T(8,128)(2,1)} %copy-done.3, bf16[64,256]{1,0:T(8,128)(2,1)} %copy-done.11, bf16[3,768,256]{2,1,0:T(8,128)(2,1)} %bitcast.14, bf16[64,256]{1,0:T(8,128)(2,1)} %bitcast.15), custom_call_target="tpu_custom_call" | custom-call | flops 640000000 | bytes 1048576 | tf_op jit(solution)/shard_map/conv/pallas_call | solution.py:31
  20.3 0.0 collective-permute-done.2.other
  20.3 0.8 %copy-done.2 = bf16[256,128]{1,0:T(8,128)(2,1)S(1)} copy-done((bf16[256,128]{1,0:T(8,128)(2,1)S(1)}, bf16[256,128]{1,0:T(8,128)(2,1)}, u32[]{:S(2)}) %copy-start.2) | copy-done | bytes 65560
  21.1 0.8 %pair.1 = (bf16[1,256]{1,0:T(2,128)(2,1)}, bf16[272,128]{1,0:T(8,128)(2,1)S(1)}) custom-call(f32[1,256]{1,0:T(1,128)S(1)} %add.7.earlier.mine, f32[1,256]{1,0:T(1,128)S(1)} %collective-permute-done.2.other, bf16[256,256]{1,0:T(8,128)(2,1)S(1)} %copy-done.1, bf16[256,128]{1,0:T(8,128)(2,1)S(1)} %copy-done.2), custom_call_target="tpu_custom_call" | custom-call | flops 1000000 | bytes 1048576 | tf_op jit(solution)/shard_map/pair/pallas_call | solution.py:31
  21.9 5.1 %collective-permute-start.6 = (bf16[272,128]{1,0:T(8,128)(2,1)S(1)}, bf16[272,128]{1,0:T(8,128)(2,1)S(1)}, u32[]{:S(2)}, u32[]{:S(2)}) collective-permute-start(bf16[272,128]{1,0:T(8,128)(2,1)S(1)} %get-tuple-element.29.couple), channel_id=1, source_target_pairs={{0,16},{1,17},{2,18},{3,19},{4,20},{5,21},{6,22},{7,23},{8,24},{9,... | collective-permute-start | bytes 208904 | tf_op jit(solution)/shard_map/ppermute | solution.py:473
  27.0 3.7 %collective-permute-start.5 = (bf16[256,128]{1,0:T(8,128)(2,1)}, bf16[256,128]{1,0:T(8,128)(2,1)S(1)}, u32[]{:S(2)}, u32[]{:S(2)}) collective-permute-start(bf16[256,128]{1,0:T(8,128)(2,1)} %get-tuple-element.28.own), channel_id=1, source_target_pairs={{0,8},{1,9},{2,10},{3,11},{4,12},{5,13},{6,14},{7,15},{8,16},{9,17... | collective-permute-start | bytes 196616 | tf_op jit(solution)/shard_map/ppermute | solution.py:461
  30.8 2.6 %collective-permute-start.7 = (bf16[256,128]{1,0:T(8,128)(2,1)}, bf16[256,128]{1,0:T(8,128)(2,1)S(1)}, u32[]{:S(2)}, u32[]{:S(2)}) collective-permute-start(bf16[256,128]{1,0:T(8,128)(2,1)} %get-tuple-element.28.own), channel_id=1, source_target_pairs={{0,24},{1,25},{2,26},{3,27},{4,28},{5,29},{6,30},{7,31},{12,32},{1... | collective-permute-start | bytes 196616 | tf_op jit(solution)/shard_map/ppermute | solution.py:462
  33.3 0.0 collective-permute-done.5.first
  33.3 6.6 %collective-permute-done.7.third = bf16[256,128]{1,0:T(8,128)(2,1)S(1)} collective-permute-done((bf16[256,128]{1,0:T(8,128)(2,1)}, bf16[256,128]{1,0:T(8,128)(2,1)S(1)}, u32[]{:S(2)}, u32[]{:S(2)}) %collective-permute-start.7) | collective-permute-done | bytes 65568 | tf_op jit(solution)/shard_map/ppermute | solution.py:462
  40.0 0.0 collective-permute-done.6.second
  40.0 1.4 %collective-permute-start.14 = (bf16[768,128]{1,0:T(8,128)(2,1)S(1)}, bf16[768,128]{1,0:T(8,128)(2,1)S(1)}, u32[]{:S(2)}, u32[]{:S(2)}) collective-permute-start(bf16[768,128]{1,0:T(8,128)(2,1)S(1)} %get-tuple-element.30.refs_5_), channel_id=1, source_target_pairs={{0,2},{1,3},{2,0},{3,1},{4,6},{5,7},{6,4},{7,5},{8,10},{9,11},{10,... | collective-permute-start | bytes 589832 | tf_op jit(solution)/shard_map/ppermute | solution.py:371
  41.5 3.4 %collective-permute-start.10 = (bf16[768,128]{1,0:T(8,128)(2,1)S(1)}, bf16[768,128]{1,0:T(8,128)(2,1)S(1)}, u32[]{:S(2)}, u32[]{:S(2)}) collective-permute-start(bf16[768,128]{1,0:T(8,128)(2,1)S(1)} %get-tuple-element.30.refs_5_), channel_id=1, source_target_pairs={{0,1},{1,0},{2,3},{3,2},{4,5},{5,4},{6,7},{7,6},{8,9},{9,8},{10,11... | collective-permute-start | bytes 589832 | tf_op jit(solution)/shard_map/ppermute | solution.py:371
  44.8 0.7 collective-permute-start.8
  45.5 3.3 %collective-permute-start.9 = (bf16[16,128]{1,0:T(8,128)(2,1)S(1)}, bf16[16,128]{1,0:T(8,128)(2,1)S(1)}, u32[]{:S(2)}, u32[]{:S(2)}) collective-permute-start(bf16[16,128]{1,0:T(8,128)(2,1)S(1)} %get-tuple-element.31), channel_id=1, source_target_pairs={{0,8},{8,16},{1,17},{16,24},{9,25},{28,32},{21,33},{32,40},{29,41}... | collective-permute-start | bytes 12296 | tf_op jit(solution)/shard_map/ppermute | solution.py:488
  48.8 2.6 %collective-permute-start.15 = (bf16[768,128]{1,0:T(8,128)(2,1)S(1)}, bf16[768,128]{1,0:T(8,128)(2,1)S(1)}, u32[]{:S(2)}, u32[]{:S(2)}) collective-permute-start(bf16[768,128]{1,0:T(8,128)(2,1)S(1)} %collective-permute-done.14.refs_5_), channel_id=1, source_target_pairs={{0,1},{1,0},{2,3},{3,2},{4,5},{5,4},{6,7},{7,6},{8,9},{9,8},{10,11... | collective-permute-start | bytes 589832 | tf_op jit(solution)/shard_map/ppermute | solution.py:371
  51.4 0.0 collective-permute-done.10.refs_6_
  51.5 3.6 %attention.4 = (f32[512,1]{1,0:T(8,128)S(1)}, f32[512,1]{1,0:T(8,128)S(1)}, f32[512,256]{1,0:T(8,128)S(1)}) custom-call(bf16[512,256]{1,0:T(8,128)(2,1)S(1)} %copy-done.4, bf16[64,256]{1,0:T(8,128)(2,1)S(1)} %copy-done.6, bf16[64,256]{1,0:T(8,128)(2,1)S(1)} %copy-done.7, bf16[3,64]{1,0:T(4,128)(2,1)S(1)} %copy-done.8, bf16[1,64]{1,0:T(2,128)(2,1)S(1)} %bitcast.9, ...), custom_call_target="tpu_custom_call" | custom-call | flops 2400000000 | bytes 1048576 | tf_op jit(solution)/shard_map/attention/pallas_call | solution.py:31
  55.0 0.0 collective-permute-done.9.value
  55.1 1.0 %collective-permute-start.11 = (bf16[16,128]{1,0:T(8,128)(2,1)S(1)}, bf16[16,128]{1,0:T(8,128)(2,1)S(1)}, u32[]{:S(2)}, u32[]{:S(2)}) collective-permute-start(bf16[16,128]{1,0:T(8,128)(2,1)S(1)} %order.4.tail), channel_id=1, source_target_pairs={{0,4},{1,5},{2,6},{3,7},{4,0},{5,1},{6,2},{7,3},{8,12},{9,13},{10,... | collective-permute-start | bytes 12296 | tf_op jit(solution)/shard_map/ppermute | solution.py:371
  56.1 0.4 collective-permute-done.8.block
  56.5 2.0 %collective-permute-done.11.far = bf16[16,128]{1,0:T(8,128)(2,1)S(1)} collective-permute-done((bf16[16,128]{1,0:T(8,128)(2,1)S(1)}, bf16[16,128]{1,0:T(8,128)(2,1)S(1)}, u32[]{:S(2)}, u32[]{:S(2)}) %collective-permute-start.11) | collective-permute-done | bytes 4128 | tf_op jit(solution)/shard_map/ppermute | solution.py:371
  58.5 1.3 %collective-permute-start.13 = (bf16[800,128]{1,0:T(8,128)(2,1)S(1)}, bf16[800,128]{1,0:T(8,128)(2,1)S(1)}, u32[]{:S(2)}, u32[]{:S(2)}) collective-permute-start(bf16[800,128]{1,0:T(8,128)(2,1)S(1)} %join.1.refs_5_.refs_10_), channel_id=1, source_target_pairs={{0,1},{1,0},{2,3},{3,2},{4,5},{5,4},{6,7},{7,6},{8,9},{9,8},{10,11... | collective-permute-start | bytes 614408 | tf_op jit(solution)/shard_map/ppermute | solution.py:371
  59.8 1.7 %collective-permute-start.12 = (bf16[800,128]{1,0:T(8,128)(2,1)S(1)}, bf16[800,128]{1,0:T(8,128)(2,1)S(1)}, u32[]{:S(2)}, u32[]{:S(2)}) collective-permute-start(bf16[800,128]{1,0:T(8,128)(2,1)S(1)} %join.1.refs_5_.refs_10_), channel_id=1, source_target_pairs={{0,2},{1,3},{2,0},{3,1},{4,6},{5,7},{6,4},{7,5},{8,10},{9,11},{10,... | collective-permute-start | bytes 614408 | tf_op jit(solution)/shard_map/ppermute | solution.py:371
  61.5 0.0 collective-permute-done.15.refs_6_
  61.5 3.5 %attention.5 = (f32[512,1]{1,0:T(8,128)S(1)}, f32[512,1]{1,0:T(8,128)S(1)}, f32[512,256]{1,0:T(8,128)S(1)}) custom-call(bf16[512,256]{1,0:T(8,128)(2,1)S(1)} %copy-done.4, bf16[64,256]{1,0:T(8,128)(2,1)S(1)} %copy-done.6, bf16[64,256]{1,0:T(8,128)(2,1)S(1)} %copy-done.7, bf16[3,64]{1,0:T(4,128)(2,1)S(1)} %copy-done.8, bf16[1,64]{1,0:T(2,128)(2,1)S(1)} %bitcast.10, ...), custom_call_target="tpu_custom_call" | custom-call | flops 2400000000 | bytes 1048576 | tf_op jit(solution)/shard_map/attention/pallas_call | solution.py:31
  65.0 0.0 copy-start.10
  65.0 0.0 copy-start
  65.0 0.0 copy-start.5
  65.0 3.5 %attention.6 = (f32[512,1]{1,0:T(8,128)S(1)}, f32[512,1]{1,0:T(8,128)S(1)}, f32[512,256]{1,0:T(8,128)S(1)}) custom-call(bf16[512,256]{1,0:T(8,128)(2,1)S(1)} %copy-done.4, bf16[64,256]{1,0:T(8,128)(2,1)S(1)} %copy-done.6, bf16[64,256]{1,0:T(8,128)(2,1)S(1)} %copy-done.7, bf16[3,64]{1,0:T(4,128)(2,1)S(1)} %copy-done.8, bf16[1,64]{1,0:T(2,128)(2,1)S(1)} %bitcast.11, ...), custom_call_target="tpu_custom_call" | custom-call | flops 2400000000 | bytes 1048576 | tf_op jit(solution)/shard_map/attention/pallas_call | solution.py:31
  68.5 0.0 collective-permute-done.12.value
  68.5 0.7 collective-permute-start.16
  69.2 1.1 %collective-permute-done.16.refs_6_ = bf16[800,128]{1,0:T(8,128)(2,1)S(1)} collective-permute-done((bf16[800,128]{1,0:T(8,128)(2,1)S(1)}, bf16[800,128]{1,0:T(8,128)(2,1)S(1)}, u32[]{:S(2)}, u32[]{:S(2)}) %collective-permute-start.16) | collective-permute-done | bytes 204832 | tf_op jit(solution)/shard_map/ppermute | solution.py:371
  70.3 5.0 %attention.7 = bf16[512,256]{1,0:T(8,128)(2,1)} custom-call(bf16[512,256]{1,0:T(8,128)(2,1)S(1)} %copy-done.4, bf16[64,256]{1,0:T(8,128)(2,1)S(1)} %copy-done.6, bf16[64,256]{1,0:T(8,128)(2,1)S(1)} %copy-done.7, bf16[3,64]{1,0:T(4,128)(2,1)S(1)} %copy-done.8, bf16[1,64]{1,0:T(2,128)(2,1)S(1)} %bitcast.12, bf16[800,128]{1,0:T(8,128)(2,1)S(1)} %order.5.refs_5_, ...), custom_call_target="tpu_custom_call" | custom-call | flops 2400000000 | bytes 1048576 | tf_op jit(solution)/shard_map/attention/pallas_call | solution.py:31
  (25 shorter events, 0.1 us)
Async XLA Ops:
  3.1 11.8 %collective-permute-start.3 = (bf16[64,256]{1,0:T(8,128)(2,1)}, bf16[64,256]{1,0:T(8,128)(2,1)S(1)}, u32[]{:S(2)}, u32[]{:S(2)}) collective-permute-start(bf16[64,256]{1,0:T(8,128)(2,1)} %get-tuple-element.26), channel_id=1, source_target_pairs={{1,2},{3,4},{5,6},{2,1},{4,3},{6,5},{9,10},{11,12},{13,14},{10,9},... | collective-permute-start | bytes 98312 | tf_op jit(solution)/shard_map/ppermute | solution.py:433
  7.2 8.3 %collective-permute-start.4 = (bf16[64,256]{1,0:T(8,128)(2,1)}, bf16[64,256]{1,0:T(8,128)(2,1)S(1)}, u32[]{:S(2)}, u32[]{:S(2)}) collective-permute-start(bf16[64,256]{1,0:T(8,128)(2,1)} %get-tuple-element.27), channel_id=1, source_target_pairs={{0,1},{1,0},{2,3},{3,2},{4,5},{5,4},{6,7},{7,6},{8,9},{9,8},{10,11... | collective-permute-start | bytes 98312 | tf_op jit(solution)/shard_map/ppermute | solution.py:371
  7.3 1.5 %collective-permute-start = (f32[1,256]{1,0:T(1,128)}, f32[1,256]{1,0:T(1,128)S(1)}, u32[]{:S(2)}, u32[]{:S(2)}) collective-permute-start(f32[1,256]{1,0:T(1,128)} %get-tuple-element.24), channel_id=1, source_target_pairs={{0,1},{1,0},{2,3},{3,2},{4,5},{5,4},{6,7},{7,6},{8,9},{9,8},{10,11... | collective-permute-start | bytes 3080 | tf_op jit(solution)/shard_map/ppermute | solution.py:371
  9.5 2.6 %collective-permute-start.1 = (f32[1,256]{1,0:T(1,128)S(1)}, f32[1,256]{1,0:T(1,128)S(1)}, u32[]{:S(2)}, u32[]{:S(2)}) collective-permute-start(f32[1,256]{1,0:T(1,128)S(1)} %add.6), channel_id=1, source_target_pairs={{0,2},{1,3},{2,0},{3,1},{4,6},{5,7},{6,4},{7,5},{8,10},{9,11},{10,... | collective-permute-start | bytes 3080 | tf_op jit(solution)/shard_map/ppermute | solution.py:371
  12.1 8.1 %collective-permute-start.2 = (f32[1,256]{1,0:T(1,128)S(1)}, f32[1,256]{1,0:T(1,128)S(1)}, u32[]{:S(2)}, u32[]{:S(2)}) collective-permute-start(f32[1,256]{1,0:T(1,128)S(1)} %add.7.earlier.mine), channel_id=1, source_target_pairs={{0,4},{1,5},{2,6},{3,7},{4,0},{5,1},{6,2},{7,3},{8,12},{9,13},{10,... | collective-permute-start | bytes 3080 | tf_op jit(solution)/shard_map/ppermute | solution.py:371
  14.9 0.6 copy-start.3
  15.6 0.6 copy-start.11
  16.2 4.1 %copy-start.1 = (bf16[256,256]{1,0:T(8,128)(2,1)S(1)}, bf16[256,256]{1,0:T(8,128)(2,1)}, u32[]{:S(2)}) copy-start(bf16[256,256]{1,0:T(8,128)(2,1)} %w_ptr.1) | copy-start | bytes 393220
  16.2 35.3 %copy-start.4 = (bf16[512,256]{1,0:T(8,128)(2,1)S(1)}, bf16[512,256]{1,0:T(8,128)(2,1)}, u32[]{:S(2)}) copy-start(bf16[512,256]{1,0:T(8,128)(2,1)} %get-tuple-element.23.refs_0_) | copy-start | bytes 786436
  16.2 35.3 %copy-start.6 = (bf16[64,256]{1,0:T(8,128)(2,1)S(1)}, bf16[64,256]{1,0:T(8,128)(2,1)}, u32[]{:S(2)}) copy-start(bf16[64,256]{1,0:T(8,128)(2,1)} %refs_1_.9) | copy-start | bytes 98308
  16.2 35.3 %copy-start.7 = (bf16[64,256]{1,0:T(8,128)(2,1)S(1)}, bf16[64,256]{1,0:T(8,128)(2,1)}, u32[]{:S(2)}) copy-start(bf16[64,256]{1,0:T(8,128)(2,1)} %refs_2_.7) | copy-start | bytes 98308
  16.2 35.3 %copy-start.8 = (bf16[3,64]{1,0:T(4,128)(2,1)S(1)}, bf16[3,64]{1,0:T(4,128)(2,1)}, u32[]{:S(2)}) copy-start(bf16[3,64]{1,0:T(4,128)(2,1)} %refs_3_.9) | copy-start | bytes 1156
  16.2 35.3 %copy-start.9 = (bf16[64]{0:T(256)(128)(2,1)S(1)}, bf16[64]{0:T(256)(128)(2,1)}, u32[]{:S(2)}) copy-start(bf16[64]{0:T(256)(128)(2,1)} %param.27) | copy-start | bytes 388
  20.3 0.8 %copy-start.2 = (bf16[256,128]{1,0:T(8,128)(2,1)S(1)}, bf16[256,128]{1,0:T(8,128)(2,1)}, u32[]{:S(2)}) copy-start(bf16[256,128]{1,0:T(8,128)(2,1)} %get-tuple-element.28.own) | copy-start | bytes 196612
  21.9 18.1 %collective-permute-start.6 = (bf16[272,128]{1,0:T(8,128)(2,1)S(1)}, bf16[272,128]{1,0:T(8,128)(2,1)S(1)}, u32[]{:S(2)}, u32[]{:S(2)}) collective-permute-start(bf16[272,128]{1,0:T(8,128)(2,1)S(1)} %get-tuple-element.29.couple), channel_id=1, source_target_pairs={{0,16},{1,17},{2,18},{3,19},{4,20},{5,21},{6,22},{7,23},{8,24},{9,... | collective-permute-start | bytes 208904 | tf_op jit(solution)/shard_map/ppermute | solution.py:473
  27.0 6.3 %collective-permute-start.5 = (bf16[256,128]{1,0:T(8,128)(2,1)}, bf16[256,128]{1,0:T(8,128)(2,1)S(1)}, u32[]{:S(2)}, u32[]{:S(2)}) collective-permute-start(bf16[256,128]{1,0:T(8,128)(2,1)} %get-tuple-element.28.own), channel_id=1, source_target_pairs={{0,8},{1,9},{2,10},{3,11},{4,12},{5,13},{6,14},{7,15},{8,16},{9,17... | collective-permute-start | bytes 196616 | tf_op jit(solution)/shard_map/ppermute | solution.py:461
  30.8 9.2 %collective-permute-start.7 = (bf16[256,128]{1,0:T(8,128)(2,1)}, bf16[256,128]{1,0:T(8,128)(2,1)S(1)}, u32[]{:S(2)}, u32[]{:S(2)}) collective-permute-start(bf16[256,128]{1,0:T(8,128)(2,1)} %get-tuple-element.28.own), channel_id=1, source_target_pairs={{0,24},{1,25},{2,26},{3,27},{4,28},{5,29},{6,30},{7,31},{12,32},{1... | collective-permute-start | bytes 196616 | tf_op jit(solution)/shard_map/ppermute | solution.py:462
  40.0 8.8 %collective-permute-start.14 = (bf16[768,128]{1,0:T(8,128)(2,1)S(1)}, bf16[768,128]{1,0:T(8,128)(2,1)S(1)}, u32[]{:S(2)}, u32[]{:S(2)}) collective-permute-start(bf16[768,128]{1,0:T(8,128)(2,1)S(1)} %get-tuple-element.30.refs_5_), channel_id=1, source_target_pairs={{0,2},{1,3},{2,0},{3,1},{4,6},{5,7},{6,4},{7,5},{8,10},{9,11},{10,... | collective-permute-start | bytes 589832 | tf_op jit(solution)/shard_map/ppermute | solution.py:371
  41.5 10.0 %collective-permute-start.10 = (bf16[768,128]{1,0:T(8,128)(2,1)S(1)}, bf16[768,128]{1,0:T(8,128)(2,1)S(1)}, u32[]{:S(2)}, u32[]{:S(2)}) collective-permute-start(bf16[768,128]{1,0:T(8,128)(2,1)S(1)} %get-tuple-element.30.refs_5_), channel_id=1, source_target_pairs={{0,1},{1,0},{2,3},{3,2},{4,5},{5,4},{6,7},{7,6},{8,9},{9,8},{10,11... | collective-permute-start | bytes 589832 | tf_op jit(solution)/shard_map/ppermute | solution.py:371
  44.8 11.6 %collective-permute-start.8 = (bf16[768,128]{1,0:T(8,128)(2,1)S(1)}, bf16[768,128]{1,0:T(8,128)(2,1)S(1)}, u32[]{:S(2)}, u32[]{:S(2)}) collective-permute-start(bf16[768,128]{1,0:T(8,128)(2,1)S(1)} %get-tuple-element.30.refs_5_), channel_id=1, source_target_pairs={{0,4},{1,5},{2,6},{3,7},{4,0},{5,1},{6,2},{7,3},{8,12},{9,13},{10,... | collective-permute-start | bytes 589832 | tf_op jit(solution)/shard_map/ppermute | solution.py:371
  45.5 9.5 %collective-permute-start.9 = (bf16[16,128]{1,0:T(8,128)(2,1)S(1)}, bf16[16,128]{1,0:T(8,128)(2,1)S(1)}, u32[]{:S(2)}, u32[]{:S(2)}) collective-permute-start(bf16[16,128]{1,0:T(8,128)(2,1)S(1)} %get-tuple-element.31), channel_id=1, source_target_pairs={{0,8},{8,16},{1,17},{16,24},{9,25},{28,32},{21,33},{32,40},{29,41}... | collective-permute-start | bytes 12296 | tf_op jit(solution)/shard_map/ppermute | solution.py:488
  48.8 12.6 %collective-permute-start.15 = (bf16[768,128]{1,0:T(8,128)(2,1)S(1)}, bf16[768,128]{1,0:T(8,128)(2,1)S(1)}, u32[]{:S(2)}, u32[]{:S(2)}) collective-permute-start(bf16[768,128]{1,0:T(8,128)(2,1)S(1)} %collective-permute-done.14.refs_5_), channel_id=1, source_target_pairs={{0,1},{1,0},{2,3},{3,2},{4,5},{5,4},{6,7},{7,6},{8,9},{9,8},{10,11... | collective-permute-start | bytes 589832 | tf_op jit(solution)/shard_map/ppermute | solution.py:371
  55.1 3.4 %collective-permute-start.11 = (bf16[16,128]{1,0:T(8,128)(2,1)S(1)}, bf16[16,128]{1,0:T(8,128)(2,1)S(1)}, u32[]{:S(2)}, u32[]{:S(2)}) collective-permute-start(bf16[16,128]{1,0:T(8,128)(2,1)S(1)} %order.4.tail), channel_id=1, source_target_pairs={{0,4},{1,5},{2,6},{3,7},{4,0},{5,1},{6,2},{7,3},{8,12},{9,13},{10,... | collective-permute-start | bytes 12296 | tf_op jit(solution)/shard_map/ppermute | solution.py:371
  58.5 6.5 %collective-permute-start.13 = (bf16[800,128]{1,0:T(8,128)(2,1)S(1)}, bf16[800,128]{1,0:T(8,128)(2,1)S(1)}, u32[]{:S(2)}, u32[]{:S(2)}) collective-permute-start(bf16[800,128]{1,0:T(8,128)(2,1)S(1)} %join.1.refs_5_.refs_10_), channel_id=1, source_target_pairs={{0,1},{1,0},{2,3},{3,2},{4,5},{5,4},{6,7},{7,6},{8,9},{9,8},{10,11... | collective-permute-start | bytes 614408 | tf_op jit(solution)/shard_map/ppermute | solution.py:371
  59.8 8.7 %collective-permute-start.12 = (bf16[800,128]{1,0:T(8,128)(2,1)S(1)}, bf16[800,128]{1,0:T(8,128)(2,1)S(1)}, u32[]{:S(2)}, u32[]{:S(2)}) collective-permute-start(bf16[800,128]{1,0:T(8,128)(2,1)S(1)} %join.1.refs_5_.refs_10_), channel_id=1, source_target_pairs={{0,2},{1,3},{2,0},{3,1},{4,6},{5,7},{6,4},{7,5},{8,10},{9,11},{10,... | collective-permute-start | bytes 614408 | tf_op jit(solution)/shard_map/ppermute | solution.py:371
  65.0 4.2 %copy-start.10 = (bf16[16,256]{1,0:T(8,128)(2,1)S(1)}, bf16[16,256]{1,0:T(8,128)(2,1)}, u32[]{:S(2)}) copy-start(bf16[16,256]{1,0:T(8,128)(2,1)} %param.26) | copy-start | bytes 24580
  65.0 5.3 %copy-start = (bf16[1,8,64,256]{3,2,1,0:T(8,128)(2,1)S(1)}, bf16[1,8,64,256]{3,2,1,0:T(8,128)(2,1)}, u32[]{:S(2)}) copy-start(bf16[1,8,64,256]{3,2,1,0:T(8,128)(2,1)} %param.14) | copy-start | bytes 786436
  65.0 5.3 %copy-start.5 = (bf16[256,256]{1,0:T(8,128)(2,1)S(1)}, bf16[256,256]{1,0:T(8,128)(2,1)}, u32[]{:S(2)}) copy-start(bf16[256,256]{1,0:T(8,128)(2,1)} %refs_13_.1) | copy-start | bytes 393220
  68.5 1.7 %collective-permute-start.16 = (bf16[800,128]{1,0:T(8,128)(2,1)S(1)}, bf16[800,128]{1,0:T(8,128)(2,1)S(1)}, u32[]{:S(2)}, u32[]{:S(2)}) collective-permute-start(bf16[800,128]{1,0:T(8,128)(2,1)S(1)} %order.5.refs_5_), channel_id=1, source_target_pairs={{0,1},{1,0},{2,3},{3,2},{4,5},{5,4},{6,7},{7,6},{8,9},{9,8},{10,11... | collective-permute-start | bytes 614408 | tf_op jit(solution)/shard_map/ppermute | solution.py:371
